TPU v7x, 128 devices: a whole 4x4x4 slice. The times are simulated.
128 devices in a mesh: user: 16 (over x, y_lo, core), cand: 8 (over z, y_hi).
Axes of the slice: x: 4, y: 4 (y_hi: 2, y_lo: 2; y = y_hi * 2 + y_lo), z: 4, core: 2. Of those that a mesh axis runs over, the one named last changes fastest.
Arguments:
- pooled: bfloat16 [16, 32, 1024, 1024], P('user', None, 'cand'), may hold values from -6 to 6
- cand_feats: bfloat16 [65536, 1024], P(('user', 'cand')), may hold values from -6 to 6
- hist_len: int32 [32], P('user'), may hold values from 1 to 1024, 16384 in all
- cand_user: int32 [65536], P(('user', 'cand')), may hold values from 0 to 31, as said below
- w_in: bfloat16 [1024, 4096], replicated, may hold values from -0.1875 to 0.1875
- w_out: bfloat16 [1024, 1024], replicated, may hold values from -0.1875 to 0.1875
Outputs:
- hist_out: bfloat16 [32, 1024, 1024], P('user', 'cand')
- cand_out: bfloat16 [65536, 1024], P(('user', 'cand'))
Inputs may be any that keep to these rules, and one draw needn't show every extreme that they name: `hist_len`: the lengths sum to 16384, and the longest is 1024. `cand_user`: candidate row r belongs to one of the 2 users numbered from (r // 4096) * 2 on.
All inputs are finite; a program needn't handle non-finite values. No bound on the sum of `hist_len` on one device may be relied on, other than what follows from the above.
Results may differ from a plain program's by a relative error of at most 0.022.
Values may be sent and summed in bfloat16 or wider, within the bound.
No kernel may reach another device: no remote copies, remote signals or barrier semaphores. Data moves between devices by JAX's collectives and lax.ppermute only.
A program may use at most 128 MiB of HBM per device.

v0:
```python
import functools

import jax
import jax.numpy as jnp
from jax import lax
from jax.experimental import pallas as pl
from jax.experimental.pallas import tpu as pltpu
from jax.sharding import PartitionSpec as P

F32 = jnp.float32
BF16 = jnp.bfloat16
HEADS = 8
HD = 128
D = 1024
SLOTS = 128
ROWS = 512
NX, NZ = 4, 4
WINDOW = 320
HALF_SCALE = 0.5 / (HD**0.5)
VMEM = 20 * 1024 * 1024
GROUP = 512
SHIFTS = (0, -1, 1, 2)
HIDE = 1 << 16
HOPS = (1, 3, 2)
SIDES = (lambda s: s[1], lambda s: 1 - s[1])


def silu(v):
    half = v * 0.5
    half = half.astype(BF16)
    return half + half * jnp.tanh(half)


def layer_norm(rows):
    mean = jnp.mean(rows, axis=-1, keepdims=True)
    centered = rows - mean
    var = jnp.mean(centered * centered, axis=-1, keepdims=True)
    return centered * lax.rsqrt(var + 1e-05)


def mm(a, b):
    return jnp.dot(a, b, preferred_element_type=F32)


def weights_of(queries, keys):
    s = lax.dot_general(queries, keys, (((1,), (1,)), ((), ())), preferred_element_type=F32)
    half = (s * HALF_SCALE).astype(BF16)
    return half + half * jnp.tanh(half)


def after(value, *others):
    return lax.optimization_barrier((value, others))[0]


def in_hbm(array):
    return pltpu.with_memory_space_constraint(array, pltpu.HBM)


def cost():
    return pl.CostEstimate(flops=10**6, bytes_accessed=1 << 16, transcendentals=0)


def block_sums(name, scal, arrays, shapes, sums, hbm=True):
    loads = [part for _, _, parts, _ in sums for part in parts]

    def body(scal_ref, *refs):
        ins, refs = refs[: len(arrays)], refs[len(arrays) :]
        outs, refs = refs[: len(shapes)], refs[len(shapes) :]
        bufs, refs = refs[: len(loads)], refs[len(loads) :]
        res, (in_sems, out_sems) = refs[: len(sums)], refs[len(sums) :]
        copies = []
        for n, (at, index) in enumerate(loads):
            lead = index(scal_ref)
            src = ins[at].at[lead] if lead else ins[at]
            copies.append(pltpu.make_async_copy(src, bufs[n], in_sems.at[n]))
            copies[-1].start()
        stores, used = [], 0
        for n, (out, lead, parts, norm) in enumerate(sums):
            members = range(used, used + len(parts))
            used += len(parts)
            for k in members:
                copies[k].wait()
            ready = bufs[members[0]]
            if len(parts) > 1:
                ready = res[n]

                @pl.loop(0, SLOTS // 32)
                def _(r):
                    rows = pl.ds(pl.multiple_of(r * 32, 32), 32)
                    total = None
                    for k in members:
                        value = bufs[k][rows, :].astype(F32)
                        total = value if total is None else total + value
                    ready[rows, :] = (layer_norm(total) if norm else total).astype(ready.dtype)

            lead = (lead(scal_ref),) if callable(lead) else lead
            dst = outs[out].at[lead] if lead else outs[out]
            stores.append(pltpu.make_async_copy(ready, dst, out_sems.at[n]))
            stores[-1].start()
        for store in stores:
            store.wait()

    spec = pl.BlockSpec(memory_space=pltpu.HBM)
    return pl.pallas_call(
        body,
        in_specs=[pl.BlockSpec(memory_space=pltpu.SMEM)]
        + [spec if a.ndim == 6 else pl.BlockSpec(memory_space=pl.ANY) for a in arrays],
        out_specs=[spec if hbm else pl.BlockSpec(memory_space=pl.ANY)] * len(shapes),
        out_shape=[(pltpu.HBM if hbm else jax.ShapeDtypeStruct)(shape, dtype) for shape, dtype in shapes],
        scratch_shapes=[pltpu.VMEM((SLOTS, D), arrays[at].dtype) for at, _ in loads]
        + [
            pltpu.VMEM((SLOTS if len(parts) > 1 else 16, D), shapes[out][1])
            for out, _, parts, _ in sums
        ]
        + [pltpu.SemaphoreType.DMA((len(loads),)), pltpu.SemaphoreType.DMA((len(sums),))],
        compiler_params=pltpu.CompilerParams(vmem_limit_bytes=VMEM),
        cost_estimate=cost(),
        name=name,
    )(scal, *(in_hbm(a) if a.ndim == 6 else a for a in arrays))


def pack(place, tables):
    sums = [(0, (x,), [(0, lambda s, x=x: (x, 1 - s[1], 1 - s[2], 1))], False) for x in range(NX)]
    return block_sums("pack", place, [tables], [((NX, SLOTS, D), BF16)], sums)[0]


def pack_all(place, tables):
    sums = [
        (n, (x,), [(0, lambda s, x=x, side=side: (x, side(s), 1 - s[2], 0))], False)
        for x in range(NX)
        for n, side in enumerate(SIDES)
    ]
    return block_sums("pack_all", place, [tables], [((NX, SLOTS, D), BF16)] * 2, sums)


def over_y(place, tables, got):
    sums = [
        (0, (x,), [(0, lambda s, x=x: (x, 1 - s[1], s[2], 1)), (1, lambda s, x=x: (x,))], False)
        for x in range(NX)
    ]
    return block_sums("over_y", place, [tables, got], [((NX, SLOTS, D), BF16)], sums)[0]


def away_x(place, tables, got):
    sums = []
    for n, d in enumerate(HOPS):
        for m, side in enumerate(SIDES):
            at = lambda s, d=d: lax.rem(s[0] + d, NX)
            parts = [
                (0, lambda s, at=at, side=side: (at(s), side(s), s[2], 0)),
                (1 + m, lambda s, at=at: (at(s),)),
            ]
            sums.append((n, side, parts, False))
    for n in range(NX):
        sums.append((3, (n,), [(0, lambda s, n=n: (n, s[1], 1 - s[2], 1))], False))
    shapes = [((2, SLOTS, D), BF16)] * 3 + [((NX, SLOTS, D), BF16)]
    return block_sums("away_x", place, [tables] + list(got), shapes, sums)


def join_x(place, tables, got, arrived):
    arrays = [tables] + list(got) + list(arrived)
    sums = []
    for n in (1, 0):
        side = SIDES[n]
        parts = [(0, lambda s, side=side: (s[0], side(s), s[2], 0)), (1 + n, lambda s: (s[0],))]
        parts += [(3 + k, lambda s, side=side: (side(s),)) for k in range(3)]
        sums.append((n, (), parts, False))
    return block_sums("join_x", place, arrays, [((SLOTS, D), F32), ((SLOTS, D), BF16)], sums, False)


def join_y(place, tables, got, arrived):
    sums = []
    for n, d in enumerate(HOPS):
        at = lambda s, d=d: lax.rem(s[0] + d, NX)
        parts = [
            (0, lambda s, at=at: (at(s), s[1], s[2], 1)),
            (1, lambda s, at=at: (at(s),)),
            (2, lambda s, at=at: (at(s),)),
        ]
        sums.append((n, (), parts, False))
    return block_sums("join_y", place, [tables, got, arrived], [((SLOTS, D), BF16)] * 3, sums)


def norm_sum(place, tables, got, side, arrived):
    parts = [
        (0, lambda s: (s[0], s[1], s[2], 1)),
        (1, lambda s: (s[0],)),
        (2, lambda s: (s[0],)),
    ] + [(3 + n, lambda s: ()) for n in range(3)]
    arrays = [tables, got, side] + list(arrived)
    return block_sums("norm_sum", place, arrays, [((SLOTS, D), BF16)], [(0, (), parts, True)], False)[0]


def norm_both(place, first, second):
    parts = [(n, lambda s: ()) for n in range(len(first) + 1)]
    sums = [(0, (1,), parts[-1:], False), (0, (0,), parts[:-1], True)]
    return block_sums("norm_both", place, list(first) + [second], [((2, SLOTS, D), BF16)], sums, False)[0]


def in_vmem(array):
    return pltpu.with_memory_space_constraint(array, pltpu.VMEM)


def kernel_call(body, name, arrays, out_shape, scratch, scalars=None, aliases=None):
    vmem = pl.BlockSpec(memory_space=pltpu.VMEM)
    in_specs, args = [vmem] * len(arrays), [in_vmem(array) for array in arrays]
    if scalars is not None:
        in_specs = [pl.BlockSpec(memory_space=pltpu.SMEM)] + in_specs
        args = [scalars] + args
    return pl.pallas_call(
        body,
        in_specs=in_specs,
        out_specs=[vmem] * len(out_shape),
        out_shape=out_shape,
        scratch_shapes=scratch,
        input_output_aliases=aliases or {},
        compiler_params=pltpu.CompilerParams(vmem_limit_bytes=VMEM),
        cost_estimate=cost(),
        name=name,
    )(*args)


def cand_kernel(owner_ref, feats_ref, w_ref, xs_ref, u_ref, q_ref, back_ref, a_ref):
    second = owner_ref[...].astype(F32)
    r_from = lax.broadcasted_iota(jnp.int32, (ROWS, ROWS), 0)
    r_to = lax.broadcasted_iota(jnp.int32, (ROWS, ROWS), 1)
    upper = jnp.where(r_from <= r_to, 1.0, 0.0).astype(BF16)
    ones_before = mm(jnp.broadcast_to(second, (8, ROWS)).astype(BF16), upper)[:1]
    index = lax.broadcasted_iota(jnp.int32, (1, ROWS), 1).astype(F32)
    n_first = ROWS - jnp.sum(second, axis=1, keepdims=True)
    place = jnp.where(second > 0.5, n_first + ones_before - 1.0, index - ones_before)
    onehot = jnp.where(r_from == place.astype(jnp.int32), 1.0, 0.0)
    back_ref[...] = onehot.T.astype(BF16)
    onehot = onehot.astype(BF16)
    x = layer_norm(feats_ref[...].astype(F32)).astype(BF16)
    xs_ref[...] = mm(onehot, x).astype(BF16)

    @pl.loop(0, D // GROUP)
    def _(g):
        cols = lambda n: pl.ds(pl.multiple_of(n * D + g * GROUP, GROUP), GROUP)
        u, v, q, k = (silu(mm(xs_ref[...], w_ref[:, cols(n)])).astype(BF16) for n in range(4))
        u_ref[:, cols(0)] = u
        q_ref[:, cols(0)] = q
        prod = q.astype(F32) * k.astype(F32)
        for h in range(GROUP // HD):
            hc = slice(h * HD, (h + 1) * HD)
            half = jnp.sum(prod[:, hc], axis=-1, keepdims=True) * HALF_SCALE
            own = (half + half * jnp.tanh(half)).astype(BF16).astype(F32)
            out_cols = pl.ds(pl.multiple_of(g * GROUP + h * HD, HD), HD)
            a_ref[:, out_cols] = own * v[:, hc].astype(F32)


def cand_project(owner_row, feats, w_in):
    rows = jax.ShapeDtypeStruct((ROWS, D), BF16)
    out_shape = [rows, rows, rows, jax.ShapeDtypeStruct((ROWS, ROWS), BF16), jax.ShapeDtypeStruct((ROWS, D), F32)]
    return kernel_call(cand_kernel, "cand_project", [owner_row, feats, w_in], out_shape, [])


def absorb_kernel(plan, scal_ref, *refs):
    pieces, first, final = plan
    count = len(pieces)
    refs = list(refs)
    take = lambda n: [refs.pop(0) for _ in range(n)]
    x_refs = take(count)
    w_ref, q_ref, a_ref = take(3)
    if not first:
        qh_ref, ah_ref = take(2)
    if final:
        uh_ref, own_ref, u_ref, xs_ref, back_ref, wo_ref, hist_ref, cand_ref = take(8)
    elif first:
        _, ah_ref, qh_ref, uh_ref = take(4)
    else:
        take(2)
    k_scr, v_scr = take(2)
    row_iota = lax.broadcasted_iota(jnp.int32, (SLOTS, 1), 0)
    ahead = lax.broadcasted_iota(jnp.int32, (SLOTS, SLOTS), 0) - lax.broadcasted_iota(
        jnp.int32, (SLOTS, SLOTS), 1
    )
    offs = [scal_ref[0, 4 + piece] for piece in pieces]
    my_off = scal_ref[0, 3]

    steps = D // GROUP

    def column(n, g):
        return slice(n * D + g * GROUP, n * D + (g + 1) * GROUP)

    def project(g, n):
        x = x_refs[n][...].reshape(2 * SLOTS, D)
        if first and n == 0:
            qh_ref[:, column(0, g)] = silu(mm(x, w_ref[:, column(2, g)])).astype(BF16)
            uh_ref[:, column(0, g)] = silu(mm(x, w_ref[:, column(0, g)])).astype(BF16)
        k = silu(mm(x, w_ref[:, column(3, g)])).astype(BF16)
        v = silu(mm(x, w_ref[:, column(1, g)])).astype(BF16)
        to = slice(n * SLOTS, (n + 1) * SLOTS)
        for user in (0, 1):
            at = slice(user * SLOTS, (user + 1) * SLOTS)
            live = row_iota < scal_ref[user, 0] - offs[n]
            k_scr[g % 2, user, to, :] = k[at]
            v_scr[g % 2, user, to, :] = jnp.where(live, v[at], jnp.zeros_like(v[at]))

    def attend(g, user, h, turn):
        row_lo, row_hi = scal_ref[user, 1], scal_ref[user, 2]
        covered = starts[user] + WINDOW
        start = pl.multiple_of(jnp.where(turn == 0, starts[user], ROWS - WINDOW), 16)
        rows = pl.ds(start, WINDOW)
        index = start + lax.broadcasted_iota(jnp.int32, (WINDOW, 1), 0)
        mine = (index >= jnp.where(turn == 0, row_lo, covered)) & (index < row_hi)
        mine_rows = slice(user * SLOTS, (user + 1) * SLOTS)
        hc = slice(h * HD, (h + 1) * HD)
        oc = slice(g * GROUP + h * HD, g * GROUP + (h + 1) * HD)
        q = jnp.concatenate([q_ref[rows, oc], qh_ref[mine_rows, oc]], axis=0)
        w = weights_of(q, k_scr[g % 2, user, :, hc])
        parts = []
        for n in range(count):
            part = w[WINDOW:, n * SLOTS : (n + 1) * SLOTS]
            seen = ahead >= offs[n] - my_off + turn * HIDE
            parts.append(jnp.where(seen, part, jnp.zeros_like(part)).astype(BF16))
        w = jnp.concatenate([w[:WINDOW].astype(BF16), jnp.concatenate(parts, axis=1)], axis=0)
        total = mm(w, v_scr[g % 2, user, :, hc])
        a_ref[rows, oc] += jnp.where(mine, total[:WINDOW], 0.0)
        ah_ref[mine_rows, oc] += total[WINDOW:]

    if first:
        ah_ref[...] = jnp.zeros((2 * SLOTS, D), F32)
    starts = [jnp.minimum((scal_ref[user, 1] // 16) * 16, ROWS - WINDOW) for user in (0, 1)]
    fits = [scal_ref[user, 2] <= starts[user] + WINDOW for user in (0, 1)]
    turns = jnp.where(fits[0] & fits[1], 1, 2)
    pairs = [(user, h) for user in (0, 1) for h in range(GROUP // HD)]

    @pl.loop(0, turns)
    def _(turn):
        for n in range(count):
            project(0, n)
        for g in range(steps):
            left = list(range(count)) if g + 1 < steps else []
            gap = max(1, len(pairs) // max(1, len(left)))
            for i, (user, h) in enumerate(pairs):
                if left and i % gap == 0:
                    project(g + 1, left.pop(0))
                attend(g, user, h, turn)
            for n in left:
                project(g + 1, n)

    if final:
        (y_scr,) = take(1)
        n_hist = 2 * SLOTS
        y = layer_norm(ah_ref[...]) * uh_ref[...].astype(F32)
        y_scr[:n_hist, :] = y.astype(BF16)

        @pl.loop(0, ROWS // SLOTS)
        def _(n):
            rows = pl.ds(pl.multiple_of(n * SLOTS, SLOTS), SLOTS)
            y = layer_norm(a_ref[rows, :]) * u_ref[rows, :].astype(F32)
            y_scr[pl.ds(pl.multiple_of(n_hist + n * SLOTS, SLOTS), SLOTS), :] = y.astype(BF16)

        @pl.loop(0, D // GROUP)
        def _(g):
            cols = pl.ds(pl.multiple_of(g * GROUP, GROUP), GROUP)
            res = mm(y_scr[...], wo_ref[:, cols])
            for user in (0, 1):
                out = res[user * SLOTS : (user + 1) * SLOTS] + own_ref[user, :, cols].astype(F32)
                keep = my_off + row_iota < scal_ref[user, 0]
                hist_ref[user, :, cols] = jnp.where(keep, out, 0.0).astype(BF16)
            done = (res[n_hist:] + xs_ref[:, cols].astype(F32)).astype(BF16)
            cand_ref[:, cols] = mm(back_ref[...], done).astype(BF16)


def absorb(name, scal, items, w_in, q_cand, a_cand, state=None, final=None):
    pieces = tuple(item[0] for item in items)
    arrays = [item[1] for item in items] + [w_in, q_cand, a_cand]
    a_at = len(arrays)
    scratch = [pltpu.VMEM((2, 2, len(pieces) * SLOTS, GROUP), BF16)] * 2
    sums = jax.ShapeDtypeStruct((2 * SLOTS, D), F32)
    rows = jax.ShapeDtypeStruct((2 * SLOTS, D), BF16)
    out_shape = [jax.ShapeDtypeStruct((ROWS, D), F32), sums]
    aliases = {a_at: 0}
    first = state is None
    if first:
        out_shape += [rows, rows]
    else:
        arrays += [state[0], state[2]]
        aliases[a_at + 2] = 1
    if final is not None:
        arrays += [state[1]] + list(final)
        out_shape = [jax.ShapeDtypeStruct((2, SLOTS, D), BF16), jax.ShapeDtypeStruct((ROWS, D), BF16)]
        aliases = {}
        scratch.append(pltpu.VMEM((2 * SLOTS + ROWS, D), BF16))
    outs = kernel_call(
        functools.partial(absorb_kernel, (pieces, first, final is not None)),
        name,
        arrays,
        out_shape,
        scratch,
        scal,
        aliases,
    )
    if final is not None:
        return outs
    return outs[0], (outs[2], outs[3], outs[1]) if first else (state[0], state[1], outs[1])


def user_perm(dx, dy, dcore):
    pairs = []
    for u in range(4 * NX):
        x, y, core = u >> 2, (u >> 1) & 1, u & 1
        pairs.append((u, (((x + dx) % NX) * 2 + (y ^ dy)) * 2 + (core ^ dcore)))
    return pairs


def cand_perm(dz, dy):
    return [(c, (((c >> 1) + dz) % NZ) * 2 + ((c & 1) ^ dy)) for c in range(2 * NZ)]


def to_user(array, dx, dy, dcore):
    return lax.ppermute(array, "user", user_perm(dx, dy, dcore))


def to_cand(array, dz, dy):
    return lax.ppermute(array, "cand", cand_perm(dz, dy))


def local(pooled, cand_feats, hist_len, cand_user, w_in, w_out):
    user = lax.axis_index("user")
    cand = lax.axis_index("cand")
    x, y, core = user >> 2, (user >> 1) & 1, user & 1
    z, y_hi = cand >> 1, cand & 1
    owner = cand_user - 2 * user
    n_first = ROWS - jnp.sum(owner)
    offsets = [SLOTS * (((z + dz + NZ) % NZ) * 2 + (y_hi ^ e)) for dz in SHIFTS for e in range(2)]
    scal = jnp.stack(
        [
            jnp.stack([hist_len[0], 0 * user, n_first, cand * SLOTS] + offsets),
            jnp.stack([hist_len[1], n_first, 0 * user + ROWS, cand * SLOTS] + offsets),
        ]
    ).astype(jnp.int32)

    tables = pooled.reshape(NX, 2, 2, 2, SLOTS, D)
    place = jnp.stack([x, y, core]).astype(jnp.int32)
    with jax.named_scope("sum_core"):
        pack1 = pack(place, tables)
        got1 = to_user(pack1, 0, 0, 1)
        pack0 = pack_all(place, after(tables, pack1))
        got0 = [to_user(part, 0, 0, 1) for part in pack0]
    with jax.named_scope("sum_y_second"):
        over1 = over_y(place, tables, after(got1, pack0))
        y1 = to_user(over1, 0, 1, 0)
    with jax.named_scope("sum_x_first"):
        *away0, pack2 = away_x(place, tables, after(got0, over1))
        x0 = [to_user(part, d, 0, 0) for part, d in zip(away0, HOPS)]
    with jax.named_scope("sum_core"):
        got2 = to_user(pack2, 0, 0, 1)
    owner_row, scal = after((owner.reshape(1, ROWS), scal), pack2)
    xs, u_cand, q_cand, back, a_cand = cand_project(owner_row, cand_feats, w_in)
    with jax.named_scope("sum_y_second"):
        y1 = after(y1, xs, scal)
        away1 = join_y(place, tables, got2, y1)
        x1 = [to_user(part, d, 0, 0) for part, d in zip(away1, HOPS)]
    with jax.named_scope("sum_x_first"):
        mine0, over0 = join_x(place, tables, got0, after(x0, away1))
        y0 = to_user(over0, 0, 1, 0)
    with jax.named_scope("gather"):
        own1 = norm_sum(place, tables, got2, y1, after(x1, mine0))
        own = norm_both(place, [mine0, after(y0, own1)], own1)
        near = to_cand(own, 0, 1)
        own_left, own_right = to_cand(own, 1, 0), to_cand(own, -1, 0)
    put = functools.partial(absorb, scal=scal, w_in=w_in, q_cand=q_cand)
    piece = lambda shift, e: 2 * SHIFTS.index(shift) + e
    a_cand, state = put("own_keys", items=[(piece(0, 0), own)], a_cand=a_cand)
    with jax.named_scope("gather"):
        near = after(near, a_cand)
        near_left, near_right = to_cand(near, 1, 0), to_cand(near, -1, 0)
        own_left, own_right = after((own_left, own_right), near)
        own_far = to_cand(own_left, 1, 0)
    a_cand, state = put(
        "own_sides",
        items=[(piece(-1, 0), own_left), (piece(1, 0), own_right), (piece(0, 1), near)],
        a_cand=a_cand,
        state=state,
    )
    with jax.named_scope("gather"):
        near_left, near_right = after((near_left, near_right), a_cand)
        near_far = to_cand(near_right, -1, 0)
    a_cand, state = put(
        "near_sides",
        items=[(piece(-1, 1), near_left), (piece(1, 1), near_right)],
        a_cand=a_cand,
        state=state,
    )
    return put(
        "far_finish",
        items=[(piece(2, 0), own_far), (piece(2, 1), near_far)],
        a_cand=a_cand,
        state=state,
        final=(own, u_cand, xs, back, w_out),
    )


def solution(mesh):
    placed = (
        P("user", None, "cand", None),
        P(("user", "cand"), None),
        P("user"),
        P(("user", "cand")),
        P(),
        P(),
    )
    return jax.shard_map(
        local,
        mesh=mesh,
        in_specs=placed,
        out_specs=(P("user", "cand", None), P(("user", "cand"), None)),
        check_vma=False,
    )
```

profile of v0, /device:TPU:0, one launch (start us, length us, event | category | flops | bytes accessed | tf_op | source)
XLA Modules:
  0.0 112.4 jit_solution(15363520304705861751)
XLA Ops:
  0.6 0.1 pad_add_fusion.1.scal_ref
  0.7 2.5 %pack.1 = bf16[4,128,1024]{2,1,0:T(8,128)(2,1)} custom-call(s32[3]{0:T(128)S(1)} %pad_add_fusion.1.scal_ref, bf16[4,2,2,2,128,1024]{5,4,3,2,1,0:T(8,128)(2,1)} %bitcast.20), custom_call_target="tpu_custom_call" | custom-call | flops 1000000 | bytes 65536 | tf_op jit(solution)/shard_map/sum_core/pack/pallas_call | solution.py:104
  3.3 0.1 collective-permute-start.2
  3.3 3.0 %pack_all.1 = (bf16[4,128,1024]{2,1,0:T(8,128)(2,1)}, bf16[4,128,1024]{2,1,0:T(8,128)(2,1)}) custom-call(s32[3]{0:T(128)S(1)} %pad_add_fusion.1.scal_ref, bf16[4,2,2,2,128,1024]{5,4,3,2,1,0:T(8,128)(2,1)} %bitcast.21), custom_call_target="tpu_custom_call" | custom-call | flops 1000000 | bytes 65536 | tf_op jit(solution)/shard_map/sum_core/pack_all/pallas_call | solution.py:104
  6.3 0.6 collective-permute-start
  6.9 0.1 collective-permute-start.1
  7.0 0.0 collective-permute-done.2.refs_1_
  7.0 2.6 %over_y.1 = bf16[4,128,1024]{2,1,0:T(8,128)(2,1)} custom-call(s32[3]{0:T(128)S(1)} %pad_add_fusion.1.scal_ref, bf16[4,2,2,2,128,1024]{5,4,3,2,1,0:T(8,128)(2,1)} %bitcast.22, bf16[4,128,1024]{2,1,0:T(8,128)(2,1)S(1)} %collective-permute-done.2.refs_1_), custom_call_target="tpu_custom_call" | custom-call | flops 1000000 | bytes 65536 | tf_op jit(solution)/shard_map/sum_y_second/over_y/pallas_call | solution.py:104
  9.6 0.0 copy-start.3
  9.6 0.0 copy-start.4
  9.7 1.7 %collective-permute-start.7 = (bf16[4,128,1024]{2,1,0:T(8,128)(2,1)}, bf16[4,128,1024]{2,1,0:T(8,128)(2,1)S(1)}, u32[]{:S(2)}, u32[]{:S(2)}) collective-permute-start(bf16[4,128,1024]{2,1,0:T(8,128)(2,1)} %over_y.1), channel_id=1, source_target_pairs={{0,16},{8,24},{16,0},{24,8},{32,48},{40,56},{48,32},{56,40},{64,80... | collective-permute-start | bytes 3145736 | tf_op jit(solution)/shard_map/sum_y_second/ppermute | solution.py:415
  11.4 0.0 collective-permute-done.refs_1_
  11.4 0.0 collective-permute-done.1.refs_2_
  11.4 3.3 %away_x.1 = (bf16[2,128,1024]{2,1,0:T(8,128)(2,1)}, bf16[2,128,1024]{2,1,0:T(8,128)(2,1)}, bf16[2,128,1024]{2,1,0:T(8,128)(2,1)}, bf16[4,128,1024]{2,1,0:T(8,128)(2,1)}) custom-call(s32[3]{0:T(128)S(1)} %pad_add_fusion.1.scal_ref, bf16[4,2,2,2,128,1024]{5,4,3,2,1,0:T(8,128)(2,1)} %bitcast.23, bf16[4,128,1024]{2,1,0:T(8,128)(2,1)S(1)} %collective-permute-done.refs_1_, ...), custom_call_target="tpu_custom_call" | custom-call | flops 1000000 | bytes 65536 | tf_op jit(solution)/shard_map/sum_x_first/away_x/pallas_call | solution.py:104
  14.7 0.2 collective-permute-start.6
  14.9 1.5 %collective-permute-start.3 = (bf16[2,128,1024]{2,1,0:T(8,128)(2,1)}, bf16[2,128,1024]{2,1,0:T(8,128)(2,1)}, u32[]{:S(2)}, u32[]{:S(2)}) collective-permute-start(bf16[2,128,1024]{2,1,0:T(8,128)(2,1)} %get-tuple-element.53), channel_id=1, source_target_pairs={{0,32},{8,40},{16,48},{24,56},{32,64},{40,72},{48,80},{56,88},{64,... | collective-permute-start | bytes 1572872 | tf_op jit(solution)/shard_map/sum_x_first/ppermute | solution.py:415
  16.4 1.7 %collective-permute-start.4 = (bf16[2,128,1024]{2,1,0:T(8,128)(2,1)}, bf16[2,128,1024]{2,1,0:T(8,128)(2,1)}, u32[]{:S(2)}, u32[]{:S(2)}) collective-permute-start(bf16[2,128,1024]{2,1,0:T(8,128)(2,1)} %get-tuple-element.54), channel_id=1, source_target_pairs={{0,96},{8,104},{16,112},{24,120},{32,0},{40,8},{48,16},{56,24},{64... | collective-permute-start | bytes 1572872 | tf_op jit(solution)/shard_map/sum_x_first/ppermute | solution.py:415
  18.2 1.8 %collective-permute-start.5 = (bf16[2,128,1024]{2,1,0:T(8,128)(2,1)}, bf16[2,128,1024]{2,1,0:T(8,128)(2,1)}, u32[]{:S(2)}, u32[]{:S(2)}) collective-permute-start(bf16[2,128,1024]{2,1,0:T(8,128)(2,1)} %get-tuple-element.55), channel_id=1, source_target_pairs={{0,64},{8,72},{16,80},{24,88},{32,96},{40,104},{48,112},{56,120},{... | collective-permute-start | bytes 1572872 | tf_op jit(solution)/shard_map/sum_x_first/ppermute | solution.py:415
  20.0 0.0 copy-done.3
  20.0 0.7 fusion
  21.3 0.0 copy-done.4
  21.3 0.6 fusion.1
  21.9 0.7 stack.79
  22.6 0.7 stack.77
  23.4 0.0 copy-start
  23.4 3.4 %copy-done = bf16[1024,4096]{1,0:T(8,128)(2,1)S(1)} copy-done((bf16[1024,4096]{1,0:T(8,128)(2,1)S(1)}, bf16[1024,4096]{1,0:T(8,128)(2,1)}, u32[]{:S(2)}) %copy-start) | copy-done | bytes 8388632
  26.7 1.2 %copy-done.2 = bf16[512,1024]{1,0:T(8,128)(2,1)S(1)} copy-done((bf16[512,1024]{1,0:T(8,128)(2,1)S(1)}, bf16[512,1024]{1,0:T(8,128)(2,1)}, u32[]{:S(2)}) %copy-start.2) | copy-done | bytes 1048600
  28.0 7.2 %cand_project.1 = (bf16[512,1024]{1,0:T(8,128)(2,1)S(1)}, bf16[512,1024]{1,0:T(8,128)(2,1)S(1)}, bf16[512,1024]{1,0:T(8,128)(2,1)S(1)}, bf16[512,512]{1,0:T(8,128)(2,1)S(1)}, f32[512,1024]{1,0:T(8,128)S(1)}) custom-call(s32[1,512]{1,0:T(1,128)S(1)} %bitcast.19, bf16[512,1024]{1,0:T(8,128)(2,1)S(1)} %copy-done.2, bf16[1024,4096]{1,0:T(8,128)(2,1)S(1)} %copy-done), custom_call_target="tpu_custom_call" | custom-call | flops 1000000 | bytes 65536 | tf_op jit(solution)/shard_map/cand_project/pallas_call | solution.py:210
  35.2 0.3 collective-permute-done.7.refs_2_
  35.4 0.0 collective-permute-done.6.refs_1_
  35.4 2.8 %join_y.1 = (bf16[128,1024]{1,0:T(8,128)(2,1)}, bf16[128,1024]{1,0:T(8,128)(2,1)}, bf16[128,1024]{1,0:T(8,128)(2,1)}) custom-call(s32[3]{0:T(128)S(1)} %pad_add_fusion.1.scal_ref, bf16[4,2,2,2,128,1024]{5,4,3,2,1,0:T(8,128)(2,1)} %bitcast.24, bf16[4,128,1024]{2,1,0:T(8,128)(2,1)} %collective-permute-done.6.refs_1_, ...), custom_call_target="tpu_custom_call" | custom-call | flops 1000000 | bytes 65536 | tf_op jit(solution)/shard_map/sum_y_second/join_y/pallas_call | solution.py:104
  38.3 1.6 %collective-permute-start.9 = (bf16[128,1024]{1,0:T(8,128)(2,1)}, bf16[128,1024]{1,0:T(8,128)(2,1)S(1)}, u32[]{:S(2)}, u32[]{:S(2)}) collective-permute-start(bf16[128,1024]{1,0:T(8,128)(2,1)} %get-tuple-element.59), channel_id=1, source_target_pairs={{0,32},{8,40},{16,48},{24,56},{32,64},{40,72},{48,80},{56,88},{64,... | collective-permute-start | bytes 786440 | tf_op jit(solution)/shard_map/sum_y_second/ppermute | solution.py:415
  39.9 1.7 %collective-permute-start.10 = (bf16[128,1024]{1,0:T(8,128)(2,1)}, bf16[128,1024]{1,0:T(8,128)(2,1)S(1)}, u32[]{:S(2)}, u32[]{:S(2)}) collective-permute-start(bf16[128,1024]{1,0:T(8,128)(2,1)} %get-tuple-element.60), channel_id=1, source_target_pairs={{0,96},{8,104},{16,112},{24,120},{32,0},{40,8},{48,16},{56,24},{64... | collective-permute-start | bytes 786440 | tf_op jit(solution)/shard_map/sum_y_second/ppermute | solution.py:415
  41.6 0.0 collective-permute-done.3.refs_3_
  41.6 1.9 %collective-permute-start.11 = (bf16[128,1024]{1,0:T(8,128)(2,1)}, bf16[128,1024]{1,0:T(8,128)(2,1)S(1)}, u32[]{:S(2)}, u32[]{:S(2)}) collective-permute-start(bf16[128,1024]{1,0:T(8,128)(2,1)} %get-tuple-element.61), channel_id=1, source_target_pairs={{0,64},{8,72},{16,80},{24,88},{32,96},{40,104},{48,112},{56,120},{... | collective-permute-start | bytes 786440 | tf_op jit(solution)/shard_map/sum_y_second/ppermute | solution.py:415
  43.5 0.0 collective-permute-done.4.refs_4_
  43.5 0.0 collective-permute-done.5.refs_5_
  43.5 2.6 %join_x.1 = (f32[128,1024]{1,0:T(8,128)S(1)}, bf16[128,1024]{1,0:T(8,128)(2,1)S(1)}) custom-call(s32[3]{0:T(128)S(1)} %pad_add_fusion.1.scal_ref, bf16[4,2,2,2,128,1024]{5,4,3,2,1,0:T(8,128)(2,1)} %bitcast.25, bf16[4,128,1024]{2,1,0:T(8,128)(2,1)S(1)} %collective-permute-done.refs_1_, bf16[4,128,1024]{2,1,0:T(8,128)(2,1)S(1)} %collective-permute-done.1.refs_2_, ...), custom_call_target="tpu_custom_call" | custom-call | flops 1000000 | bytes 65536 | tf_op jit(solution)/shard_map/sum_x_first/join_x/pallas_call | solution.py:104
  46.1 1.7 %collective-permute-start.8 = (bf16[128,1024]{1,0:T(8,128)(2,1)S(1)}, bf16[128,1024]{1,0:T(8,128)(2,1)S(1)}, u32[]{:S(2)}, u32[]{:S(2)}) collective-permute-start(bf16[128,1024]{1,0:T(8,128)(2,1)S(1)} %get-tuple-element.66), channel_id=1, source_target_pairs={{0,16},{8,24},{16,0},{24,8},{32,48},{40,56},{48,32},{56,40},{64,80... | collective-permute-start | bytes 786440 | tf_op jit(solution)/shard_map/sum_x_first/ppermute | solution.py:415
  47.8 1.4 %collective-permute-done.9.refs_3_ = bf16[128,1024]{1,0:T(8,128)(2,1)S(1)} collective-permute-done((bf16[128,1024]{1,0:T(8,128)(2,1)}, bf16[128,1024]{1,0:T(8,128)(2,1)S(1)}, u32[]{:S(2)}, u32[]{:S(2)}) %collective-permute-start.9) | collective-permute-done | bytes 262176 | tf_op jit(solution)/shard_map/sum_y_second/ppermute | solution.py:415
  49.2 0.2 collective-permute-done.10.refs_4_
  49.4 5.0 %collective-permute-done.11.refs_5_ = bf16[128,1024]{1,0:T(8,128)(2,1)S(1)} collective-permute-done((bf16[128,1024]{1,0:T(8,128)(2,1)}, bf16[128,1024]{1,0:T(8,128)(2,1)S(1)}, u32[]{:S(2)}, u32[]{:S(2)}) %collective-permute-start.11) | collective-permute-done | bytes 262176 | tf_op jit(solution)/shard_map/sum_y_second/ppermute | solution.py:415
  54.4 2.9 %norm_sum.1.refs_2_ = bf16[128,1024]{1,0:T(8,128)(2,1)S(1)} custom-call(s32[3]{0:T(128)S(1)} %pad_add_fusion.1.scal_ref, bf16[4,2,2,2,128,1024]{5,4,3,2,1,0:T(8,128)(2,1)} %bitcast.26, bf16[4,128,1024]{2,1,0:T(8,128)(2,1)} %collective-permute-done.6.refs_1_, bf16[4,128,1024]{2,1,0:T(8,128)(2,1)S(1)} %collective-permute-done.7.refs_2_, ...), custom_call_target="tpu_custom_call" | custom-call | flops 1000000 | bytes 65536 | tf_op jit(solution)/shard_map/gather/norm_sum/pallas_call | solution.py:104
  57.3 0.0 collective-permute-done.8.refs_1_
  57.3 1.5 %norm_both.1.refs_0_.refs_8_ = bf16[2,128,1024]{2,1,0:T(8,128)(2,1)S(1)} custom-call(s32[3]{0:T(128)S(1)} %pad_add_fusion.1.scal_ref, f32[128,1024]{1,0:T(8,128)S(1)} %get-tuple-element.65.refs_0_, bf16[128,1024]{1,0:T(8,128)(2,1)S(1)} %collective-permute-done.8.refs_1_, bf16[128,1024]{1,0:T(8,128)(2,1)S(1)} %norm_sum.1.refs_2_), custom_call_target="tpu_custom_call" | custom-call | flops 1000000 | bytes 65536 | tf_op jit(solution)/shard_map/gather/norm_both/pallas_call | solution.py:104
  58.8 3.3 %collective-permute-start.14 = (bf16[2,128,1024]{2,1,0:T(8,128)(2,1)S(1)}, bf16[2,128,1024]{2,1,0:T(8,128)(2,1)S(1)}, u32[]{:S(2)}, u32[]{:S(2)}) collective-permute-start(bf16[2,128,1024]{2,1,0:T(8,128)(2,1)S(1)} %norm_both.1.refs_0_.refs_8_), channel_id=1, source_target_pairs={{0,1},{1,0},{2,3},{3,2},{4,5},{5,4},{6,7},{7,6},{8,9},{9,8},{10,11... | collective-permute-start | bytes 1572872 | tf_op jit(solution)/shard_map/gather/ppermute | solution.py:419
  62.0 4.0 %collective-permute-start.13 = (bf16[2,128,1024]{2,1,0:T(8,128)(2,1)S(1)}, bf16[2,128,1024]{2,1,0:T(8,128)(2,1)S(1)}, u32[]{:S(2)}, u32[]{:S(2)}) collective-permute-start(bf16[2,128,1024]{2,1,0:T(8,128)(2,1)S(1)} %norm_both.1.refs_0_.refs_8_), channel_id=1, source_target_pairs={{0,6},{1,7},{2,0},{3,1},{4,2},{5,3},{6,4},{7,5},{8,14},{9,15},{10,... | collective-permute-start | bytes 1572872 | tf_op jit(solution)/shard_map/gather/ppermute | solution.py:419
  66.1 0.0 collective-permute-start.12
  66.1 0.0 slice-done
  66.1 4.4 %own_keys.1 = (f32[512,1024]{1,0:T(8,128)S(1)}, f32[256,1024]{1,0:T(8,128)S(1)}, bf16[256,1024]{1,0:T(8,128)(2,1)S(1)}, bf16[256,1024]{1,0:T(8,128)(2,1)S(1)}) custom-call(s32[2,12]{1,0:T(2,128)S(1)} %pad_add_fusion.scal_ref, bf16[2,128,1024]{2,1,0:T(8,128)(2,1)S(1)} %norm_both.1.refs_0_.refs_8_, ...), custom_call_target="tpu_custom_call", output_to_operand_aliasing={{0}: (4, {})} | custom-call | flops 1000000 | bytes 65536 | tf_op jit(solution)/shard_map/own_keys/pallas_call | solution.py:210
  70.5 2.6 %collective-permute-done.14.refs_2_ = bf16[2,128,1024]{2,1,0:T(8,128)(2,1)S(1)} collective-permute-done((bf16[2,128,1024]{2,1,0:T(8,128)(2,1)S(1)}, bf16[2,128,1024]{2,1,0:T(8,128)(2,1)S(1)}, u32[]{:S(2)}, u32[]{:S(2)}) %collective-permute-start.14) | collective-permute-done | bytes 524320 | tf_op jit(solution)/shard_map/gather/ppermute | solution.py:419
  73.0 4.0 %collective-permute-start.17 = (bf16[2,128,1024]{2,1,0:T(8,128)(2,1)S(1)}, bf16[2,128,1024]{2,1,0:T(8,128)(2,1)S(1)}, u32[]{:S(2)}, u32[]{:S(2)}) collective-permute-start(bf16[2,128,1024]{2,1,0:T(8,128)(2,1)S(1)} %collective-permute-done.14.refs_2_), channel_id=1, source_target_pairs={{0,6},{1,7},{2,0},{3,1},{4,2},{5,3},{6,4},{7,5},{8,14},{9,15},{10,... | collective-permute-start | bytes 1572872 | tf_op jit(solution)/shard_map/gather/ppermute | solution.py:419
  77.1 0.0 collective-permute-start.16
  77.1 0.0 collective-permute-done.13.refs_1_
  77.1 3.1 %collective-permute-done.12.refs_0_ = bf16[2,128,1024]{2,1,0:T(8,128)(2,1)S(1)} collective-permute-done((bf16[2,128,1024]{2,1,0:T(8,128)(2,1)S(1)}, bf16[2,128,1024]{2,1,0:T(8,128)(2,1)S(1)}, u32[]{:S(2)}, u32[]{:S(2)}) %collective-permute-start.12) | collective-permute-done | bytes 524320 | tf_op jit(solution)/shard_map/gather/ppermute | solution.py:419
  80.2 0.0 collective-permute-start.15
  80.2 7.8 %own_sides.1 = (f32[512,1024]{1,0:T(8,128)S(1)}, f32[256,1024]{1,0:T(8,128)S(1)}) custom-call(s32[2,12]{1,0:T(2,128)S(1)} %pad_add_fusion.scal_ref, bf16[2,128,1024]{2,1,0:T(8,128)(2,1)S(1)} %collective-permute-done.12.refs_0_, bf16[2,128,1024]{2,1,0:T(8,128)(2,1)S(1)} %collective-permute-done.13.refs_1_, ...), custom_call_target="tpu_custom_call", output_to_operand_aliasing={{0}: (6, {}), {1}: (8, {})} | custom-call | flops 1000000 | bytes 65536 | tf_op jit(solution)/shard_map/own_sides/pallas_call | solution.py:210
  88.1 0.0 collective-permute-done.17.refs_1_
  88.1 5.1 %collective-permute-done.16.refs_0_ = bf16[2,128,1024]{2,1,0:T(8,128)(2,1)S(1)} collective-permute-done((bf16[2,128,1024]{2,1,0:T(8,128)(2,1)S(1)}, bf16[2,128,1024]{2,1,0:T(8,128)(2,1)S(1)}, u32[]{:S(2)}, u32[]{:S(2)}) %collective-permute-start.16) | collective-permute-done | bytes 524320 | tf_op jit(solution)/shard_map/gather/ppermute | solution.py:419
  93.2 0.0 collective-permute-start.18
  93.2 5.1 %near_sides.1 = (f32[512,1024]{1,0:T(8,128)S(1)}, f32[256,1024]{1,0:T(8,128)S(1)}) custom-call(s32[2,12]{1,0:T(2,128)S(1)} %pad_add_fusion.scal_ref, bf16[2,128,1024]{2,1,0:T(8,128)(2,1)S(1)} %collective-permute-done.16.refs_0_, bf16[2,128,1024]{2,1,0:T(8,128)(2,1)S(1)} %collective-permute-done.17.refs_1_, ...), custom_call_target="tpu_custom_call", output_to_operand_aliasing={{0}: (5, {}), {1}: (7, {})} | custom-call | flops 1000000 | bytes 65536 | tf_op jit(solution)/shard_map/near_sides/pallas_call | solution.py:210
  98.2 3.7 %collective-permute-done.15.refs_0_ = bf16[2,128,1024]{2,1,0:T(8,128)(2,1)S(1)} collective-permute-done((bf16[2,128,1024]{2,1,0:T(8,128)(2,1)S(1)}, bf16[2,128,1024]{2,1,0:T(8,128)(2,1)S(1)}, u32[]{:S(2)}, u32[]{:S(2)}) %collective-permute-start.15) | collective-permute-done | bytes 524320 | tf_op jit(solution)/shard_map/gather/ppermute | solution.py:419
  101.9 0.4 collective-permute-done.18.refs_1_
  102.3 10.0 %far_finish.1 = (bf16[2,128,1024]{2,1,0:T(8,128)(2,1)}, bf16[512,1024]{1,0:T(8,128)(2,1)}) custom-call(s32[2,12]{1,0:T(2,128)S(1)} %pad_add_fusion.scal_ref, bf16[2,128,1024]{2,1,0:T(8,128)(2,1)S(1)} %collective-permute-done.15.refs_0_, bf16[2,128,1024]{2,1,0:T(8,128)(2,1)S(1)} %collective-permute-done.18.refs_1_, bf16[1024,4096]{1,0:T(8,128)(2,1)S(1)} %bitcast.18, ...), custom_call_target="tpu_custom_call" | custom-call | flops 1000000 | bytes 65536 | tf_op jit(solution)/shard_map/far_finish/pallas_call | solution.py:210
  (8 shorter events, 0.0 us)
Async XLA Ops:
  3.3 3.7 %collective-permute-start.2 = (bf16[4,128,1024]{2,1,0:T(8,128)(2,1)}, bf16[4,128,1024]{2,1,0:T(8,128)(2,1)S(1)}, u32[]{:S(2)}, u32[]{:S(2)}) collective-permute-start(bf16[4,128,1024]{2,1,0:T(8,128)(2,1)} %pack.1), channel_id=1, source_target_pairs={{0,8},{8,0},{16,24},{24,16},{32,40},{40,32},{48,56},{56,48},{64,72... | collective-permute-start | bytes 3145736 | tf_op jit(solution)/shard_map/sum_core/ppermute | solution.py:415
  6.3 5.1 %collective-permute-start = (bf16[4,128,1024]{2,1,0:T(8,128)(2,1)}, bf16[4,128,1024]{2,1,0:T(8,128)(2,1)S(1)}, u32[]{:S(2)}, u32[]{:S(2)}) collective-permute-start(bf16[4,128,1024]{2,1,0:T(8,128)(2,1)} %get-tuple-element.46), channel_id=1, source_target_pairs={{0,8},{8,0},{16,24},{24,16},{32,40},{40,32},{48,56},{56,48},{64,72... | collective-permute-start | bytes 3145736 | tf_op jit(solution)/shard_map/sum_core/ppermute | solution.py:415
  6.9 4.5 %collective-permute-start.1 = (bf16[4,128,1024]{2,1,0:T(8,128)(2,1)}, bf16[4,128,1024]{2,1,0:T(8,128)(2,1)S(1)}, u32[]{:S(2)}, u32[]{:S(2)}) collective-permute-start(bf16[4,128,1024]{2,1,0:T(8,128)(2,1)} %get-tuple-element.47), channel_id=1, source_target_pairs={{0,8},{8,0},{16,24},{24,16},{32,40},{40,32},{48,56},{56,48},{64,72... | collective-permute-start | bytes 3145736 | tf_op jit(solution)/shard_map/sum_core/ppermute | solution.py:415
  9.6 10.4 %copy-start.3 = (s32[512]{0:T(512)S(1)}, s32[512]{0:T(512)}, u32[]{:S(2)}) copy-start(s32[512]{0:T(512)} %param.9) | copy-start | bytes 6148
  9.6 11.6 %copy-start.4 = (s32[2]{0:T(128)S(1)}, s32[2]{0:T(128)}, u32[]{:S(2)}) copy-start(s32[2]{0:T(128)} %param.8) | copy-start | bytes 28
  9.7 25.8 %collective-permute-start.7 = (bf16[4,128,1024]{2,1,0:T(8,128)(2,1)}, bf16[4,128,1024]{2,1,0:T(8,128)(2,1)S(1)}, u32[]{:S(2)}, u32[]{:S(2)}) collective-permute-start(bf16[4,128,1024]{2,1,0:T(8,128)(2,1)} %over_y.1), channel_id=1, source_target_pairs={{0,16},{8,24},{16,0},{24,8},{32,48},{40,56},{48,32},{56,40},{64,80... | collective-permute-start | bytes 3145736 | tf_op jit(solution)/shard_map/sum_y_second/ppermute | solution.py:415
  14.7 20.8 %collective-permute-start.6 = (bf16[4,128,1024]{2,1,0:T(8,128)(2,1)}, bf16[4,128,1024]{2,1,0:T(8,128)(2,1)}, u32[]{:S(2)}, u32[]{:S(2)}) collective-permute-start(bf16[4,128,1024]{2,1,0:T(8,128)(2,1)} %get-tuple-element.51), channel_id=1, source_target_pairs={{0,8},{8,0},{16,24},{24,16},{32,40},{40,32},{48,56},{56,48},{64,72... | collective-permute-start | bytes 3145736 | tf_op jit(solution)/shard_map/sum_core/ppermute | solution.py:415
  14.9 26.7 %collective-permute-start.3 = (bf16[2,128,1024]{2,1,0:T(8,128)(2,1)}, bf16[2,128,1024]{2,1,0:T(8,128)(2,1)}, u32[]{:S(2)}, u32[]{:S(2)}) collective-permute-start(bf16[2,128,1024]{2,1,0:T(8,128)(2,1)} %get-tuple-element.53), channel_id=1, source_target_pairs={{0,32},{8,40},{16,48},{24,56},{32,64},{40,72},{48,80},{56,88},{64,... | collective-permute-start | bytes 1572872 | tf_op jit(solution)/shard_map/sum_x_first/ppermute | solution.py:415
  16.4 27.1 %collective-permute-start.4 = (bf16[2,128,1024]{2,1,0:T(8,128)(2,1)}, bf16[2,128,1024]{2,1,0:T(8,128)(2,1)}, u32[]{:S(2)}, u32[]{:S(2)}) collective-permute-start(bf16[2,128,1024]{2,1,0:T(8,128)(2,1)} %get-tuple-element.54), channel_id=1, source_target_pairs={{0,96},{8,104},{16,112},{24,120},{32,0},{40,8},{48,16},{56,24},{64... | collective-permute-start | bytes 1572872 | tf_op jit(solution)/shard_map/sum_x_first/ppermute | solution.py:415
  18.2 25.3 %collective-permute-start.5 = (bf16[2,128,1024]{2,1,0:T(8,128)(2,1)}, bf16[2,128,1024]{2,1,0:T(8,128)(2,1)}, u32[]{:S(2)}, u32[]{:S(2)}) collective-permute-start(bf16[2,128,1024]{2,1,0:T(8,128)(2,1)} %get-tuple-element.55), channel_id=1, source_target_pairs={{0,64},{8,72},{16,80},{24,88},{32,96},{40,104},{48,112},{56,120},{... | collective-permute-start | bytes 1572872 | tf_op jit(solution)/shard_map/sum_x_first/ppermute | solution.py:415
  23.4 3.4 %copy-start = (bf16[1024,4096]{1,0:T(8,128)(2,1)S(1)}, bf16[1024,4096]{1,0:T(8,128)(2,1)}, u32[]{:S(2)}) copy-start(bf16[1024,4096]{1,0:T(8,128)(2,1)} %refs_2_.3) | copy-start | bytes 25165828
  26.7 1.2 %copy-start.2 = (bf16[512,1024]{1,0:T(8,128)(2,1)S(1)}, bf16[512,1024]{1,0:T(8,128)(2,1)}, u32[]{:S(2)}) copy-start(bf16[512,1024]{1,0:T(8,128)(2,1)} %feats_ref.1) | copy-start | bytes 3145732
  38.3 10.9 %collective-permute-start.9 = (bf16[128,1024]{1,0:T(8,128)(2,1)}, bf16[128,1024]{1,0:T(8,128)(2,1)S(1)}, u32[]{:S(2)}, u32[]{:S(2)}) collective-permute-start(bf16[128,1024]{1,0:T(8,128)(2,1)} %get-tuple-element.59), channel_id=1, source_target_pairs={{0,32},{8,40},{16,48},{24,56},{32,64},{40,72},{48,80},{56,88},{64,... | collective-permute-start | bytes 786440 | tf_op jit(solution)/shard_map/sum_y_second/ppermute | solution.py:415
  39.9 9.5 %collective-permute-start.10 = (bf16[128,1024]{1,0:T(8,128)(2,1)}, bf16[128,1024]{1,0:T(8,128)(2,1)S(1)}, u32[]{:S(2)}, u32[]{:S(2)}) collective-permute-start(bf16[128,1024]{1,0:T(8,128)(2,1)} %get-tuple-element.60), channel_id=1, source_target_pairs={{0,96},{8,104},{16,112},{24,120},{32,0},{40,8},{48,16},{56,24},{64... | collective-permute-start | bytes 786440 | tf_op jit(solution)/shard_map/sum_y_second/ppermute | solution.py:415
  41.6 12.8 %collective-permute-start.11 = (bf16[128,1024]{1,0:T(8,128)(2,1)}, bf16[128,1024]{1,0:T(8,128)(2,1)S(1)}, u32[]{:S(2)}, u32[]{:S(2)}) collective-permute-start(bf16[128,1024]{1,0:T(8,128)(2,1)} %get-tuple-element.61), channel_id=1, source_target_pairs={{0,64},{8,72},{16,80},{24,88},{32,96},{40,104},{48,112},{56,120},{... | collective-permute-start | bytes 786440 | tf_op jit(solution)/shard_map/sum_y_second/ppermute | solution.py:415
  43.5 22.6 %slice-start = ((s8[8388608]{0:T(1024)(128)(4,1)}), s8[4194304]{0:T(1024)(128)(4,1)S(1)}, s32[]{:S(2)}) async-start(s8[8388608]{0:T(1024)(128)(4,1)} %bitcast.17), calls=%async_computation | async-start | bytes 8388608
  46.1 11.1 %collective-permute-start.8 = (bf16[128,1024]{1,0:T(8,128)(2,1)S(1)}, bf16[128,1024]{1,0:T(8,128)(2,1)S(1)}, u32[]{:S(2)}, u32[]{:S(2)}) collective-permute-start(bf16[128,1024]{1,0:T(8,128)(2,1)S(1)} %get-tuple-element.66), channel_id=1, source_target_pairs={{0,16},{8,24},{16,0},{24,8},{32,48},{40,56},{48,32},{56,40},{64,80... | collective-permute-start | bytes 786440 | tf_op jit(solution)/shard_map/sum_x_first/ppermute | solution.py:415
  54.4 11.7 %slice-start.1 = ((s8[8388608]{0:T(1024)(128)(4,1)}), s8[4194304]{0:T(1024)(128)(4,1)S(1)}, s32[]{:S(2)}) async-start(s8[8388608]{0:T(1024)(128)(4,1)} %bitcast.17), calls=%async_computation.1 | async-start | bytes 8388608
  58.8 14.3 %collective-permute-start.14 = (bf16[2,128,1024]{2,1,0:T(8,128)(2,1)S(1)}, bf16[2,128,1024]{2,1,0:T(8,128)(2,1)S(1)}, u32[]{:S(2)}, u32[]{:S(2)}) collective-permute-start(bf16[2,128,1024]{2,1,0:T(8,128)(2,1)S(1)} %norm_both.1.refs_0_.refs_8_), channel_id=1, source_target_pairs={{0,1},{1,0},{2,3},{3,2},{4,5},{5,4},{6,7},{7,6},{8,9},{9,8},{10,11... | collective-permute-start | bytes 1572872 | tf_op jit(solution)/shard_map/gather/ppermute | solution.py:419
  62.0 15.0 %collective-permute-start.13 = (bf16[2,128,1024]{2,1,0:T(8,128)(2,1)S(1)}, bf16[2,128,1024]{2,1,0:T(8,128)(2,1)S(1)}, u32[]{:S(2)}, u32[]{:S(2)}) collective-permute-start(bf16[2,128,1024]{2,1,0:T(8,128)(2,1)S(1)} %norm_both.1.refs_0_.refs_8_), channel_id=1, source_target_pairs={{0,6},{1,7},{2,0},{3,1},{4,2},{5,3},{6,4},{7,5},{8,14},{9,15},{10,... | collective-permute-start | bytes 1572872 | tf_op jit(solution)/shard_map/gather/ppermute | solution.py:419
  66.1 14.2 %collective-permute-start.12 = (bf16[2,128,1024]{2,1,0:T(8,128)(2,1)S(1)}, bf16[2,128,1024]{2,1,0:T(8,128)(2,1)S(1)}, u32[]{:S(2)}, u32[]{:S(2)}) collective-permute-start(bf16[2,128,1024]{2,1,0:T(8,128)(2,1)S(1)} %norm_both.1.refs_0_.refs_8_), channel_id=1, source_target_pairs={{0,2},{1,3},{2,4},{3,5},{4,6},{5,7},{6,0},{7,1},{8,10},{9,11},{10,... | collective-permute-start | bytes 1572872 | tf_op jit(solution)/shard_map/gather/ppermute | solution.py:419
  73.0 15.0 %collective-permute-start.17 = (bf16[2,128,1024]{2,1,0:T(8,128)(2,1)S(1)}, bf16[2,128,1024]{2,1,0:T(8,128)(2,1)S(1)}, u32[]{:S(2)}, u32[]{:S(2)}) collective-permute-start(bf16[2,128,1024]{2,1,0:T(8,128)(2,1)S(1)} %collective-permute-done.14.refs_2_), channel_id=1, source_target_pairs={{0,6},{1,7},{2,0},{3,1},{4,2},{5,3},{6,4},{7,5},{8,14},{9,15},{10,... | collective-permute-start | bytes 1572872 | tf_op jit(solution)/shard_map/gather/ppermute | solution.py:419
  77.1 16.1 %collective-permute-start.16 = (bf16[2,128,1024]{2,1,0:T(8,128)(2,1)S(1)}, bf16[2,128,1024]{2,1,0:T(8,128)(2,1)S(1)}, u32[]{:S(2)}, u32[]{:S(2)}) collective-permute-start(bf16[2,128,1024]{2,1,0:T(8,128)(2,1)S(1)} %collective-permute-done.14.refs_2_), channel_id=1, source_target_pairs={{0,2},{1,3},{2,4},{3,5},{4,6},{5,7},{6,0},{7,1},{8,10},{9,11},{10,... | collective-permute-start | bytes 1572872 | tf_op jit(solution)/shard_map/gather/ppermute | solution.py:419
  80.2 21.7 %collective-permute-start.15 = (bf16[2,128,1024]{2,1,0:T(8,128)(2,1)S(1)}, bf16[2,128,1024]{2,1,0:T(8,128)(2,1)S(1)}, u32[]{:S(2)}, u32[]{:S(2)}) collective-permute-start(bf16[2,128,1024]{2,1,0:T(8,128)(2,1)S(1)} %collective-permute-done.12.refs_0_), channel_id=1, source_target_pairs={{0,2},{1,3},{2,4},{3,5},{4,6},{5,7},{6,0},{7,1},{8,10},{9,11},{10,... | collective-permute-start | bytes 1572872 | tf_op jit(solution)/shard_map/gather/ppermute | solution.py:419
  93.2 9.2 %collective-permute-start.18 = (bf16[2,128,1024]{2,1,0:T(8,128)(2,1)S(1)}, bf16[2,128,1024]{2,1,0:T(8,128)(2,1)S(1)}, u32[]{:S(2)}, u32[]{:S(2)}) collective-permute-start(bf16[2,128,1024]{2,1,0:T(8,128)(2,1)S(1)} %collective-permute-done.17.refs_1_), channel_id=1, source_target_pairs={{0,6},{1,7},{2,0},{3,1},{4,2},{5,3},{6,4},{7,5},{8,14},{9,15},{10,... | collective-permute-start | bytes 1572872 | tf_op jit(solution)/shard_map/gather/ppermute | solution.py:419
  93.2 9.2 %copy-start.1 = (bf16[1024,1024]{1,0:T(8,128)(2,1)S(1)}, bf16[1024,1024]{1,0:T(8,128)(2,1)}, u32[]{:S(2)}) copy-start(bf16[1024,1024]{1,0:T(8,128)(2,1)} %refs_12_.1) | copy-start | bytes 6291460
where the time goes:
time: 113 us; the launch traced here: 112 us
  Pallas kernels  55.7 us (49%)
  starting transfers between devices  26 us (23%)
  waiting for transfers between devices  21.8 us (19%)
  local copies, waits for them, and re-layouts  6.67 us (6%)
  between operations  1.47 us (1%)
    pallas_call x5, Pallas kernels, kernel_call(): pl.pallas_call(body, in_specs=in_specs, out_specs=[vmem] * len(out_shape)...  34.5 us
    pallas_call x8, Pallas kernels, block_sums(): pl.pallas_call(body, in_specs=[pl.BlockSpec(memory_space=pltpu.SMEM)] + [...  21.2 us
    ppermute x7, waiting for transfers between devices, to_cand(): return lax.ppermute(array, 'cand', cand_perm(dz, dy))  14.9 us
    ppermute x12, starting transfers between devices, to_user(): return lax.ppermute(array, 'user', user_perm(dx, dy, dcore))  14.6 us
    ppermute x7, starting transfers between devices, to_cand(): return lax.ppermute(array, 'cand', cand_perm(dz, dy))  11.4 us
    ppermute x12, waiting for transfers between devices, to_user(): return lax.ppermute(array, 'user', user_perm(dx, dy, dcore))  6.9 us
    unnamed x14, local copies, waits for them, and re-layouts  4.62 us
  transfers between devices with their start and end apart: 19, of which 9 were waited for; matrix products, arithmetic and copies ran while one was open for 2% of the time, Pallas kernels for 37%

commit v1 on v0

--- a/solution.py
+++ b/solution.py
@@ -60,59 +60,52 @@
     return pl.CostEstimate(flops=10**6, bytes_accessed=1 << 16, transcendentals=0)
 
 
-def block_sums(name, scal, arrays, shapes, sums, hbm=True):
-    loads = [part for _, _, parts, _ in sums for part in parts]
+def block_sums(name, scal, arrays, shapes, sums):
+    added = [part for _, _, parts, _ in sums if len(parts) > 1 for part in parts]
+    n_loads = sum(len(parts) for _, _, parts, _ in sums)
 
     def body(scal_ref, *refs):
         ins, refs = refs[: len(arrays)], refs[len(arrays) :]
         outs, refs = refs[: len(shapes)], refs[len(shapes) :]
-        bufs, refs = refs[: len(loads)], refs[len(loads) :]
-        res, (in_sems, out_sems) = refs[: len(sums)], refs[len(sums) :]
-        copies = []
-        for n, (at, index) in enumerate(loads):
-            lead = index(scal_ref)
-            src = ins[at].at[lead] if lead else ins[at]
-            copies.append(pltpu.make_async_copy(src, bufs[n], in_sems.at[n]))
-            copies[-1].start()
-        stores, used = [], 0
-        for n, (out, lead, parts, norm) in enumerate(sums):
-            members = range(used, used + len(parts))
-            used += len(parts)
-            for k in members:
-                copies[k].wait()
-            ready = bufs[members[0]]
-            if len(parts) > 1:
-                ready = res[n]
-
-                @pl.loop(0, SLOTS // 32)
-                def _(r):
-                    rows = pl.ds(pl.multiple_of(r * 32, 32), 32)
-                    total = None
-                    for k in members:
-                        value = bufs[k][rows, :].astype(F32)
-                        total = value if total is None else total + value
-                    ready[rows, :] = (layer_norm(total) if norm else total).astype(ready.dtype)
-
+        bufs, in_sems = list(refs[: len(added)]), refs[len(added)]
+        work, count = [], 0
+        for out, lead, parts, norm in sums:
             lead = (lead(scal_ref),) if callable(lead) else lead
             dst = outs[out].at[lead] if lead else outs[out]
-            stores.append(pltpu.make_async_copy(ready, dst, out_sems.at[n]))
-            stores[-1].start()
-        for store in stores:
-            store.wait()
-
-    spec = pl.BlockSpec(memory_space=pltpu.HBM)
+            copies, held = [], []
+            for at, index in parts:
+                from_ = index(scal_ref)
+                src = ins[at].at[from_] if from_ else ins[at]
+                to = bufs.pop(0) if len(parts) > 1 else dst
+                copies.append(pltpu.make_async_copy(src, to, in_sems.at[count]))
+                copies[-1].start()
+                held.append(to)
+                count += 1
+            work.append((dst, copies, held, norm))
+        for dst, copies, held, norm in work:
+            for copy in copies:
+                copy.wait()
+            if len(held) > 1:
+                step = SLOTS if norm else SLOTS // 2
+
+                @pl.loop(0, SLOTS // step)
+                def _(r):
+                    rows = pl.ds(pl.multiple_of(r * step, step), step)
+                    total = None
+                    for ref in held:
+                        value = ref[rows, :].astype(F32)
+                        total = value if total is None else total + value
+                    dst[rows, :] = (layer_norm(total) if norm else total).astype(dst.dtype)
+
+    hbm, anywhere = pl.BlockSpec(memory_space=pltpu.HBM), pl.BlockSpec(memory_space=pl.ANY)
     return pl.pallas_call(
         body,
         in_specs=[pl.BlockSpec(memory_space=pltpu.SMEM)]
-        + [spec if a.ndim == 6 else pl.BlockSpec(memory_space=pl.ANY) for a in arrays],
-        out_specs=[spec if hbm else pl.BlockSpec(memory_space=pl.ANY)] * len(shapes),
-        out_shape=[(pltpu.HBM if hbm else jax.ShapeDtypeStruct)(shape, dtype) for shape, dtype in shapes],
-        scratch_shapes=[pltpu.VMEM((SLOTS, D), arrays[at].dtype) for at, _ in loads]
-        + [
-            pltpu.VMEM((SLOTS if len(parts) > 1 else 16, D), shapes[out][1])
-            for out, _, parts, _ in sums
-        ]
-        + [pltpu.SemaphoreType.DMA((len(loads),)), pltpu.SemaphoreType.DMA((len(sums),))],
+        + [hbm if a.ndim == 6 else anywhere for a in arrays],
+        out_specs=[pl.BlockSpec(memory_space=pltpu.VMEM)] * len(shapes),
+        out_shape=[jax.ShapeDtypeStruct(shape, dtype) for shape, dtype in shapes],
+        scratch_shapes=[pltpu.VMEM((SLOTS, D), arrays[at].dtype) for at, _ in added]
+        + [pltpu.SemaphoreType.DMA((n_loads,))],
         compiler_params=pltpu.CompilerParams(vmem_limit_bytes=VMEM),
         cost_estimate=cost(),
         name=name,
@@ -165,7 +158,7 @@
         parts = [(0, lambda s, side=side: (s[0], side(s), s[2], 0)), (1 + n, lambda s: (s[0],))]
         parts += [(3 + k, lambda s, side=side: (side(s),)) for k in range(3)]
         sums.append((n, (), parts, False))
-    return block_sums("join_x", place, arrays, [((SLOTS, D), F32), ((SLOTS, D), BF16)], sums, False)
+    return block_sums("join_x", place, arrays, [((SLOTS, D), F32), ((SLOTS, D), BF16)], sums)
 
 
 def join_y(place, tables, got, arrived):
@@ -188,13 +181,13 @@
         (2, lambda s: (s[0],)),
     ] + [(3 + n, lambda s: ()) for n in range(3)]
     arrays = [tables, got, side] + list(arrived)
-    return block_sums("norm_sum", place, arrays, [((SLOTS, D), BF16)], [(0, (), parts, True)], False)[0]
+    return block_sums("norm_sum", place, arrays, [((SLOTS, D), BF16)], [(0, (), parts, True)])[0]
 
 
 def norm_both(place, first, second):
     parts = [(n, lambda s: ()) for n in range(len(first) + 1)]
     sums = [(0, (1,), parts[-1:], False), (0, (0,), parts[:-1], True)]
-    return block_sums("norm_both", place, list(first) + [second], [((2, SLOTS, D), BF16)], sums, False)[0]
+    return block_sums("norm_both", place, list(first) + [second], [((2, SLOTS, D), BF16)], sums)[0]
 
 
 def in_vmem(array):

time: 113 us -> 111 us (0.982)
  waiting for transfers between devices: 21.8 us -> 24.7 us
  Pallas kernels: 55.7 us -> 53 us
  starting transfers between devices: 26 us -> 24.1 us
    pallas_call x8, Pallas kernels: 21.2 us -> 18.4 us  [block_sums(): pl.pallas_call(body, in_specs=[pl.BlockSpec(memory_space=pltpu.SMEM)] + [...]
    ppermute x12, waiting for transfers between devices: 6.9 us -> 8.86 us  [to_user(): return lax.ppermute(array, 'user', user_perm(dx, dy, dcore))]
    ppermute x12, starting transfers between devices: 14.6 us -> 13 us  [to_user(): return lax.ppermute(array, 'user', user_perm(dx, dy, dcore))]
  transfers between devices with their start and end apart: 19 -> 19, of which waited for: 9 -> 9; matrix products, arithmetic and copies ran while one was open for 2% -> 2% of each run, Pallas kernels for 37% -> 36%
where the time goes in v1:
time: 111 us
  Pallas kernels  53 us (48%)
  waiting for transfers between devices  24.7 us (22%)
  starting transfers between devices  24.1 us (22%)
  local copies, waits for them, and re-layouts  6.67 us (6%)
  between operations  1.47 us (1%)
    pallas_call x5, Pallas kernels, kernel_call(): pl.pallas_call(body, in_specs=in_specs, out_specs=[vmem] * len(out_shape)...  34.6 us
    pallas_call x8, Pallas kernels, block_sums(): pl.pallas_call(body, in_specs=[pl.BlockSpec(memory_space=pltpu.SMEM)] + [...  18.4 us
    ppermute x7, waiting for transfers between devices, to_cand(): return lax.ppermute(array, 'cand', cand_perm(dz, dy))  15.9 us
    ppermute x12, starting transfers between devices, to_user(): return lax.ppermute(array, 'user', user_perm(dx, dy, dcore))  13 us
    ppermute x7, starting transfers between devices, to_cand(): return lax.ppermute(array, 'cand', cand_perm(dz, dy))  11.1 us
    ppermute x12, waiting for transfers between devices, to_user(): return lax.ppermute(array, 'user', user_perm(dx, dy, dcore))  8.86 us
    unnamed x14, local copies, waits for them, and re-layouts  4.62 us
  transfers between devices with their start and end apart: 19, of which 9 were waited for; matrix products, arithmetic and copies ran while one was open for 2% of the time, Pallas kernels for 36%

profile of v1, /device:TPU:0, one launch (start us, length us, event | category | flops | bytes accessed | tf_op | source)
XLA Modules:
  0.0 110.7 jit_solution(12681417208849096432)
XLA Ops:
  0.6 0.1 pad_add_fusion.1.scal_ref
  0.7 1.8 %pack.1 = bf16[4,128,1024]{2,1,0:T(8,128)(2,1)S(1)} custom-call(s32[3]{0:T(128)S(1)} %pad_add_fusion.1.scal_ref, bf16[4,2,2,2,128,1024]{5,4,3,2,1,0:T(8,128)(2,1)} %bitcast.20), custom_call_target="tpu_custom_call" | custom-call | flops 1000000 | bytes 65536 | tf_op jit(solution)/shard_map/sum_core/pack/pallas_call | solution.py:101
  2.5 0.1 collective-permute-start.2
  2.6 2.1 %pack_all.1 = (bf16[4,128,1024]{2,1,0:T(8,128)(2,1)S(1)}, bf16[4,128,1024]{2,1,0:T(8,128)(2,1)S(1)}) custom-call(s32[3]{0:T(128)S(1)} %pad_add_fusion.1.scal_ref, bf16[4,2,2,2,128,1024]{5,4,3,2,1,0:T(8,128)(2,1)} %bitcast.21), custom_call_target="tpu_custom_call" | custom-call | flops 1000000 | bytes 65536 | tf_op jit(solution)/shard_map/sum_core/pack_all/pallas_call | solution.py:101
  4.7 0.6 collective-permute-start
  5.3 0.1 collective-permute-start.1
  5.4 0.0 collective-permute-done.2.refs_1_
  5.4 2.9 %over_y.1 = bf16[4,128,1024]{2,1,0:T(8,128)(2,1)} custom-call(s32[3]{0:T(128)S(1)} %pad_add_fusion.1.scal_ref, bf16[4,2,2,2,128,1024]{5,4,3,2,1,0:T(8,128)(2,1)} %bitcast.22, bf16[4,128,1024]{2,1,0:T(8,128)(2,1)S(1)} %collective-permute-done.2.refs_1_), custom_call_target="tpu_custom_call" | custom-call | flops 1000000 | bytes 65536 | tf_op jit(solution)/shard_map/sum_y_second/over_y/pallas_call | solution.py:101
  8.2 0.0 copy-start.3
  8.2 0.0 copy-start.4
  8.3 1.7 %collective-permute-start.7 = (bf16[4,128,1024]{2,1,0:T(8,128)(2,1)}, bf16[4,128,1024]{2,1,0:T(8,128)(2,1)S(1)}, u32[]{:S(2)}, u32[]{:S(2)}) collective-permute-start(bf16[4,128,1024]{2,1,0:T(8,128)(2,1)} %over_y.1), channel_id=1, source_target_pairs={{0,16},{8,24},{16,0},{24,8},{32,48},{40,56},{48,32},{56,40},{64,80... | collective-permute-start | bytes 3145736 | tf_op jit(solution)/shard_map/sum_y_second/ppermute | solution.py:408
  10.0 0.0 collective-permute-done.refs_1_
  10.0 0.0 collective-permute-done.1.refs_2_
  10.0 3.9 %away_x.1 = (bf16[2,128,1024]{2,1,0:T(8,128)(2,1)}, bf16[2,128,1024]{2,1,0:T(8,128)(2,1)}, bf16[2,128,1024]{2,1,0:T(8,128)(2,1)}, bf16[4,128,1024]{2,1,0:T(8,128)(2,1)}) custom-call(s32[3]{0:T(128)S(1)} %pad_add_fusion.1.scal_ref, bf16[4,2,2,2,128,1024]{5,4,3,2,1,0:T(8,128)(2,1)} %bitcast.23, bf16[4,128,1024]{2,1,0:T(8,128)(2,1)S(1)} %collective-permute-done.refs_1_, ...), custom_call_target="tpu_custom_call" | custom-call | flops 1000000 | bytes 65536 | tf_op jit(solution)/shard_map/sum_x_first/away_x/pallas_call | solution.py:101
  13.9 0.2 collective-permute-start.6
  14.1 1.5 %collective-permute-start.3 = (bf16[2,128,1024]{2,1,0:T(8,128)(2,1)}, bf16[2,128,1024]{2,1,0:T(8,128)(2,1)}, u32[]{:S(2)}, u32[]{:S(2)}) collective-permute-start(bf16[2,128,1024]{2,1,0:T(8,128)(2,1)} %get-tuple-element.53), channel_id=1, source_target_pairs={{0,32},{8,40},{16,48},{24,56},{32,64},{40,72},{48,80},{56,88},{64,... | collective-permute-start | bytes 1572872 | tf_op jit(solution)/shard_map/sum_x_first/ppermute | solution.py:408
  15.6 1.7 %collective-permute-start.4 = (bf16[2,128,1024]{2,1,0:T(8,128)(2,1)}, bf16[2,128,1024]{2,1,0:T(8,128)(2,1)}, u32[]{:S(2)}, u32[]{:S(2)}) collective-permute-start(bf16[2,128,1024]{2,1,0:T(8,128)(2,1)} %get-tuple-element.54), channel_id=1, source_target_pairs={{0,96},{8,104},{16,112},{24,120},{32,0},{40,8},{48,16},{56,24},{64... | collective-permute-start | bytes 1572872 | tf_op jit(solution)/shard_map/sum_x_first/ppermute | solution.py:408
  17.4 1.8 %collective-permute-start.5 = (bf16[2,128,1024]{2,1,0:T(8,128)(2,1)}, bf16[2,128,1024]{2,1,0:T(8,128)(2,1)}, u32[]{:S(2)}, u32[]{:S(2)}) collective-permute-start(bf16[2,128,1024]{2,1,0:T(8,128)(2,1)} %get-tuple-element.55), channel_id=1, source_target_pairs={{0,64},{8,72},{16,80},{24,88},{32,96},{40,104},{48,112},{56,120},{... | collective-permute-start | bytes 1572872 | tf_op jit(solution)/shard_map/sum_x_first/ppermute | solution.py:408
  19.2 0.0 copy-done.3
  19.2 0.7 fusion
  20.5 0.0 copy-done.4
  20.5 0.6 fusion.1
  21.1 0.7 stack.79
  21.8 0.7 stack.77
  22.6 0.0 copy-start
  22.6 3.4 %copy-done = bf16[1024,4096]{1,0:T(8,128)(2,1)S(1)} copy-done((bf16[1024,4096]{1,0:T(8,128)(2,1)S(1)}, bf16[1024,4096]{1,0:T(8,128)(2,1)}, u32[]{:S(2)}) %copy-start) | copy-done | bytes 8388632
  25.9 1.2 %copy-done.2 = bf16[512,1024]{1,0:T(8,128)(2,1)S(1)} copy-done((bf16[512,1024]{1,0:T(8,128)(2,1)S(1)}, bf16[512,1024]{1,0:T(8,128)(2,1)}, u32[]{:S(2)}) %copy-start.2) | copy-done | bytes 1048600
  27.2 7.2 %cand_project.1 = (bf16[512,1024]{1,0:T(8,128)(2,1)S(1)}, bf16[512,1024]{1,0:T(8,128)(2,1)S(1)}, bf16[512,1024]{1,0:T(8,128)(2,1)S(1)}, bf16[512,512]{1,0:T(8,128)(2,1)S(1)}, f32[512,1024]{1,0:T(8,128)S(1)}) custom-call(s32[1,512]{1,0:T(1,128)S(1)} %bitcast.19, bf16[512,1024]{1,0:T(8,128)(2,1)S(1)} %copy-done.2, bf16[1024,4096]{1,0:T(8,128)(2,1)S(1)} %copy-done), custom_call_target="tpu_custom_call" | custom-call | flops 1000000 | bytes 65536 | tf_op jit(solution)/shard_map/cand_project/pallas_call | solution.py:203
  34.4 0.0 collective-permute-done.7.refs_2_
  34.4 0.0 collective-permute-done.6.refs_1_
  34.4 2.1 %join_y.1 = (bf16[128,1024]{1,0:T(8,128)(2,1)S(1)}, bf16[128,1024]{1,0:T(8,128)(2,1)S(1)}, bf16[128,1024]{1,0:T(8,128)(2,1)S(1)}) custom-call(s32[3]{0:T(128)S(1)} %pad_add_fusion.1.scal_ref, bf16[4,2,2,2,128,1024]{5,4,3,2,1,0:T(8,128)(2,1)} %bitcast.24, bf16[4,128,1024]{2,1,0:T(8,128)(2,1)} %collective-permute-done.6.refs_1_, ...), custom_call_target="tpu_custom_call" | custom-call | flops 1000000 | bytes 65536 | tf_op jit(solution)/shard_map/sum_y_second/join_y/pallas_call | solution.py:101
  36.5 1.3 %collective-permute-start.9 = (bf16[128,1024]{1,0:T(8,128)(2,1)S(1)}, bf16[128,1024]{1,0:T(8,128)(2,1)S(1)}, u32[]{:S(2)}, u32[]{:S(2)}) collective-permute-start(bf16[128,1024]{1,0:T(8,128)(2,1)S(1)} %get-tuple-element.59), channel_id=1, source_target_pairs={{0,32},{8,40},{16,48},{24,56},{32,64},{40,72},{48,80},{56,88},{64,... | collective-permute-start | bytes 786440 | tf_op jit(solution)/shard_map/sum_y_second/ppermute | solution.py:408
  37.8 2.0 %collective-permute-start.10 = (bf16[128,1024]{1,0:T(8,128)(2,1)S(1)}, bf16[128,1024]{1,0:T(8,128)(2,1)S(1)}, u32[]{:S(2)}, u32[]{:S(2)}) collective-permute-start(bf16[128,1024]{1,0:T(8,128)(2,1)S(1)} %get-tuple-element.60), channel_id=1, source_target_pairs={{0,96},{8,104},{16,112},{24,120},{32,0},{40,8},{48,16},{56,24},{64... | collective-permute-start | bytes 786440 | tf_op jit(solution)/shard_map/sum_y_second/ppermute | solution.py:408
  39.8 0.0 collective-permute-done.3.refs_3_
  39.8 1.5 %collective-permute-start.11 = (bf16[128,1024]{1,0:T(8,128)(2,1)S(1)}, bf16[128,1024]{1,0:T(8,128)(2,1)S(1)}, u32[]{:S(2)}, u32[]{:S(2)}) collective-permute-start(bf16[128,1024]{1,0:T(8,128)(2,1)S(1)} %get-tuple-element.61), channel_id=1, source_target_pairs={{0,64},{8,72},{16,80},{24,88},{32,96},{40,104},{48,112},{56,120},{... | collective-permute-start | bytes 786440 | tf_op jit(solution)/shard_map/sum_y_second/ppermute | solution.py:408
  41.4 0.0 collective-permute-done.4.refs_4_
  41.4 1.3 %collective-permute-done.5.refs_5_ = bf16[2,128,1024]{2,1,0:T(8,128)(2,1)} collective-permute-done((bf16[2,128,1024]{2,1,0:T(8,128)(2,1)}, bf16[2,128,1024]{2,1,0:T(8,128)(2,1)}, u32[]{:S(2)}, u32[]{:S(2)}) %collective-permute-start.5) | collective-permute-done | bytes 524320 | tf_op jit(solution)/shard_map/sum_x_first/ppermute | solution.py:408
  42.6 2.6 %join_x.1 = (f32[128,1024]{1,0:T(8,128)S(1)}, bf16[128,1024]{1,0:T(8,128)(2,1)S(1)}) custom-call(s32[3]{0:T(128)S(1)} %pad_add_fusion.1.scal_ref, bf16[4,2,2,2,128,1024]{5,4,3,2,1,0:T(8,128)(2,1)} %bitcast.25, bf16[4,128,1024]{2,1,0:T(8,128)(2,1)S(1)} %collective-permute-done.refs_1_, bf16[4,128,1024]{2,1,0:T(8,128)(2,1)S(1)} %collective-permute-done.1.refs_2_, ...), custom_call_target="tpu_custom_call" | custom-call | flops 1000000 | bytes 65536 | tf_op jit(solution)/shard_map/sum_x_first/join_x/pallas_call | solution.py:101
  45.2 0.4 collective-permute-start.8
  45.6 2.5 %collective-permute-done.9.refs_3_ = bf16[128,1024]{1,0:T(8,128)(2,1)S(1)} collective-permute-done((bf16[128,1024]{1,0:T(8,128)(2,1)S(1)}, bf16[128,1024]{1,0:T(8,128)(2,1)S(1)}, u32[]{:S(2)}, u32[]{:S(2)}) %collective-permute-start.9) | collective-permute-done | bytes 262176 | tf_op jit(solution)/shard_map/sum_y_second/ppermute | solution.py:408
  48.1 0.0 collective-permute-done.10.refs_4_
  48.1 5.0 %collective-permute-done.11.refs_5_ = bf16[128,1024]{1,0:T(8,128)(2,1)S(1)} collective-permute-done((bf16[128,1024]{1,0:T(8,128)(2,1)S(1)}, bf16[128,1024]{1,0:T(8,128)(2,1)S(1)}, u32[]{:S(2)}, u32[]{:S(2)}) %collective-permute-start.11) | collective-permute-done | bytes 262176 | tf_op jit(solution)/shard_map/sum_y_second/ppermute | solution.py:408
  53.2 2.3 %norm_sum.1.refs_2_ = bf16[128,1024]{1,0:T(8,128)(2,1)S(1)} custom-call(s32[3]{0:T(128)S(1)} %pad_add_fusion.1.scal_ref, bf16[4,2,2,2,128,1024]{5,4,3,2,1,0:T(8,128)(2,1)} %bitcast.26, bf16[4,128,1024]{2,1,0:T(8,128)(2,1)} %collective-permute-done.6.refs_1_, bf16[4,128,1024]{2,1,0:T(8,128)(2,1)S(1)} %collective-permute-done.7.refs_2_, ...), custom_call_target="tpu_custom_call" | custom-call | flops 1000000 | bytes 65536 | tf_op jit(solution)/shard_map/gather/norm_sum/pallas_call | solution.py:101
  55.5 0.0 collective-permute-done.8.refs_1_
  55.5 0.9 norm_both.1.refs_0_.refs_8_
  56.4 3.0 %collective-permute-start.14 = (bf16[2,128,1024]{2,1,0:T(8,128)(2,1)S(1)}, bf16[2,128,1024]{2,1,0:T(8,128)(2,1)S(1)}, u32[]{:S(2)}, u32[]{:S(2)}) collective-permute-start(bf16[2,128,1024]{2,1,0:T(8,128)(2,1)S(1)} %norm_both.1.refs_0_.refs_8_), channel_id=1, source_target_pairs={{0,1},{1,0},{2,3},{3,2},{4,5},{5,4},{6,7},{7,6},{8,9},{9,8},{10,11... | collective-permute-start | bytes 1572872 | tf_op jit(solution)/shard_map/gather/ppermute | solution.py:412
  59.4 4.0 %collective-permute-start.13 = (bf16[2,128,1024]{2,1,0:T(8,128)(2,1)S(1)}, bf16[2,128,1024]{2,1,0:T(8,128)(2,1)S(1)}, u32[]{:S(2)}, u32[]{:S(2)}) collective-permute-start(bf16[2,128,1024]{2,1,0:T(8,128)(2,1)S(1)} %norm_both.1.refs_0_.refs_8_), channel_id=1, source_target_pairs={{0,6},{1,7},{2,0},{3,1},{4,2},{5,3},{6,4},{7,5},{8,14},{9,15},{10,... | collective-permute-start | bytes 1572872 | tf_op jit(solution)/shard_map/gather/ppermute | solution.py:412
  63.4 0.0 collective-permute-start.12
  63.4 0.0 slice-done
  63.4 4.4 %own_keys.1 = (f32[512,1024]{1,0:T(8,128)S(1)}, f32[256,1024]{1,0:T(8,128)S(1)}, bf16[256,1024]{1,0:T(8,128)(2,1)S(1)}, bf16[256,1024]{1,0:T(8,128)(2,1)S(1)}) custom-call(s32[2,12]{1,0:T(2,128)S(1)} %pad_add_fusion.scal_ref, bf16[2,128,1024]{2,1,0:T(8,128)(2,1)S(1)} %norm_both.1.refs_0_.refs_8_, ...), custom_call_target="tpu_custom_call", output_to_operand_aliasing={{0}: (4, {})} | custom-call | flops 1000000 | bytes 65536 | tf_op jit(solution)/shard_map/own_keys/pallas_call | solution.py:203
  67.8 3.5 %collective-permute-done.14.refs_2_ = bf16[2,128,1024]{2,1,0:T(8,128)(2,1)S(1)} collective-permute-done((bf16[2,128,1024]{2,1,0:T(8,128)(2,1)S(1)}, bf16[2,128,1024]{2,1,0:T(8,128)(2,1)S(1)}, u32[]{:S(2)}, u32[]{:S(2)}) %collective-permute-start.14) | collective-permute-done | bytes 524320 | tf_op jit(solution)/shard_map/gather/ppermute | solution.py:412
  71.3 4.0 %collective-permute-start.17 = (bf16[2,128,1024]{2,1,0:T(8,128)(2,1)S(1)}, bf16[2,128,1024]{2,1,0:T(8,128)(2,1)S(1)}, u32[]{:S(2)}, u32[]{:S(2)}) collective-permute-start(bf16[2,128,1024]{2,1,0:T(8,128)(2,1)S(1)} %collective-permute-done.14.refs_2_), channel_id=1, source_target_pairs={{0,6},{1,7},{2,0},{3,1},{4,2},{5,3},{6,4},{7,5},{8,14},{9,15},{10,... | collective-permute-start | bytes 1572872 | tf_op jit(solution)/shard_map/gather/ppermute | solution.py:412
  75.4 0.0 collective-permute-start.16
  75.4 0.0 collective-permute-done.13.refs_1_
  75.4 2.0 %collective-permute-done.12.refs_0_ = bf16[2,128,1024]{2,1,0:T(8,128)(2,1)S(1)} collective-permute-done((bf16[2,128,1024]{2,1,0:T(8,128)(2,1)S(1)}, bf16[2,128,1024]{2,1,0:T(8,128)(2,1)S(1)}, u32[]{:S(2)}, u32[]{:S(2)}) %collective-permute-start.12) | collective-permute-done | bytes 524320 | tf_op jit(solution)/shard_map/gather/ppermute | solution.py:412
  77.4 0.0 collective-permute-start.15
  77.4 7.8 %own_sides.1 = (f32[512,1024]{1,0:T(8,128)S(1)}, f32[256,1024]{1,0:T(8,128)S(1)}) custom-call(s32[2,12]{1,0:T(2,128)S(1)} %pad_add_fusion.scal_ref, bf16[2,128,1024]{2,1,0:T(8,128)(2,1)S(1)} %collective-permute-done.12.refs_0_, bf16[2,128,1024]{2,1,0:T(8,128)(2,1)S(1)} %collective-permute-done.13.refs_1_, ...), custom_call_target="tpu_custom_call", output_to_operand_aliasing={{0}: (6, {}), {1}: (8, {})} | custom-call | flops 1000000 | bytes 65536 | tf_op jit(solution)/shard_map/own_sides/pallas_call | solution.py:203
  85.3 0.1 collective-permute-done.17.refs_1_
  85.3 6.1 %collective-permute-done.16.refs_0_ = bf16[2,128,1024]{2,1,0:T(8,128)(2,1)S(1)} collective-permute-done((bf16[2,128,1024]{2,1,0:T(8,128)(2,1)S(1)}, bf16[2,128,1024]{2,1,0:T(8,128)(2,1)S(1)}, u32[]{:S(2)}, u32[]{:S(2)}) %collective-permute-start.16) | collective-permute-done | bytes 524320 | tf_op jit(solution)/shard_map/gather/ppermute | solution.py:412
  91.4 0.0 collective-permute-start.18
  91.4 5.1 %near_sides.1 = (f32[512,1024]{1,0:T(8,128)S(1)}, f32[256,1024]{1,0:T(8,128)S(1)}) custom-call(s32[2,12]{1,0:T(2,128)S(1)} %pad_add_fusion.scal_ref, bf16[2,128,1024]{2,1,0:T(8,128)(2,1)S(1)} %collective-permute-done.16.refs_0_, bf16[2,128,1024]{2,1,0:T(8,128)(2,1)S(1)} %collective-permute-done.17.refs_1_, ...), custom_call_target="tpu_custom_call", output_to_operand_aliasing={{0}: (5, {}), {1}: (7, {})} | custom-call | flops 1000000 | bytes 65536 | tf_op jit(solution)/shard_map/near_sides/pallas_call | solution.py:203
  96.5 3.5 %collective-permute-done.15.refs_0_ = bf16[2,128,1024]{2,1,0:T(8,128)(2,1)S(1)} collective-permute-done((bf16[2,128,1024]{2,1,0:T(8,128)(2,1)S(1)}, bf16[2,128,1024]{2,1,0:T(8,128)(2,1)S(1)}, u32[]{:S(2)}, u32[]{:S(2)}) %collective-permute-start.15) | collective-permute-done | bytes 524320 | tf_op jit(solution)/shard_map/gather/ppermute | solution.py:412
  100.0 0.6 collective-permute-done.18.refs_1_
  100.6 10.1 %far_finish.1 = (bf16[2,128,1024]{2,1,0:T(8,128)(2,1)}, bf16[512,1024]{1,0:T(8,128)(2,1)}) custom-call(s32[2,12]{1,0:T(2,128)S(1)} %pad_add_fusion.scal_ref, bf16[2,128,1024]{2,1,0:T(8,128)(2,1)S(1)} %collective-permute-done.15.refs_0_, bf16[2,128,1024]{2,1,0:T(8,128)(2,1)S(1)} %collective-permute-done.18.refs_1_, bf16[1024,4096]{1,0:T(8,128)(2,1)S(1)} %bitcast.18, ...), custom_call_target="tpu_custom_call" | custom-call | flops 1000000 | bytes 65536 | tf_op jit(solution)/shard_map/far_finish/pallas_call | solution.py:203
  (8 shorter events, 0.0 us)
Async XLA Ops:
  2.5 2.9 %collective-permute-start.2 = (bf16[4,128,1024]{2,1,0:T(8,128)(2,1)S(1)}, bf16[4,128,1024]{2,1,0:T(8,128)(2,1)S(1)}, u32[]{:S(2)}, u32[]{:S(2)}) collective-permute-start(bf16[4,128,1024]{2,1,0:T(8,128)(2,1)S(1)} %pack.1), channel_id=1, source_target_pairs={{0,8},{8,0},{16,24},{24,16},{32,40},{40,32},{48,56},{56,48},{64,72... | collective-permute-start | bytes 3145736 | tf_op jit(solution)/shard_map/sum_core/ppermute | solution.py:408
  4.7 5.3 %collective-permute-start = (bf16[4,128,1024]{2,1,0:T(8,128)(2,1)S(1)}, bf16[4,128,1024]{2,1,0:T(8,128)(2,1)S(1)}, u32[]{:S(2)}, u32[]{:S(2)}) collective-permute-start(bf16[4,128,1024]{2,1,0:T(8,128)(2,1)S(1)} %get-tuple-element.46), channel_id=1, source_target_pairs={{0,8},{8,0},{16,24},{24,16},{32,40},{40,32},{48,56},{56,48},{64,72... | collective-permute-start | bytes 3145736 | tf_op jit(solution)/shard_map/sum_core/ppermute | solution.py:408
  5.3 4.7 %collective-permute-start.1 = (bf16[4,128,1024]{2,1,0:T(8,128)(2,1)S(1)}, bf16[4,128,1024]{2,1,0:T(8,128)(2,1)S(1)}, u32[]{:S(2)}, u32[]{:S(2)}) collective-permute-start(bf16[4,128,1024]{2,1,0:T(8,128)(2,1)S(1)} %get-tuple-element.47), channel_id=1, source_target_pairs={{0,8},{8,0},{16,24},{24,16},{32,40},{40,32},{48,56},{56,48},{64,72... | collective-permute-start | bytes 3145736 | tf_op jit(solution)/shard_map/sum_core/ppermute | solution.py:408
  8.2 10.9 %copy-start.3 = (s32[512]{0:T(512)S(1)}, s32[512]{0:T(512)}, u32[]{:S(2)}) copy-start(s32[512]{0:T(512)} %param.9) | copy-start | bytes 6148
  8.2 12.2 %copy-start.4 = (s32[2]{0:T(128)S(1)}, s32[2]{0:T(128)}, u32[]{:S(2)}) copy-start(s32[2]{0:T(128)} %param.8) | copy-start | bytes 28
  8.3 26.2 %collective-permute-start.7 = (bf16[4,128,1024]{2,1,0:T(8,128)(2,1)}, bf16[4,128,1024]{2,1,0:T(8,128)(2,1)S(1)}, u32[]{:S(2)}, u32[]{:S(2)}) collective-permute-start(bf16[4,128,1024]{2,1,0:T(8,128)(2,1)} %over_y.1), channel_id=1, source_target_pairs={{0,16},{8,24},{16,0},{24,8},{32,48},{40,56},{48,32},{56,40},{64,80... | collective-permute-start | bytes 3145736 | tf_op jit(solution)/shard_map/sum_y_second/ppermute | solution.py:408
  13.9 20.5 %collective-permute-start.6 = (bf16[4,128,1024]{2,1,0:T(8,128)(2,1)}, bf16[4,128,1024]{2,1,0:T(8,128)(2,1)}, u32[]{:S(2)}, u32[]{:S(2)}) collective-permute-start(bf16[4,128,1024]{2,1,0:T(8,128)(2,1)} %get-tuple-element.51), channel_id=1, source_target_pairs={{0,8},{8,0},{16,24},{24,16},{32,40},{40,32},{48,56},{56,48},{64,72... | collective-permute-start | bytes 3145736 | tf_op jit(solution)/shard_map/sum_core/ppermute | solution.py:408
  14.1 25.7 %collective-permute-start.3 = (bf16[2,128,1024]{2,1,0:T(8,128)(2,1)}, bf16[2,128,1024]{2,1,0:T(8,128)(2,1)}, u32[]{:S(2)}, u32[]{:S(2)}) collective-permute-start(bf16[2,128,1024]{2,1,0:T(8,128)(2,1)} %get-tuple-element.53), channel_id=1, source_target_pairs={{0,32},{8,40},{16,48},{24,56},{32,64},{40,72},{48,80},{56,88},{64,... | collective-permute-start | bytes 1572872 | tf_op jit(solution)/shard_map/sum_x_first/ppermute | solution.py:408
  15.6 25.7 %collective-permute-start.4 = (bf16[2,128,1024]{2,1,0:T(8,128)(2,1)}, bf16[2,128,1024]{2,1,0:T(8,128)(2,1)}, u32[]{:S(2)}, u32[]{:S(2)}) collective-permute-start(bf16[2,128,1024]{2,1,0:T(8,128)(2,1)} %get-tuple-element.54), channel_id=1, source_target_pairs={{0,96},{8,104},{16,112},{24,120},{32,0},{40,8},{48,16},{56,24},{64... | collective-permute-start | bytes 1572872 | tf_op jit(solution)/shard_map/sum_x_first/ppermute | solution.py:408
  17.4 25.3 %collective-permute-start.5 = (bf16[2,128,1024]{2,1,0:T(8,128)(2,1)}, bf16[2,128,1024]{2,1,0:T(8,128)(2,1)}, u32[]{:S(2)}, u32[]{:S(2)}) collective-permute-start(bf16[2,128,1024]{2,1,0:T(8,128)(2,1)} %get-tuple-element.55), channel_id=1, source_target_pairs={{0,64},{8,72},{16,80},{24,88},{32,96},{40,104},{48,112},{56,120},{... | collective-permute-start | bytes 1572872 | tf_op jit(solution)/shard_map/sum_x_first/ppermute | solution.py:408
  22.6 3.4 %copy-start = (bf16[1024,4096]{1,0:T(8,128)(2,1)S(1)}, bf16[1024,4096]{1,0:T(8,128)(2,1)}, u32[]{:S(2)}) copy-start(bf16[1024,4096]{1,0:T(8,128)(2,1)} %refs_2_.3) | copy-start | bytes 25165828
  25.9 1.2 %copy-start.2 = (bf16[512,1024]{1,0:T(8,128)(2,1)S(1)}, bf16[512,1024]{1,0:T(8,128)(2,1)}, u32[]{:S(2)}) copy-start(bf16[512,1024]{1,0:T(8,128)(2,1)} %feats_ref.1) | copy-start | bytes 3145732
  36.5 11.6 %collective-permute-start.9 = (bf16[128,1024]{1,0:T(8,128)(2,1)S(1)}, bf16[128,1024]{1,0:T(8,128)(2,1)S(1)}, u32[]{:S(2)}, u32[]{:S(2)}) collective-permute-start(bf16[128,1024]{1,0:T(8,128)(2,1)S(1)} %get-tuple-element.59), channel_id=1, source_target_pairs={{0,32},{8,40},{16,48},{24,56},{32,64},{40,72},{48,80},{56,88},{64,... | collective-permute-start | bytes 786440 | tf_op jit(solution)/shard_map/sum_y_second/ppermute | solution.py:408
  37.8 10.4 %collective-permute-start.10 = (bf16[128,1024]{1,0:T(8,128)(2,1)S(1)}, bf16[128,1024]{1,0:T(8,128)(2,1)S(1)}, u32[]{:S(2)}, u32[]{:S(2)}) collective-permute-start(bf16[128,1024]{1,0:T(8,128)(2,1)S(1)} %get-tuple-element.60), channel_id=1, source_target_pairs={{0,96},{8,104},{16,112},{24,120},{32,0},{40,8},{48,16},{56,24},{64... | collective-permute-start | bytes 786440 | tf_op jit(solution)/shard_map/sum_y_second/ppermute | solution.py:408
  39.8 13.3 %collective-permute-start.11 = (bf16[128,1024]{1,0:T(8,128)(2,1)S(1)}, bf16[128,1024]{1,0:T(8,128)(2,1)S(1)}, u32[]{:S(2)}, u32[]{:S(2)}) collective-permute-start(bf16[128,1024]{1,0:T(8,128)(2,1)S(1)} %get-tuple-element.61), channel_id=1, source_target_pairs={{0,64},{8,72},{16,80},{24,88},{32,96},{40,104},{48,112},{56,120},{... | collective-permute-start | bytes 786440 | tf_op jit(solution)/shard_map/sum_y_second/ppermute | solution.py:408
  42.6 20.8 %slice-start = ((s8[8388608]{0:T(1024)(128)(4,1)}), s8[4194304]{0:T(1024)(128)(4,1)S(1)}, s32[]{:S(2)}) async-start(s8[8388608]{0:T(1024)(128)(4,1)} %bitcast.17), calls=%async_computation | async-start | bytes 8388608
  45.2 10.3 %collective-permute-start.8 = (bf16[128,1024]{1,0:T(8,128)(2,1)S(1)}, bf16[128,1024]{1,0:T(8,128)(2,1)S(1)}, u32[]{:S(2)}, u32[]{:S(2)}) collective-permute-start(bf16[128,1024]{1,0:T(8,128)(2,1)S(1)} %get-tuple-element.66), channel_id=1, source_target_pairs={{0,16},{8,24},{16,0},{24,8},{32,48},{40,56},{48,32},{56,40},{64,80... | collective-permute-start | bytes 786440 | tf_op jit(solution)/shard_map/sum_x_first/ppermute | solution.py:408
  53.2 10.2 %slice-start.1 = ((s8[8388608]{0:T(1024)(128)(4,1)}), s8[4194304]{0:T(1024)(128)(4,1)S(1)}, s32[]{:S(2)}) async-start(s8[8388608]{0:T(1024)(128)(4,1)} %bitcast.17), calls=%async_computation.1 | async-start | bytes 8388608
  56.4 15.0 %collective-permute-start.14 = (bf16[2,128,1024]{2,1,0:T(8,128)(2,1)S(1)}, bf16[2,128,1024]{2,1,0:T(8,128)(2,1)S(1)}, u32[]{:S(2)}, u32[]{:S(2)}) collective-permute-start(bf16[2,128,1024]{2,1,0:T(8,128)(2,1)S(1)} %norm_both.1.refs_0_.refs_8_), channel_id=1, source_target_pairs={{0,1},{1,0},{2,3},{3,2},{4,5},{5,4},{6,7},{7,6},{8,9},{9,8},{10,11... | collective-permute-start | bytes 1572872 | tf_op jit(solution)/shard_map/gather/ppermute | solution.py:412
  59.4 16.0 %collective-permute-start.13 = (bf16[2,128,1024]{2,1,0:T(8,128)(2,1)S(1)}, bf16[2,128,1024]{2,1,0:T(8,128)(2,1)S(1)}, u32[]{:S(2)}, u32[]{:S(2)}) collective-permute-start(bf16[2,128,1024]{2,1,0:T(8,128)(2,1)S(1)} %norm_both.1.refs_0_.refs_8_), channel_id=1, source_target_pairs={{0,6},{1,7},{2,0},{3,1},{4,2},{5,3},{6,4},{7,5},{8,14},{9,15},{10,... | collective-permute-start | bytes 1572872 | tf_op jit(solution)/shard_map/gather/ppermute | solution.py:412
  63.4 14.0 %collective-permute-start.12 = (bf16[2,128,1024]{2,1,0:T(8,128)(2,1)S(1)}, bf16[2,128,1024]{2,1,0:T(8,128)(2,1)S(1)}, u32[]{:S(2)}, u32[]{:S(2)}) collective-permute-start(bf16[2,128,1024]{2,1,0:T(8,128)(2,1)S(1)} %norm_both.1.refs_0_.refs_8_), channel_id=1, source_target_pairs={{0,2},{1,3},{2,4},{3,5},{4,6},{5,7},{6,0},{7,1},{8,10},{9,11},{10,... | collective-permute-start | bytes 1572872 | tf_op jit(solution)/shard_map/gather/ppermute | solution.py:412
  71.3 14.0 %collective-permute-start.17 = (bf16[2,128,1024]{2,1,0:T(8,128)(2,1)S(1)}, bf16[2,128,1024]{2,1,0:T(8,128)(2,1)S(1)}, u32[]{:S(2)}, u32[]{:S(2)}) collective-permute-start(bf16[2,128,1024]{2,1,0:T(8,128)(2,1)S(1)} %collective-permute-done.14.refs_2_), channel_id=1, source_target_pairs={{0,6},{1,7},{2,0},{3,1},{4,2},{5,3},{6,4},{7,5},{8,14},{9,15},{10,... | collective-permute-start | bytes 1572872 | tf_op jit(solution)/shard_map/gather/ppermute | solution.py:412
  75.4 16.1 %collective-permute-start.16 = (bf16[2,128,1024]{2,1,0:T(8,128)(2,1)S(1)}, bf16[2,128,1024]{2,1,0:T(8,128)(2,1)S(1)}, u32[]{:S(2)}, u32[]{:S(2)}) collective-permute-start(bf16[2,128,1024]{2,1,0:T(8,128)(2,1)S(1)} %collective-permute-done.14.refs_2_), channel_id=1, source_target_pairs={{0,2},{1,3},{2,4},{3,5},{4,6},{5,7},{6,0},{7,1},{8,10},{9,11},{10,... | collective-permute-start | bytes 1572872 | tf_op jit(solution)/shard_map/gather/ppermute | solution.py:412
  77.4 22.6 %collective-permute-start.15 = (bf16[2,128,1024]{2,1,0:T(8,128)(2,1)S(1)}, bf16[2,128,1024]{2,1,0:T(8,128)(2,1)S(1)}, u32[]{:S(2)}, u32[]{:S(2)}) collective-permute-start(bf16[2,128,1024]{2,1,0:T(8,128)(2,1)S(1)} %collective-permute-done.12.refs_0_), channel_id=1, source_target_pairs={{0,2},{1,3},{2,4},{3,5},{4,6},{5,7},{6,0},{7,1},{8,10},{9,11},{10,... | collective-permute-start | bytes 1572872 | tf_op jit(solution)/shard_map/gather/ppermute | solution.py:412
  91.4 9.2 %collective-permute-start.18 = (bf16[2,128,1024]{2,1,0:T(8,128)(2,1)S(1)}, bf16[2,128,1024]{2,1,0:T(8,128)(2,1)S(1)}, u32[]{:S(2)}, u32[]{:S(2)}) collective-permute-start(bf16[2,128,1024]{2,1,0:T(8,128)(2,1)S(1)} %collective-permute-done.17.refs_1_), channel_id=1, source_target_pairs={{0,6},{1,7},{2,0},{3,1},{4,2},{5,3},{6,4},{7,5},{8,14},{9,15},{10,... | collective-permute-start | bytes 1572872 | tf_op jit(solution)/shard_map/gather/ppermute | solution.py:412
  91.4 9.2 %copy-start.1 = (bf16[1024,1024]{1,0:T(8,128)(2,1)S(1)}, bf16[1024,1024]{1,0:T(8,128)(2,1)}, u32[]{:S(2)}) copy-start(bf16[1024,1024]{1,0:T(8,128)(2,1)} %refs_12_.1) | copy-start | bytes 6291460

commit v2 on v1

--- a/solution.py
+++ b/solution.py
@@ -91,9 +91,10 @@
                 @pl.loop(0, SLOTS // step)
                 def _(r):
                     rows = pl.ds(pl.multiple_of(r * step, step), step)
+                    exact = len(held) == 2 and not norm and all(ref.dtype == BF16 for ref in held)
                     total = None
                     for ref in held:
-                        value = ref[rows, :].astype(F32)
+                        value = ref[rows, :] if exact else ref[rows, :].astype(F32)
                         total = value if total is None else total + value
                     dst[rows, :] = (layer_norm(total) if norm else total).astype(dst.dtype)
 
@@ -150,15 +151,18 @@
     return block_sums("away_x", place, [tables] + list(got), shapes, sums)
 
 
-def join_x(place, tables, got, arrived):
-    arrays = [tables] + list(got) + list(arrived)
+def join_x(place, tables, got, arrived, got1, side1):
+    arrays = [tables] + list(got) + list(arrived) + [got1, side1]
     sums = []
     for n in (1, 0):
         side = SIDES[n]
         parts = [(0, lambda s, side=side: (s[0], side(s), s[2], 0)), (1 + n, lambda s: (s[0],))]
         parts += [(3 + k, lambda s, side=side: (side(s),)) for k in range(3)]
         sums.append((n, (), parts, False))
-    return block_sums("join_x", place, arrays, [((SLOTS, D), F32), ((SLOTS, D), BF16)], sums)
+    parts = [(0, lambda s: (s[0], s[1], s[2], 1)), (6, lambda s: (s[0],)), (7, lambda s: (s[0],))]
+    sums.append((2, (), parts, False))
+    shapes = [((SLOTS, D), F32), ((SLOTS, D), BF16), ((SLOTS, D), F32)]
+    return block_sums("join_x", place, arrays, shapes, sums)
 
 
 def join_y(place, tables, got, arrived):
@@ -174,13 +178,8 @@
     return block_sums("join_y", place, [tables, got, arrived], [((SLOTS, D), BF16)] * 3, sums)
 
 
-def norm_sum(place, tables, got, side, arrived):
-    parts = [
-        (0, lambda s: (s[0], s[1], s[2], 1)),
-        (1, lambda s: (s[0],)),
-        (2, lambda s: (s[0],)),
-    ] + [(3 + n, lambda s: ()) for n in range(3)]
-    arrays = [tables, got, side] + list(arrived)
+def norm_sum(place, arrays):
+    parts = [(n, lambda s: ()) for n in range(len(arrays))]
     return block_sums("norm_sum", place, arrays, [((SLOTS, D), BF16)], [(0, (), parts, True)])[0]
 
 
@@ -194,7 +193,7 @@
     return pltpu.with_memory_space_constraint(array, pltpu.VMEM)
 
 
-def kernel_call(body, name, arrays, out_shape, scratch, scalars=None, aliases=None):
+def kernel_call(body, name, arrays, out_shape, scratch, scalars=None, aliases=None, out=pltpu.VMEM):
     vmem = pl.BlockSpec(memory_space=pltpu.VMEM)
     in_specs, args = [vmem] * len(arrays), [in_vmem(array) for array in arrays]
     if scalars is not None:
@@ -203,7 +202,7 @@
     return pl.pallas_call(
         body,
         in_specs=in_specs,
-        out_specs=[vmem] * len(out_shape),
+        out_specs=[pl.BlockSpec(memory_space=out)] * len(out_shape),
         out_shape=out_shape,
         scratch_shapes=scratch,
         input_output_aliases=aliases or {},
@@ -335,27 +334,44 @@
                 project(g + 1, n)
 
     if final:
-        (y_scr,) = take(1)
-        n_hist = 2 * SLOTS
-        y = layer_norm(ah_ref[...]) * uh_ref[...].astype(F32)
-        y_scr[:n_hist, :] = y.astype(BF16)
-
-        @pl.loop(0, ROWS // SLOTS)
-        def _(n):
-            rows = pl.ds(pl.multiple_of(n * SLOTS, SLOTS), SLOTS)
-            y = layer_norm(a_ref[rows, :]) * u_ref[rows, :].astype(F32)
-            y_scr[pl.ds(pl.multiple_of(n_hist + n * SLOTS, SLOTS), SLOTS), :] = y.astype(BF16)
-
-        @pl.loop(0, D // GROUP)
-        def _(g):
-            cols = pl.ds(pl.multiple_of(g * GROUP, GROUP), GROUP)
-            res = mm(y_scr[...], wo_ref[:, cols])
-            for user in (0, 1):
-                out = res[user * SLOTS : (user + 1) * SLOTS] + own_ref[user, :, cols].astype(F32)
-                keep = my_off + row_iota < scal_ref[user, 0]
-                hist_ref[user, :, cols] = jnp.where(keep, out, 0.0).astype(BF16)
-            done = (res[n_hist:] + xs_ref[:, cols].astype(F32)).astype(BF16)
-            cand_ref[:, cols] = mm(back_ref[...], done).astype(BF16)
+        y_scr, hist_vm, cand_vm, sems = take(4)
+        block = 2 * SLOTS
+        half = D // 2
+
+        def normed(n):
+            sums, gate = (ah_ref, uh_ref) if n == 0 else (a_ref, u_ref)
+            rows = slice(max(n - 1, 0) * block, (max(n - 1, 0) + 1) * block)
+            y = layer_norm(sums[rows, :]) * gate[rows, :].astype(F32)
+            y_scr[n * block : (n + 1) * block, :] = y.astype(BF16)
+
+        stores = [pltpu.make_async_copy(hist_vm, hist_ref, sems.at[0])]
+        for n in range(2):
+            cols = slice(n * half, (n + 1) * half)
+            stores.append(
+                pltpu.make_async_copy(cand_vm.at[:, cols], cand_ref.at[:, cols], sems.at[1 + n])
+            )
+        normed(0)
+        for n in range(1 + ROWS // block):
+            at = slice(n * block, (n + 1) * block)
+            res = mm(y_scr[at, :], wo_ref[...])
+            if n < ROWS // block:
+                normed(n + 1)
+            if n == 0:
+                res = res + own_ref[...].reshape(block, D).astype(F32)
+                for user in (0, 1):
+                    keep = my_off + row_iota < scal_ref[user, 0]
+                    out = res[user * SLOTS : (user + 1) * SLOTS]
+                    hist_vm[user] = jnp.where(keep, out, 0.0).astype(BF16)
+                stores[0].start()
+            else:
+                rows = slice((n - 1) * block, n * block)
+                y_scr[at, :] = (res + xs_ref[rows, :].astype(F32)).astype(BF16)
+        for n in range(2):
+            cols = slice(n * half, (n + 1) * half)
+            cand_vm[:, cols] = mm(back_ref[...], y_scr[block:, cols]).astype(BF16)
+            stores[1 + n].start()
+        for store in stores:
+            store.wait()
 
 
 def absorb(name, scal, items, w_in, q_cand, a_cand, state=None, final=None):
@@ -377,7 +393,12 @@
         arrays += [state[1]] + list(final)
         out_shape = [jax.ShapeDtypeStruct((2, SLOTS, D), BF16), jax.ShapeDtypeStruct((ROWS, D), BF16)]
         aliases = {}
-        scratch.append(pltpu.VMEM((2 * SLOTS + ROWS, D), BF16))
+        scratch += [
+            pltpu.VMEM((2 * SLOTS + ROWS, D), BF16),
+            pltpu.VMEM((2, SLOTS, D), BF16),
+            pltpu.VMEM((ROWS, D), BF16),
+            pltpu.SemaphoreType.DMA((3,)),
+        ]
     outs = kernel_call(
         functools.partial(absorb_kernel, (pieces, first, final is not None)),
         name,
@@ -386,6 +407,7 @@
         scratch,
         scal,
         aliases,
+        pl.ANY if final is not None else pltpu.VMEM,
     )
     if final is not None:
         return outs
@@ -449,10 +471,10 @@
         away1 = join_y(place, tables, got2, y1)
         x1 = [to_user(part, d, 0, 0) for part, d in zip(away1, HOPS)]
     with jax.named_scope("sum_x_first"):
-        mine0, over0 = join_x(place, tables, got0, after(x0, away1))
+        mine0, over0, mine1 = join_x(place, tables, got0, after(x0, away1), got2, y1)
         y0 = to_user(over0, 0, 1, 0)
     with jax.named_scope("gather"):
-        own1 = norm_sum(place, tables, got2, y1, after(x1, mine0))
+        own1 = norm_sum(place, [mine1] + after(x1, mine0))
         own = norm_both(place, [mine0, after(y0, own1)], own1)
         near = to_cand(own, 0, 1)
         own_left, own_right = to_cand(own, 1, 0), to_cand(own, -1, 0)

time: 111 us -> 109 us (0.982)
  Pallas kernels: 53 us -> 50.3 us
    pallas_call x8, Pallas kernels: 18.4 us -> 16.9 us  [block_sums(): pl.pallas_call(body, in_specs=[pl.BlockSpec(memory_space=pltpu.SMEM)] + [...]
    pallas_call x5, Pallas kernels: 34.6 us -> 33.4 us  [kernel_call(): pl.pallas_call(body, in_specs=in_specs, out_specs=[pl.BlockSpec(memory_sp...]
where the time goes in v2:
time: 109 us; the launch traced here: 108 us
  Pallas kernels  50.3 us (46%)
  waiting for transfers between devices  24.8 us (23%)
  starting transfers between devices  24.2 us (22%)
  local copies, waits for them, and re-layouts  6.67 us (6%)
  between operations  1.65 us (2%)
    pallas_call x5, Pallas kernels, kernel_call(): pl.pallas_call(body, in_specs=in_specs, out_specs=[pl.BlockSpec(memory_sp...  33.4 us
    pallas_call x8, Pallas kernels, block_sums(): pl.pallas_call(body, in_specs=[pl.BlockSpec(memory_space=pltpu.SMEM)] + [...  16.9 us
    ppermute x7, waiting for transfers between devices, to_cand(): return lax.ppermute(array, 'cand', cand_perm(dz, dy))  15.9 us
    ppermute x12, starting transfers between devices, to_user(): return lax.ppermute(array, 'user', user_perm(dx, dy, dcore))  13.1 us
    ppermute x7, starting transfers between devices, to_cand(): return lax.ppermute(array, 'cand', cand_perm(dz, dy))  11.1 us
    ppermute x12, waiting for transfers between devices, to_user(): return lax.ppermute(array, 'user', user_perm(dx, dy, dcore))  8.91 us
    unnamed x14, local copies, waits for them, and re-layouts  4.62 us
  transfers between devices with their start and end apart: 19, of which 9 were waited for; matrix products, arithmetic and copies ran while one was open for 2% of the time, Pallas kernels for 36%

profile of v2, /device:TPU:0, one launch (start us, length us, event | category | flops | bytes accessed | tf_op | source)
XLA Modules:
  0.0 108.3 jit_solution(4627099390259920163)
XLA Ops:
  0.6 0.1 pad_add_fusion.1.scal_ref
  0.7 1.8 %pack.1 = bf16[4,128,1024]{2,1,0:T(8,128)(2,1)S(1)} custom-call(s32[3]{0:T(128)S(1)} %pad_add_fusion.1.scal_ref, bf16[4,2,2,2,128,1024]{5,4,3,2,1,0:T(8,128)(2,1)} %bitcast.20), custom_call_target="tpu_custom_call" | custom-call | flops 1000000 | bytes 65536 | tf_op jit(solution)/shard_map/sum_core/pack/pallas_call | solution.py:102
  2.5 0.1 collective-permute-start.2
  2.6 2.1 %pack_all.1 = (bf16[4,128,1024]{2,1,0:T(8,128)(2,1)S(1)}, bf16[4,128,1024]{2,1,0:T(8,128)(2,1)S(1)}) custom-call(s32[3]{0:T(128)S(1)} %pad_add_fusion.1.scal_ref, bf16[4,2,2,2,128,1024]{5,4,3,2,1,0:T(8,128)(2,1)} %bitcast.21), custom_call_target="tpu_custom_call" | custom-call | flops 1000000 | bytes 65536 | tf_op jit(solution)/shard_map/sum_core/pack_all/pallas_call | solution.py:102
  4.7 0.6 collective-permute-start
  5.3 0.1 collective-permute-start.1
  5.4 0.0 collective-permute-done.2.refs_1_
  5.4 2.8 %over_y.1 = bf16[4,128,1024]{2,1,0:T(8,128)(2,1)} custom-call(s32[3]{0:T(128)S(1)} %pad_add_fusion.1.scal_ref, bf16[4,2,2,2,128,1024]{5,4,3,2,1,0:T(8,128)(2,1)} %bitcast.22, bf16[4,128,1024]{2,1,0:T(8,128)(2,1)S(1)} %collective-permute-done.2.refs_1_), custom_call_target="tpu_custom_call" | custom-call | flops 1000000 | bytes 65536 | tf_op jit(solution)/shard_map/sum_y_second/over_y/pallas_call | solution.py:102
  8.2 0.0 copy-start.3
  8.2 0.0 copy-start.4
  8.2 1.7 %collective-permute-start.7 = (bf16[4,128,1024]{2,1,0:T(8,128)(2,1)}, bf16[4,128,1024]{2,1,0:T(8,128)(2,1)S(1)}, u32[]{:S(2)}, u32[]{:S(2)}) collective-permute-start(bf16[4,128,1024]{2,1,0:T(8,128)(2,1)} %over_y.1), channel_id=1, source_target_pairs={{0,16},{8,24},{16,0},{24,8},{32,48},{40,56},{48,32},{56,40},{64,80... | collective-permute-start | bytes 3145736 | tf_op jit(solution)/shard_map/sum_y_second/ppermute | solution.py:430
  10.0 0.0 collective-permute-done.refs_1_
  10.0 0.0 collective-permute-done.1.refs_2_
  10.0 3.9 %away_x.1 = (bf16[2,128,1024]{2,1,0:T(8,128)(2,1)}, bf16[2,128,1024]{2,1,0:T(8,128)(2,1)}, bf16[2,128,1024]{2,1,0:T(8,128)(2,1)}, bf16[4,128,1024]{2,1,0:T(8,128)(2,1)}) custom-call(s32[3]{0:T(128)S(1)} %pad_add_fusion.1.scal_ref, bf16[4,2,2,2,128,1024]{5,4,3,2,1,0:T(8,128)(2,1)} %bitcast.23, bf16[4,128,1024]{2,1,0:T(8,128)(2,1)S(1)} %collective-permute-done.refs_1_, ...), custom_call_target="tpu_custom_call" | custom-call | flops 1000000 | bytes 65536 | tf_op jit(solution)/shard_map/sum_x_first/away_x/pallas_call | solution.py:102
  13.9 0.2 collective-permute-start.6
  14.1 1.5 %collective-permute-start.3 = (bf16[2,128,1024]{2,1,0:T(8,128)(2,1)}, bf16[2,128,1024]{2,1,0:T(8,128)(2,1)}, u32[]{:S(2)}, u32[]{:S(2)}) collective-permute-start(bf16[2,128,1024]{2,1,0:T(8,128)(2,1)} %get-tuple-element.54), channel_id=1, source_target_pairs={{0,32},{8,40},{16,48},{24,56},{32,64},{40,72},{48,80},{56,88},{64,... | collective-permute-start | bytes 1572872 | tf_op jit(solution)/shard_map/sum_x_first/ppermute | solution.py:430
  15.6 1.7 %collective-permute-start.4 = (bf16[2,128,1024]{2,1,0:T(8,128)(2,1)}, bf16[2,128,1024]{2,1,0:T(8,128)(2,1)}, u32[]{:S(2)}, u32[]{:S(2)}) collective-permute-start(bf16[2,128,1024]{2,1,0:T(8,128)(2,1)} %get-tuple-element.55), channel_id=1, source_target_pairs={{0,96},{8,104},{16,112},{24,120},{32,0},{40,8},{48,16},{56,24},{64... | collective-permute-start | bytes 1572872 | tf_op jit(solution)/shard_map/sum_x_first/ppermute | solution.py:430
  17.3 1.8 %collective-permute-start.5 = (bf16[2,128,1024]{2,1,0:T(8,128)(2,1)}, bf16[2,128,1024]{2,1,0:T(8,128)(2,1)}, u32[]{:S(2)}, u32[]{:S(2)}) collective-permute-start(bf16[2,128,1024]{2,1,0:T(8,128)(2,1)} %get-tuple-element.56), channel_id=1, source_target_pairs={{0,64},{8,72},{16,80},{24,88},{32,96},{40,104},{48,112},{56,120},{... | collective-permute-start | bytes 1572872 | tf_op jit(solution)/shard_map/sum_x_first/ppermute | solution.py:430
  19.1 0.0 copy-done.3
  19.2 0.7 fusion
  20.4 0.0 copy-done.4
  20.5 0.6 fusion.1
  21.1 0.7 stack.79
  21.8 0.7 stack.77
  22.5 0.0 copy-start
  22.5 3.4 %copy-done = bf16[1024,4096]{1,0:T(8,128)(2,1)S(1)} copy-done((bf16[1024,4096]{1,0:T(8,128)(2,1)S(1)}, bf16[1024,4096]{1,0:T(8,128)(2,1)}, u32[]{:S(2)}) %copy-start) | copy-done | bytes 8388632
  25.9 1.2 %copy-done.2 = bf16[512,1024]{1,0:T(8,128)(2,1)S(1)} copy-done((bf16[512,1024]{1,0:T(8,128)(2,1)S(1)}, bf16[512,1024]{1,0:T(8,128)(2,1)}, u32[]{:S(2)}) %copy-start.2) | copy-done | bytes 1048600
  27.1 7.3 %cand_project.1 = (bf16[512,1024]{1,0:T(8,128)(2,1)S(1)}, bf16[512,1024]{1,0:T(8,128)(2,1)S(1)}, bf16[512,1024]{1,0:T(8,128)(2,1)S(1)}, bf16[512,512]{1,0:T(8,128)(2,1)S(1)}, f32[512,1024]{1,0:T(8,128)S(1)}) custom-call(s32[1,512]{1,0:T(1,128)S(1)} %bitcast.19, bf16[512,1024]{1,0:T(8,128)(2,1)S(1)} %copy-done.2, bf16[1024,4096]{1,0:T(8,128)(2,1)S(1)} %copy-done), custom_call_target="tpu_custom_call" | custom-call | flops 1000000 | bytes 65536 | tf_op jit(solution)/shard_map/cand_project/pallas_call | solution.py:202
  34.4 0.0 collective-permute-done.7.refs_2_.refs_7_
  34.4 0.0 collective-permute-done.6.refs_1_.refs_6_
  34.4 2.1 %join_y.1 = (bf16[128,1024]{1,0:T(8,128)(2,1)S(1)}, bf16[128,1024]{1,0:T(8,128)(2,1)S(1)}, bf16[128,1024]{1,0:T(8,128)(2,1)S(1)}) custom-call(s32[3]{0:T(128)S(1)} %pad_add_fusion.1.scal_ref, bf16[4,2,2,2,128,1024]{5,4,3,2,1,0:T(8,128)(2,1)} %bitcast.24, bf16[4,128,1024]{2,1,0:T(8,128)(2,1)} %collective-permute-done.6.refs_1_.refs_6_, ...), custom_call_target="tpu_custom_call" | custom-call | flops 1000000 | bytes 65536 | tf_op jit(solution)/shard_map/sum_y_second/join_y/pallas_call | solution.py:102
  36.5 1.2 %collective-permute-start.9 = (bf16[128,1024]{1,0:T(8,128)(2,1)S(1)}, bf16[128,1024]{1,0:T(8,128)(2,1)S(1)}, u32[]{:S(2)}, u32[]{:S(2)}) collective-permute-start(bf16[128,1024]{1,0:T(8,128)(2,1)S(1)} %get-tuple-element.60), channel_id=1, source_target_pairs={{0,32},{8,40},{16,48},{24,56},{32,64},{40,72},{48,80},{56,88},{64,... | collective-permute-start | bytes 786440 | tf_op jit(solution)/shard_map/sum_y_second/ppermute | solution.py:430
  37.8 2.1 %collective-permute-start.10 = (bf16[128,1024]{1,0:T(8,128)(2,1)S(1)}, bf16[128,1024]{1,0:T(8,128)(2,1)S(1)}, u32[]{:S(2)}, u32[]{:S(2)}) collective-permute-start(bf16[128,1024]{1,0:T(8,128)(2,1)S(1)} %get-tuple-element.61), channel_id=1, source_target_pairs={{0,96},{8,104},{16,112},{24,120},{32,0},{40,8},{48,16},{56,24},{64... | collective-permute-start | bytes 786440 | tf_op jit(solution)/shard_map/sum_y_second/ppermute | solution.py:430
  39.8 0.0 collective-permute-done.3.refs_3_
  39.8 1.5 %collective-permute-start.11 = (bf16[128,1024]{1,0:T(8,128)(2,1)S(1)}, bf16[128,1024]{1,0:T(8,128)(2,1)S(1)}, u32[]{:S(2)}, u32[]{:S(2)}) collective-permute-start(bf16[128,1024]{1,0:T(8,128)(2,1)S(1)} %get-tuple-element.62), channel_id=1, source_target_pairs={{0,64},{8,72},{16,80},{24,88},{32,96},{40,104},{48,112},{56,120},{... | collective-permute-start | bytes 786440 | tf_op jit(solution)/shard_map/sum_y_second/ppermute | solution.py:430
  41.3 0.0 collective-permute-done.4.refs_4_
  41.3 1.3 %collective-permute-done.5.refs_5_ = bf16[2,128,1024]{2,1,0:T(8,128)(2,1)} collective-permute-done((bf16[2,128,1024]{2,1,0:T(8,128)(2,1)}, bf16[2,128,1024]{2,1,0:T(8,128)(2,1)}, u32[]{:S(2)}, u32[]{:S(2)}) %collective-permute-start.5) | collective-permute-done | bytes 524320 | tf_op jit(solution)/shard_map/sum_x_first/ppermute | solution.py:430
  42.6 2.4 %join_x.1 = (f32[128,1024]{1,0:T(8,128)S(1)}, bf16[128,1024]{1,0:T(8,128)(2,1)S(1)}, f32[128,1024]{1,0:T(8,128)S(1)}) custom-call(s32[3]{0:T(128)S(1)} %pad_add_fusion.1.scal_ref, bf16[4,2,2,2,128,1024]{5,4,3,2,1,0:T(8,128)(2,1)} %bitcast.25, bf16[4,128,1024]{2,1,0:T(8,128)(2,1)S(1)} %collective-permute-done.refs_1_, ...), custom_call_target="tpu_custom_call" | custom-call | flops 1000000 | bytes 65536 | tf_op jit(solution)/shard_map/sum_x_first/join_x/pallas_call | solution.py:102
  45.0 0.5 collective-permute-start.8
  45.5 2.6 %collective-permute-done.9.refs_1_ = bf16[128,1024]{1,0:T(8,128)(2,1)S(1)} collective-permute-done((bf16[128,1024]{1,0:T(8,128)(2,1)S(1)}, bf16[128,1024]{1,0:T(8,128)(2,1)S(1)}, u32[]{:S(2)}, u32[]{:S(2)}) %collective-permute-start.9) | collective-permute-done | bytes 262176 | tf_op jit(solution)/shard_map/sum_y_second/ppermute | solution.py:430
  48.1 0.0 collective-permute-done.10.refs_2_
  48.1 5.0 %collective-permute-done.11.refs_3_ = bf16[128,1024]{1,0:T(8,128)(2,1)S(1)} collective-permute-done((bf16[128,1024]{1,0:T(8,128)(2,1)S(1)}, bf16[128,1024]{1,0:T(8,128)(2,1)S(1)}, u32[]{:S(2)}, u32[]{:S(2)}) %collective-permute-start.11) | collective-permute-done | bytes 262176 | tf_op jit(solution)/shard_map/sum_y_second/ppermute | solution.py:430
  53.1 1.0 norm_sum.1.refs_2_
  54.1 0.0 collective-permute-done.8.refs_1_
  54.1 0.9 norm_both.1.refs_0_.refs_8_
  55.0 3.0 %collective-permute-start.14 = (bf16[2,128,1024]{2,1,0:T(8,128)(2,1)S(1)}, bf16[2,128,1024]{2,1,0:T(8,128)(2,1)S(1)}, u32[]{:S(2)}, u32[]{:S(2)}) collective-permute-start(bf16[2,128,1024]{2,1,0:T(8,128)(2,1)S(1)} %norm_both.1.refs_0_.refs_8_), channel_id=1, source_target_pairs={{0,1},{1,0},{2,3},{3,2},{4,5},{5,4},{6,7},{7,6},{8,9},{9,8},{10,11... | collective-permute-start | bytes 1572872 | tf_op jit(solution)/shard_map/gather/ppermute | solution.py:434
  58.0 4.0 %collective-permute-start.13 = (bf16[2,128,1024]{2,1,0:T(8,128)(2,1)S(1)}, bf16[2,128,1024]{2,1,0:T(8,128)(2,1)S(1)}, u32[]{:S(2)}, u32[]{:S(2)}) collective-permute-start(bf16[2,128,1024]{2,1,0:T(8,128)(2,1)S(1)} %norm_both.1.refs_0_.refs_8_), channel_id=1, source_target_pairs={{0,6},{1,7},{2,0},{3,1},{4,2},{5,3},{6,4},{7,5},{8,14},{9,15},{10,... | collective-permute-start | bytes 1572872 | tf_op jit(solution)/shard_map/gather/ppermute | solution.py:434
  62.0 0.0 collective-permute-start.12
  62.0 0.0 slice-done.1
  62.1 4.4 %own_keys.1 = (f32[512,1024]{1,0:T(8,128)S(1)}, f32[256,1024]{1,0:T(8,128)S(1)}, bf16[256,1024]{1,0:T(8,128)(2,1)S(1)}, bf16[256,1024]{1,0:T(8,128)(2,1)S(1)}) custom-call(s32[2,12]{1,0:T(2,128)S(1)} %pad_add_fusion.scal_ref, bf16[2,128,1024]{2,1,0:T(8,128)(2,1)S(1)} %norm_both.1.refs_0_.refs_8_, ...), custom_call_target="tpu_custom_call", output_to_operand_aliasing={{0}: (4, {})} | custom-call | flops 1000000 | bytes 65536 | tf_op jit(solution)/shard_map/own_keys/pallas_call | solution.py:202
  66.4 3.5 %collective-permute-done.14.refs_2_ = bf16[2,128,1024]{2,1,0:T(8,128)(2,1)S(1)} collective-permute-done((bf16[2,128,1024]{2,1,0:T(8,128)(2,1)S(1)}, bf16[2,128,1024]{2,1,0:T(8,128)(2,1)S(1)}, u32[]{:S(2)}, u32[]{:S(2)}) %collective-permute-start.14) | collective-permute-done | bytes 524320 | tf_op jit(solution)/shard_map/gather/ppermute | solution.py:434
  70.0 4.0 %collective-permute-start.17 = (bf16[2,128,1024]{2,1,0:T(8,128)(2,1)S(1)}, bf16[2,128,1024]{2,1,0:T(8,128)(2,1)S(1)}, u32[]{:S(2)}, u32[]{:S(2)}) collective-permute-start(bf16[2,128,1024]{2,1,0:T(8,128)(2,1)S(1)} %collective-permute-done.14.refs_2_), channel_id=1, source_target_pairs={{0,6},{1,7},{2,0},{3,1},{4,2},{5,3},{6,4},{7,5},{8,14},{9,15},{10,... | collective-permute-start | bytes 1572872 | tf_op jit(solution)/shard_map/gather/ppermute | solution.py:434
  74.0 0.0 collective-permute-start.16
  74.0 0.0 collective-permute-done.13.refs_1_
  74.0 2.0 %collective-permute-done.12.refs_0_ = bf16[2,128,1024]{2,1,0:T(8,128)(2,1)S(1)} collective-permute-done((bf16[2,128,1024]{2,1,0:T(8,128)(2,1)S(1)}, bf16[2,128,1024]{2,1,0:T(8,128)(2,1)S(1)}, u32[]{:S(2)}, u32[]{:S(2)}) %collective-permute-start.12) | collective-permute-done | bytes 524320 | tf_op jit(solution)/shard_map/gather/ppermute | solution.py:434
  76.1 0.0 collective-permute-start.15
  76.1 7.8 %own_sides.1 = (f32[512,1024]{1,0:T(8,128)S(1)}, f32[256,1024]{1,0:T(8,128)S(1)}) custom-call(s32[2,12]{1,0:T(2,128)S(1)} %pad_add_fusion.scal_ref, bf16[2,128,1024]{2,1,0:T(8,128)(2,1)S(1)} %collective-permute-done.12.refs_0_, bf16[2,128,1024]{2,1,0:T(8,128)(2,1)S(1)} %collective-permute-done.13.refs_1_, ...), custom_call_target="tpu_custom_call", output_to_operand_aliasing={{0}: (6, {}), {1}: (8, {})} | custom-call | flops 1000000 | bytes 65536 | tf_op jit(solution)/shard_map/own_sides/pallas_call | solution.py:202
  83.9 0.1 collective-permute-done.17.refs_1_
  84.0 6.1 %collective-permute-done.16.refs_0_ = bf16[2,128,1024]{2,1,0:T(8,128)(2,1)S(1)} collective-permute-done((bf16[2,128,1024]{2,1,0:T(8,128)(2,1)S(1)}, bf16[2,128,1024]{2,1,0:T(8,128)(2,1)S(1)}, u32[]{:S(2)}, u32[]{:S(2)}) %collective-permute-start.16) | collective-permute-done | bytes 524320 | tf_op jit(solution)/shard_map/gather/ppermute | solution.py:434
  90.1 0.0 collective-permute-start.18
  90.1 5.1 %near_sides.1 = (f32[512,1024]{1,0:T(8,128)S(1)}, f32[256,1024]{1,0:T(8,128)S(1)}) custom-call(s32[2,12]{1,0:T(2,128)S(1)} %pad_add_fusion.scal_ref, bf16[2,128,1024]{2,1,0:T(8,128)(2,1)S(1)} %collective-permute-done.16.refs_0_, bf16[2,128,1024]{2,1,0:T(8,128)(2,1)S(1)} %collective-permute-done.17.refs_1_, ...), custom_call_target="tpu_custom_call", output_to_operand_aliasing={{0}: (5, {}), {1}: (7, {})} | custom-call | flops 1000000 | bytes 65536 | tf_op jit(solution)/shard_map/near_sides/pallas_call | solution.py:202
  95.2 3.5 %collective-permute-done.15.refs_0_ = bf16[2,128,1024]{2,1,0:T(8,128)(2,1)S(1)} collective-permute-done((bf16[2,128,1024]{2,1,0:T(8,128)(2,1)S(1)}, bf16[2,128,1024]{2,1,0:T(8,128)(2,1)S(1)}, u32[]{:S(2)}, u32[]{:S(2)}) %collective-permute-start.15) | collective-permute-done | bytes 524320 | tf_op jit(solution)/shard_map/gather/ppermute | solution.py:434
  98.6 0.6 collective-permute-done.18.refs_1_
  99.3 8.9 %far_finish.1 = (bf16[2,128,1024]{2,1,0:T(8,128)(2,1)}, bf16[512,1024]{1,0:T(8,128)(2,1)}) custom-call(s32[2,12]{1,0:T(2,128)S(1)} %pad_add_fusion.scal_ref, bf16[2,128,1024]{2,1,0:T(8,128)(2,1)S(1)} %collective-permute-done.15.refs_0_, bf16[2,128,1024]{2,1,0:T(8,128)(2,1)S(1)} %collective-permute-done.18.refs_1_, bf16[1024,4096]{1,0:T(8,128)(2,1)S(1)} %bitcast.18, ...), custom_call_target="tpu_custom_call" | custom-call | flops 1000000 | bytes 65536 | tf_op jit(solution)/shard_map/far_finish/pallas_call | solution.py:202
  (8 shorter events, 0.0 us)
Async XLA Ops:
  2.5 2.9 %collective-permute-start.2 = (bf16[4,128,1024]{2,1,0:T(8,128)(2,1)S(1)}, bf16[4,128,1024]{2,1,0:T(8,128)(2,1)S(1)}, u32[]{:S(2)}, u32[]{:S(2)}) collective-permute-start(bf16[4,128,1024]{2,1,0:T(8,128)(2,1)S(1)} %pack.1), channel_id=1, source_target_pairs={{0,8},{8,0},{16,24},{24,16},{32,40},{40,32},{48,56},{56,48},{64,72... | collective-permute-start | bytes 3145736 | tf_op jit(solution)/shard_map/sum_core/ppermute | solution.py:430
  4.7 5.3 %collective-permute-start = (bf16[4,128,1024]{2,1,0:T(8,128)(2,1)S(1)}, bf16[4,128,1024]{2,1,0:T(8,128)(2,1)S(1)}, u32[]{:S(2)}, u32[]{:S(2)}) collective-permute-start(bf16[4,128,1024]{2,1,0:T(8,128)(2,1)S(1)} %get-tuple-element.47), channel_id=1, source_target_pairs={{0,8},{8,0},{16,24},{24,16},{32,40},{40,32},{48,56},{56,48},{64,72... | collective-permute-start | bytes 3145736 | tf_op jit(solution)/shard_map/sum_core/ppermute | solution.py:430
  5.3 4.7 %collective-permute-start.1 = (bf16[4,128,1024]{2,1,0:T(8,128)(2,1)S(1)}, bf16[4,128,1024]{2,1,0:T(8,128)(2,1)S(1)}, u32[]{:S(2)}, u32[]{:S(2)}) collective-permute-start(bf16[4,128,1024]{2,1,0:T(8,128)(2,1)S(1)} %get-tuple-element.48), channel_id=1, source_target_pairs={{0,8},{8,0},{16,24},{24,16},{32,40},{40,32},{48,56},{56,48},{64,72... | collective-permute-start | bytes 3145736 | tf_op jit(solution)/shard_map/sum_core/ppermute | solution.py:430
  8.2 10.9 %copy-start.3 = (s32[512]{0:T(512)S(1)}, s32[512]{0:T(512)}, u32[]{:S(2)}) copy-start(s32[512]{0:T(512)} %param.9) | copy-start | bytes 6148
  8.2 12.2 %copy-start.4 = (s32[2]{0:T(128)S(1)}, s32[2]{0:T(128)}, u32[]{:S(2)}) copy-start(s32[2]{0:T(128)} %param.8) | copy-start | bytes 28
  8.2 26.2 %collective-permute-start.7 = (bf16[4,128,1024]{2,1,0:T(8,128)(2,1)}, bf16[4,128,1024]{2,1,0:T(8,128)(2,1)S(1)}, u32[]{:S(2)}, u32[]{:S(2)}) collective-permute-start(bf16[4,128,1024]{2,1,0:T(8,128)(2,1)} %over_y.1), channel_id=1, source_target_pairs={{0,16},{8,24},{16,0},{24,8},{32,48},{40,56},{48,32},{56,40},{64,80... | collective-permute-start | bytes 3145736 | tf_op jit(solution)/shard_map/sum_y_second/ppermute | solution.py:430
  13.9 20.5 %collective-permute-start.6 = (bf16[4,128,1024]{2,1,0:T(8,128)(2,1)}, bf16[4,128,1024]{2,1,0:T(8,128)(2,1)}, u32[]{:S(2)}, u32[]{:S(2)}) collective-permute-start(bf16[4,128,1024]{2,1,0:T(8,128)(2,1)} %get-tuple-element.52), channel_id=1, source_target_pairs={{0,8},{8,0},{16,24},{24,16},{32,40},{40,32},{48,56},{56,48},{64,72... | collective-permute-start | bytes 3145736 | tf_op jit(solution)/shard_map/sum_core/ppermute | solution.py:430
  14.1 25.7 %collective-permute-start.3 = (bf16[2,128,1024]{2,1,0:T(8,128)(2,1)}, bf16[2,128,1024]{2,1,0:T(8,128)(2,1)}, u32[]{:S(2)}, u32[]{:S(2)}) collective-permute-start(bf16[2,128,1024]{2,1,0:T(8,128)(2,1)} %get-tuple-element.54), channel_id=1, source_target_pairs={{0,32},{8,40},{16,48},{24,56},{32,64},{40,72},{48,80},{56,88},{64,... | collective-permute-start | bytes 1572872 | tf_op jit(solution)/shard_map/sum_x_first/ppermute | solution.py:430
  15.6 25.7 %collective-permute-start.4 = (bf16[2,128,1024]{2,1,0:T(8,128)(2,1)}, bf16[2,128,1024]{2,1,0:T(8,128)(2,1)}, u32[]{:S(2)}, u32[]{:S(2)}) collective-permute-start(bf16[2,128,1024]{2,1,0:T(8,128)(2,1)} %get-tuple-element.55), channel_id=1, source_target_pairs={{0,96},{8,104},{16,112},{24,120},{32,0},{40,8},{48,16},{56,24},{64... | collective-permute-start | bytes 1572872 | tf_op jit(solution)/shard_map/sum_x_first/ppermute | solution.py:430
  17.3 25.3 %collective-permute-start.5 = (bf16[2,128,1024]{2,1,0:T(8,128)(2,1)}, bf16[2,128,1024]{2,1,0:T(8,128)(2,1)}, u32[]{:S(2)}, u32[]{:S(2)}) collective-permute-start(bf16[2,128,1024]{2,1,0:T(8,128)(2,1)} %get-tuple-element.56), channel_id=1, source_target_pairs={{0,64},{8,72},{16,80},{24,88},{32,96},{40,104},{48,112},{56,120},{... | collective-permute-start | bytes 1572872 | tf_op jit(solution)/shard_map/sum_x_first/ppermute | solution.py:430
  22.5 3.4 %copy-start = (bf16[1024,4096]{1,0:T(8,128)(2,1)S(1)}, bf16[1024,4096]{1,0:T(8,128)(2,1)}, u32[]{:S(2)}) copy-start(bf16[1024,4096]{1,0:T(8,128)(2,1)} %refs_2_.3) | copy-start | bytes 25165828
  25.9 1.2 %copy-start.2 = (bf16[512,1024]{1,0:T(8,128)(2,1)S(1)}, bf16[512,1024]{1,0:T(8,128)(2,1)}, u32[]{:S(2)}) copy-start(bf16[512,1024]{1,0:T(8,128)(2,1)} %feats_ref.1) | copy-start | bytes 3145732
  36.5 11.6 %collective-permute-start.9 = (bf16[128,1024]{1,0:T(8,128)(2,1)S(1)}, bf16[128,1024]{1,0:T(8,128)(2,1)S(1)}, u32[]{:S(2)}, u32[]{:S(2)}) collective-permute-start(bf16[128,1024]{1,0:T(8,128)(2,1)S(1)} %get-tuple-element.60), channel_id=1, source_target_pairs={{0,32},{8,40},{16,48},{24,56},{32,64},{40,72},{48,80},{56,88},{64,... | collective-permute-start | bytes 786440 | tf_op jit(solution)/shard_map/sum_y_second/ppermute | solution.py:430
  37.8 10.4 %collective-permute-start.10 = (bf16[128,1024]{1,0:T(8,128)(2,1)S(1)}, bf16[128,1024]{1,0:T(8,128)(2,1)S(1)}, u32[]{:S(2)}, u32[]{:S(2)}) collective-permute-start(bf16[128,1024]{1,0:T(8,128)(2,1)S(1)} %get-tuple-element.61), channel_id=1, source_target_pairs={{0,96},{8,104},{16,112},{24,120},{32,0},{40,8},{48,16},{56,24},{64... | collective-permute-start | bytes 786440 | tf_op jit(solution)/shard_map/sum_y_second/ppermute | solution.py:430
  39.8 22.2 %slice-start = ((s8[8388608]{0:T(1024)(128)(4,1)}), s8[4194304]{0:T(1024)(128)(4,1)S(1)}, s32[]{:S(2)}) async-start(s8[8388608]{0:T(1024)(128)(4,1)} %bitcast.17), calls=%async_computation | async-start | bytes 8388608
  39.8 22.2 %slice-start.1 = ((s8[8388608]{0:T(1024)(128)(4,1)}), s8[4194304]{0:T(1024)(128)(4,1)S(1)}, s32[]{:S(2)}) async-start(s8[8388608]{0:T(1024)(128)(4,1)} %bitcast.17), calls=%async_computation.1 | async-start | bytes 8388608
  39.8 13.3 %collective-permute-start.11 = (bf16[128,1024]{1,0:T(8,128)(2,1)S(1)}, bf16[128,1024]{1,0:T(8,128)(2,1)S(1)}, u32[]{:S(2)}, u32[]{:S(2)}) collective-permute-start(bf16[128,1024]{1,0:T(8,128)(2,1)S(1)} %get-tuple-element.62), channel_id=1, source_target_pairs={{0,64},{8,72},{16,80},{24,88},{32,96},{40,104},{48,112},{56,120},{... | collective-permute-start | bytes 786440 | tf_op jit(solution)/shard_map/sum_y_second/ppermute | solution.py:430
  45.0 9.1 %collective-permute-start.8 = (bf16[128,1024]{1,0:T(8,128)(2,1)S(1)}, bf16[128,1024]{1,0:T(8,128)(2,1)S(1)}, u32[]{:S(2)}, u32[]{:S(2)}) collective-permute-start(bf16[128,1024]{1,0:T(8,128)(2,1)S(1)} %get-tuple-element.67), channel_id=1, source_target_pairs={{0,16},{8,24},{16,0},{24,8},{32,48},{40,56},{48,32},{56,40},{64,80... | collective-permute-start | bytes 786440 | tf_op jit(solution)/shard_map/sum_x_first/ppermute | solution.py:430
  55.0 15.0 %collective-permute-start.14 = (bf16[2,128,1024]{2,1,0:T(8,128)(2,1)S(1)}, bf16[2,128,1024]{2,1,0:T(8,128)(2,1)S(1)}, u32[]{:S(2)}, u32[]{:S(2)}) collective-permute-start(bf16[2,128,1024]{2,1,0:T(8,128)(2,1)S(1)} %norm_both.1.refs_0_.refs_8_), channel_id=1, source_target_pairs={{0,1},{1,0},{2,3},{3,2},{4,5},{5,4},{6,7},{7,6},{8,9},{9,8},{10,11... | collective-permute-start | bytes 1572872 | tf_op jit(solution)/shard_map/gather/ppermute | solution.py:434
  58.0 16.0 %collective-permute-start.13 = (bf16[2,128,1024]{2,1,0:T(8,128)(2,1)S(1)}, bf16[2,128,1024]{2,1,0:T(8,128)(2,1)S(1)}, u32[]{:S(2)}, u32[]{:S(2)}) collective-permute-start(bf16[2,128,1024]{2,1,0:T(8,128)(2,1)S(1)} %norm_both.1.refs_0_.refs_8_), channel_id=1, source_target_pairs={{0,6},{1,7},{2,0},{3,1},{4,2},{5,3},{6,4},{7,5},{8,14},{9,15},{10,... | collective-permute-start | bytes 1572872 | tf_op jit(solution)/shard_map/gather/ppermute | solution.py:434
  62.0 14.0 %collective-permute-start.12 = (bf16[2,128,1024]{2,1,0:T(8,128)(2,1)S(1)}, bf16[2,128,1024]{2,1,0:T(8,128)(2,1)S(1)}, u32[]{:S(2)}, u32[]{:S(2)}) collective-permute-start(bf16[2,128,1024]{2,1,0:T(8,128)(2,1)S(1)} %norm_both.1.refs_0_.refs_8_), channel_id=1, source_target_pairs={{0,2},{1,3},{2,4},{3,5},{4,6},{5,7},{6,0},{7,1},{8,10},{9,11},{10,... | collective-permute-start | bytes 1572872 | tf_op jit(solution)/shard_map/gather/ppermute | solution.py:434
  70.0 14.0 %collective-permute-start.17 = (bf16[2,128,1024]{2,1,0:T(8,128)(2,1)S(1)}, bf16[2,128,1024]{2,1,0:T(8,128)(2,1)S(1)}, u32[]{:S(2)}, u32[]{:S(2)}) collective-permute-start(bf16[2,128,1024]{2,1,0:T(8,128)(2,1)S(1)} %collective-permute-done.14.refs_2_), channel_id=1, source_target_pairs={{0,6},{1,7},{2,0},{3,1},{4,2},{5,3},{6,4},{7,5},{8,14},{9,15},{10,... | collective-permute-start | bytes 1572872 | tf_op jit(solution)/shard_map/gather/ppermute | solution.py:434
  74.0 16.1 %collective-permute-start.16 = (bf16[2,128,1024]{2,1,0:T(8,128)(2,1)S(1)}, bf16[2,128,1024]{2,1,0:T(8,128)(2,1)S(1)}, u32[]{:S(2)}, u32[]{:S(2)}) collective-permute-start(bf16[2,128,1024]{2,1,0:T(8,128)(2,1)S(1)} %collective-permute-done.14.refs_2_), channel_id=1, source_target_pairs={{0,2},{1,3},{2,4},{3,5},{4,6},{5,7},{6,0},{7,1},{8,10},{9,11},{10,... | collective-permute-start | bytes 1572872 | tf_op jit(solution)/shard_map/gather/ppermute | solution.py:434
  76.1 22.6 %collective-permute-start.15 = (bf16[2,128,1024]{2,1,0:T(8,128)(2,1)S(1)}, bf16[2,128,1024]{2,1,0:T(8,128)(2,1)S(1)}, u32[]{:S(2)}, u32[]{:S(2)}) collective-permute-start(bf16[2,128,1024]{2,1,0:T(8,128)(2,1)S(1)} %collective-permute-done.12.refs_0_), channel_id=1, source_target_pairs={{0,2},{1,3},{2,4},{3,5},{4,6},{5,7},{6,0},{7,1},{8,10},{9,11},{10,... | collective-permute-start | bytes 1572872 | tf_op jit(solution)/shard_map/gather/ppermute | solution.py:434
  90.1 9.2 %collective-permute-start.18 = (bf16[2,128,1024]{2,1,0:T(8,128)(2,1)S(1)}, bf16[2,128,1024]{2,1,0:T(8,128)(2,1)S(1)}, u32[]{:S(2)}, u32[]{:S(2)}) collective-permute-start(bf16[2,128,1024]{2,1,0:T(8,128)(2,1)S(1)} %collective-permute-done.17.refs_1_), channel_id=1, source_target_pairs={{0,6},{1,7},{2,0},{3,1},{4,2},{5,3},{6,4},{7,5},{8,14},{9,15},{10,... | collective-permute-start | bytes 1572872 | tf_op jit(solution)/shard_map/gather/ppermute | solution.py:434
  90.1 9.2 %copy-start.1 = (bf16[1024,1024]{1,0:T(8,128)(2,1)S(1)}, bf16[1024,1024]{1,0:T(8,128)(2,1)}, u32[]{:S(2)}) copy-start(bf16[1024,1024]{1,0:T(8,128)(2,1)} %refs_12_.1) | copy-start | bytes 6291460

commit v3 on v2

--- a/solution.py
+++ b/solution.py
@@ -60,9 +60,9 @@
     return pl.CostEstimate(flops=10**6, bytes_accessed=1 << 16, transcendentals=0)
 
 
-def block_sums(name, scal, arrays, shapes, sums):
-    added = [part for _, _, parts, _ in sums if len(parts) > 1 for part in parts]
-    n_loads = sum(len(parts) for _, _, parts, _ in sums)
+def block_sums(name, scal, arrays, shapes, sums, held_in=()):
+    added = [p for _, _, parts, _ in sums if len(parts) > 1 for p in parts if p[0] not in held_in]
+    n_loads = sum(p[0] not in held_in for _, _, parts, _ in sums for p in parts)
 
     def body(scal_ref, *refs):
         ins, refs = refs[: len(arrays)], refs[len(arrays) :]
@@ -76,6 +76,9 @@
             for at, index in parts:
                 from_ = index(scal_ref)
                 src = ins[at].at[from_] if from_ else ins[at]
+                if at in held_in:
+                    held.append(src)
+                    continue
                 to = bufs.pop(0) if len(parts) > 1 else dst
                 copies.append(pltpu.make_async_copy(src, to, in_sems.at[count]))
                 copies[-1].start()
@@ -85,6 +88,8 @@
         for dst, copies, held, norm in work:
             for copy in copies:
                 copy.wait()
+            if len(held) == 1 and not copies:
+                dst[...] = held[0][...]
             if len(held) > 1:
                 step = SLOTS if norm else SLOTS // 2
 
@@ -102,11 +107,14 @@
     return pl.pallas_call(
         body,
         in_specs=[pl.BlockSpec(memory_space=pltpu.SMEM)]
-        + [hbm if a.ndim == 6 else anywhere for a in arrays],
+        + [
+            pl.BlockSpec(memory_space=pltpu.VMEM) if n in held_in else hbm if a.ndim == 6 else anywhere
+            for n, a in enumerate(arrays)
+        ],
         out_specs=[pl.BlockSpec(memory_space=pltpu.VMEM)] * len(shapes),
         out_shape=[jax.ShapeDtypeStruct(shape, dtype) for shape, dtype in shapes],
         scratch_shapes=[pltpu.VMEM((SLOTS, D), arrays[at].dtype) for at, _ in added]
-        + [pltpu.SemaphoreType.DMA((n_loads,))],
+        + [pltpu.SemaphoreType.DMA((max(n_loads, 1),))],
         compiler_params=pltpu.CompilerParams(vmem_limit_bytes=VMEM),
         cost_estimate=cost(),
         name=name,
@@ -132,7 +140,7 @@
         (0, (x,), [(0, lambda s, x=x: (x, 1 - s[1], s[2], 1)), (1, lambda s, x=x: (x,))], False)
         for x in range(NX)
     ]
-    return block_sums("over_y", place, [tables, got], [((NX, SLOTS, D), BF16)], sums)[0]
+    return block_sums("over_y", place, [tables, got], [((NX, SLOTS, D), BF16)], sums, (1,))[0]
 
 
 def away_x(place, tables, got):
@@ -148,7 +156,7 @@
     for n in range(NX):
         sums.append((3, (n,), [(0, lambda s, n=n: (n, s[1], 1 - s[2], 1))], False))
     shapes = [((2, SLOTS, D), BF16)] * 3 + [((NX, SLOTS, D), BF16)]
-    return block_sums("away_x", place, [tables] + list(got), shapes, sums)
+    return block_sums("away_x", place, [tables] + list(got), shapes, sums, (1, 2))
 
 
 def join_x(place, tables, got, arrived, got1, side1):
@@ -175,18 +183,20 @@
             (2, lambda s, at=at: (at(s),)),
         ]
         sums.append((n, (), parts, False))
-    return block_sums("join_y", place, [tables, got, arrived], [((SLOTS, D), BF16)] * 3, sums)
+    return block_sums("join_y", place, [tables, got, arrived], [((SLOTS, D), BF16)] * 3, sums, (2,))
 
 
 def norm_sum(place, arrays):
     parts = [(n, lambda s: ()) for n in range(len(arrays))]
-    return block_sums("norm_sum", place, arrays, [((SLOTS, D), BF16)], [(0, (), parts, True)])[0]
+    held_in = range(len(arrays))
+    return block_sums("norm_sum", place, arrays, [((SLOTS, D), BF16)], [(0, (), parts, True)], held_in)[0]
 
 
 def norm_both(place, first, second):
     parts = [(n, lambda s: ()) for n in range(len(first) + 1)]
     sums = [(0, (1,), parts[-1:], False), (0, (0,), parts[:-1], True)]
-    return block_sums("norm_both", place, list(first) + [second], [((2, SLOTS, D), BF16)], sums)[0]
+    arrays = list(first) + [second]
+    return block_sums("norm_both", place, arrays, [((2, SLOTS, D), BF16)], sums, range(len(arrays)))[0]
 
 
 def in_vmem(array):

time: 109 us -> 108 us (level)
  transfers between devices with their start and end apart: 19 -> 19, of which waited for: 9 -> 9; matrix products, arithmetic and copies ran while one was open for 2% -> 3% of each run, Pallas kernels for 36% -> 36%
where the time goes in v3:
time: 108 us
  Pallas kernels  49.9 us (46%)
  waiting for transfers between devices  24.7 us (23%)
  starting transfers between devices  24.3 us (22%)
  local copies, waits for them, and re-layouts  6.67 us (6%)
  between operations  1.65 us (2%)
    pallas_call x5, Pallas kernels, kernel_call(): pl.pallas_call(body, in_specs=in_specs, out_specs=[pl.BlockSpec(memory_sp...  33.4 us
    pallas_call x8, Pallas kernels, block_sums(): pl.pallas_call(body, in_specs=[pl.BlockSpec(memory_space=pltpu.SMEM)] + [...  16.5 us
    ppermute x7, waiting for transfers between devices, to_cand(): return lax.ppermute(array, 'cand', cand_perm(dz, dy))  15.9 us
    ppermute x12, starting transfers between devices, to_user(): return lax.ppermute(array, 'user', user_perm(dx, dy, dcore))  13.2 us
    ppermute x7, starting transfers between devices, to_cand(): return lax.ppermute(array, 'cand', cand_perm(dz, dy))  11.1 us
    ppermute x12, waiting for transfers between devices, to_user(): return lax.ppermute(array, 'user', user_perm(dx, dy, dcore))  8.84 us
    unnamed x14, local copies, waits for them, and re-layouts  4.62 us
  transfers between devices with their start and end apart: 19, of which 9 were waited for; matrix products, arithmetic and copies ran while one was open for 3% of the time, Pallas kernels for 36%

profile of v3, /device:TPU:0, one launch (start us, length us, event | category | flops | bytes accessed | tf_op | source)
XLA Modules:
  0.0 108.0 jit_solution(11998409114169152137)
XLA Ops:
  0.6 0.1 pad_add_fusion.1.scal_ref
  0.7 1.8 %pack.1 = bf16[4,128,1024]{2,1,0:T(8,128)(2,1)S(1)} custom-call(s32[3]{0:T(128)S(1)} %pad_add_fusion.1.scal_ref, bf16[4,2,2,2,128,1024]{5,4,3,2,1,0:T(8,128)(2,1)} %bitcast.20), custom_call_target="tpu_custom_call" | custom-call | flops 1000000 | bytes 65536 | tf_op jit(solution)/shard_map/sum_core/pack/pallas_call | solution.py:107
  2.5 0.1 collective-permute-start.2
  2.6 2.1 %pack_all.1 = (bf16[4,128,1024]{2,1,0:T(8,128)(2,1)S(1)}, bf16[4,128,1024]{2,1,0:T(8,128)(2,1)S(1)}) custom-call(s32[3]{0:T(128)S(1)} %pad_add_fusion.1.scal_ref, bf16[4,2,2,2,128,1024]{5,4,3,2,1,0:T(8,128)(2,1)} %bitcast.21), custom_call_target="tpu_custom_call" | custom-call | flops 1000000 | bytes 65536 | tf_op jit(solution)/shard_map/sum_core/pack_all/pallas_call | solution.py:107
  4.7 0.6 collective-permute-start
  5.3 0.1 collective-permute-start.1
  5.4 0.0 collective-permute-done.2.refs_1_
  5.4 2.8 %over_y.1 = bf16[4,128,1024]{2,1,0:T(8,128)(2,1)} custom-call(s32[3]{0:T(128)S(1)} %pad_add_fusion.1.scal_ref, bf16[4,2,2,2,128,1024]{5,4,3,2,1,0:T(8,128)(2,1)} %bitcast.22, bf16[4,128,1024]{2,1,0:T(8,128)(2,1)S(1)} %collective-permute-done.2.refs_1_), custom_call_target="tpu_custom_call" | custom-call | flops 1000000 | bytes 65536 | tf_op jit(solution)/shard_map/sum_y_second/over_y/pallas_call | solution.py:107
  8.2 0.0 copy-start.3
  8.2 0.0 copy-start.4
  8.2 1.7 %collective-permute-start.7 = (bf16[4,128,1024]{2,1,0:T(8,128)(2,1)}, bf16[4,128,1024]{2,1,0:T(8,128)(2,1)S(1)}, u32[]{:S(2)}, u32[]{:S(2)}) collective-permute-start(bf16[4,128,1024]{2,1,0:T(8,128)(2,1)} %over_y.1), channel_id=1, source_target_pairs={{0,16},{8,24},{16,0},{24,8},{32,48},{40,56},{48,32},{56,40},{64,80... | collective-permute-start | bytes 3145736 | tf_op jit(solution)/shard_map/sum_y_second/ppermute | solution.py:440
  9.9 0.0 collective-permute-done.refs_1_
  9.9 0.0 collective-permute-done.1.refs_2_
  9.9 3.8 %away_x.1 = (bf16[2,128,1024]{2,1,0:T(8,128)(2,1)}, bf16[2,128,1024]{2,1,0:T(8,128)(2,1)}, bf16[2,128,1024]{2,1,0:T(8,128)(2,1)}, bf16[4,128,1024]{2,1,0:T(8,128)(2,1)}) custom-call(s32[3]{0:T(128)S(1)} %pad_add_fusion.1.scal_ref, bf16[4,2,2,2,128,1024]{5,4,3,2,1,0:T(8,128)(2,1)} %bitcast.23, bf16[4,128,1024]{2,1,0:T(8,128)(2,1)S(1)} %collective-permute-done.refs_1_, ...), custom_call_target="tpu_custom_call" | custom-call | flops 1000000 | bytes 65536 | tf_op jit(solution)/shard_map/sum_x_first/away_x/pallas_call | solution.py:107
  13.7 0.2 collective-permute-start.6
  14.0 1.5 %collective-permute-start.3 = (bf16[2,128,1024]{2,1,0:T(8,128)(2,1)}, bf16[2,128,1024]{2,1,0:T(8,128)(2,1)}, u32[]{:S(2)}, u32[]{:S(2)}) collective-permute-start(bf16[2,128,1024]{2,1,0:T(8,128)(2,1)} %get-tuple-element.54), channel_id=1, source_target_pairs={{0,32},{8,40},{16,48},{24,56},{32,64},{40,72},{48,80},{56,88},{64,... | collective-permute-start | bytes 1572872 | tf_op jit(solution)/shard_map/sum_x_first/ppermute | solution.py:440
  15.5 1.7 %collective-permute-start.4 = (bf16[2,128,1024]{2,1,0:T(8,128)(2,1)}, bf16[2,128,1024]{2,1,0:T(8,128)(2,1)}, u32[]{:S(2)}, u32[]{:S(2)}) collective-permute-start(bf16[2,128,1024]{2,1,0:T(8,128)(2,1)} %get-tuple-element.55), channel_id=1, source_target_pairs={{0,96},{8,104},{16,112},{24,120},{32,0},{40,8},{48,16},{56,24},{64... | collective-permute-start | bytes 1572872 | tf_op jit(solution)/shard_map/sum_x_first/ppermute | solution.py:440
  17.2 1.8 %collective-permute-start.5 = (bf16[2,128,1024]{2,1,0:T(8,128)(2,1)}, bf16[2,128,1024]{2,1,0:T(8,128)(2,1)}, u32[]{:S(2)}, u32[]{:S(2)}) collective-permute-start(bf16[2,128,1024]{2,1,0:T(8,128)(2,1)} %get-tuple-element.56), channel_id=1, source_target_pairs={{0,64},{8,72},{16,80},{24,88},{32,96},{40,104},{48,112},{56,120},{... | collective-permute-start | bytes 1572872 | tf_op jit(solution)/shard_map/sum_x_first/ppermute | solution.py:440
  19.0 0.0 copy-done.3
  19.0 0.7 fusion
  20.3 0.0 copy-done.4
  20.3 0.6 fusion.1
  20.9 0.7 stack.79
  21.6 0.7 stack.77
  22.4 0.0 copy-start
  22.4 3.4 %copy-done = bf16[1024,4096]{1,0:T(8,128)(2,1)S(1)} copy-done((bf16[1024,4096]{1,0:T(8,128)(2,1)S(1)}, bf16[1024,4096]{1,0:T(8,128)(2,1)}, u32[]{:S(2)}) %copy-start) | copy-done | bytes 8388632
  25.8 1.2 %copy-done.2 = bf16[512,1024]{1,0:T(8,128)(2,1)S(1)} copy-done((bf16[512,1024]{1,0:T(8,128)(2,1)S(1)}, bf16[512,1024]{1,0:T(8,128)(2,1)}, u32[]{:S(2)}) %copy-start.2) | copy-done | bytes 1048600
  27.0 7.2 %cand_project.1 = (bf16[512,1024]{1,0:T(8,128)(2,1)S(1)}, bf16[512,1024]{1,0:T(8,128)(2,1)S(1)}, bf16[512,1024]{1,0:T(8,128)(2,1)S(1)}, bf16[512,512]{1,0:T(8,128)(2,1)S(1)}, f32[512,1024]{1,0:T(8,128)S(1)}) custom-call(s32[1,512]{1,0:T(1,128)S(1)} %bitcast.19, bf16[512,1024]{1,0:T(8,128)(2,1)S(1)} %copy-done.2, bf16[1024,4096]{1,0:T(8,128)(2,1)S(1)} %copy-done), custom_call_target="tpu_custom_call" | custom-call | flops 1000000 | bytes 65536 | tf_op jit(solution)/shard_map/cand_project/pallas_call | solution.py:212
  34.2 0.0 collective-permute-done.7.refs_2_.refs_7_
  34.3 0.0 collective-permute-done.6.refs_1_.refs_6_
  34.3 2.0 %join_y.1 = (bf16[128,1024]{1,0:T(8,128)(2,1)S(1)}, bf16[128,1024]{1,0:T(8,128)(2,1)S(1)}, bf16[128,1024]{1,0:T(8,128)(2,1)S(1)}) custom-call(s32[3]{0:T(128)S(1)} %pad_add_fusion.1.scal_ref, bf16[4,2,2,2,128,1024]{5,4,3,2,1,0:T(8,128)(2,1)} %bitcast.24, bf16[4,128,1024]{2,1,0:T(8,128)(2,1)} %collective-permute-done.6.refs_1_.refs_6_, ...), custom_call_target="tpu_custom_call" | custom-call | flops 1000000 | bytes 65536 | tf_op jit(solution)/shard_map/sum_y_second/join_y/pallas_call | solution.py:107
  36.3 1.3 %collective-permute-start.9 = (bf16[128,1024]{1,0:T(8,128)(2,1)S(1)}, bf16[128,1024]{1,0:T(8,128)(2,1)S(1)}, u32[]{:S(2)}, u32[]{:S(2)}) collective-permute-start(bf16[128,1024]{1,0:T(8,128)(2,1)S(1)} %get-tuple-element.60), channel_id=1, source_target_pairs={{0,32},{8,40},{16,48},{24,56},{32,64},{40,72},{48,80},{56,88},{64,... | collective-permute-start | bytes 786440 | tf_op jit(solution)/shard_map/sum_y_second/ppermute | solution.py:440
  37.7 2.0 %collective-permute-start.10 = (bf16[128,1024]{1,0:T(8,128)(2,1)S(1)}, bf16[128,1024]{1,0:T(8,128)(2,1)S(1)}, u32[]{:S(2)}, u32[]{:S(2)}) collective-permute-start(bf16[128,1024]{1,0:T(8,128)(2,1)S(1)} %get-tuple-element.61), channel_id=1, source_target_pairs={{0,96},{8,104},{16,112},{24,120},{32,0},{40,8},{48,16},{56,24},{64... | collective-permute-start | bytes 786440 | tf_op jit(solution)/shard_map/sum_y_second/ppermute | solution.py:440
  39.6 0.0 collective-permute-done.3.refs_3_
  39.6 1.6 %collective-permute-start.11 = (bf16[128,1024]{1,0:T(8,128)(2,1)S(1)}, bf16[128,1024]{1,0:T(8,128)(2,1)S(1)}, u32[]{:S(2)}, u32[]{:S(2)}) collective-permute-start(bf16[128,1024]{1,0:T(8,128)(2,1)S(1)} %get-tuple-element.62), channel_id=1, source_target_pairs={{0,64},{8,72},{16,80},{24,88},{32,96},{40,104},{48,112},{56,120},{... | collective-permute-start | bytes 786440 | tf_op jit(solution)/shard_map/sum_y_second/ppermute | solution.py:440
  41.2 0.0 collective-permute-done.4.refs_4_
  41.2 1.2 %collective-permute-done.5.refs_5_ = bf16[2,128,1024]{2,1,0:T(8,128)(2,1)} collective-permute-done((bf16[2,128,1024]{2,1,0:T(8,128)(2,1)}, bf16[2,128,1024]{2,1,0:T(8,128)(2,1)}, u32[]{:S(2)}, u32[]{:S(2)}) %collective-permute-start.5) | collective-permute-done | bytes 524320 | tf_op jit(solution)/shard_map/sum_x_first/ppermute | solution.py:440
  42.5 2.4 %join_x.1 = (f32[128,1024]{1,0:T(8,128)S(1)}, bf16[128,1024]{1,0:T(8,128)(2,1)S(1)}, f32[128,1024]{1,0:T(8,128)S(1)}) custom-call(s32[3]{0:T(128)S(1)} %pad_add_fusion.1.scal_ref, bf16[4,2,2,2,128,1024]{5,4,3,2,1,0:T(8,128)(2,1)} %bitcast.25, bf16[4,128,1024]{2,1,0:T(8,128)(2,1)S(1)} %collective-permute-done.refs_1_, ...), custom_call_target="tpu_custom_call" | custom-call | flops 1000000 | bytes 65536 | tf_op jit(solution)/shard_map/sum_x_first/join_x/pallas_call | solution.py:107
  44.9 0.5 collective-permute-start.8
  45.4 2.5 %collective-permute-done.9.refs_1_ = bf16[128,1024]{1,0:T(8,128)(2,1)S(1)} collective-permute-done((bf16[128,1024]{1,0:T(8,128)(2,1)S(1)}, bf16[128,1024]{1,0:T(8,128)(2,1)S(1)}, u32[]{:S(2)}, u32[]{:S(2)}) %collective-permute-start.9) | collective-permute-done | bytes 262176 | tf_op jit(solution)/shard_map/sum_y_second/ppermute | solution.py:440
  48.0 0.0 collective-permute-done.10.refs_2_
  48.0 5.1 %collective-permute-done.11.refs_3_ = bf16[128,1024]{1,0:T(8,128)(2,1)S(1)} collective-permute-done((bf16[128,1024]{1,0:T(8,128)(2,1)S(1)}, bf16[128,1024]{1,0:T(8,128)(2,1)S(1)}, u32[]{:S(2)}, u32[]{:S(2)}) %collective-permute-start.11) | collective-permute-done | bytes 262176 | tf_op jit(solution)/shard_map/sum_y_second/ppermute | solution.py:440
  53.0 0.8 norm_sum.1.refs_2_
  53.9 0.0 collective-permute-done.8.refs_1_
  53.9 0.8 norm_both.1.refs_0_.refs_8_
  54.7 3.0 %collective-permute-start.14 = (bf16[2,128,1024]{2,1,0:T(8,128)(2,1)S(1)}, bf16[2,128,1024]{2,1,0:T(8,128)(2,1)S(1)}, u32[]{:S(2)}, u32[]{:S(2)}) collective-permute-start(bf16[2,128,1024]{2,1,0:T(8,128)(2,1)S(1)} %norm_both.1.refs_0_.refs_8_), channel_id=1, source_target_pairs={{0,1},{1,0},{2,3},{3,2},{4,5},{5,4},{6,7},{7,6},{8,9},{9,8},{10,11... | collective-permute-start | bytes 1572872 | tf_op jit(solution)/shard_map/gather/ppermute | solution.py:444
  57.7 4.0 %collective-permute-start.13 = (bf16[2,128,1024]{2,1,0:T(8,128)(2,1)S(1)}, bf16[2,128,1024]{2,1,0:T(8,128)(2,1)S(1)}, u32[]{:S(2)}, u32[]{:S(2)}) collective-permute-start(bf16[2,128,1024]{2,1,0:T(8,128)(2,1)S(1)} %norm_both.1.refs_0_.refs_8_), channel_id=1, source_target_pairs={{0,6},{1,7},{2,0},{3,1},{4,2},{5,3},{6,4},{7,5},{8,14},{9,15},{10,... | collective-permute-start | bytes 1572872 | tf_op jit(solution)/shard_map/gather/ppermute | solution.py:444
  61.7 0.0 collective-permute-start.12
  61.7 0.0 slice-done
  61.7 4.4 %own_keys.1 = (f32[512,1024]{1,0:T(8,128)S(1)}, f32[256,1024]{1,0:T(8,128)S(1)}, bf16[256,1024]{1,0:T(8,128)(2,1)S(1)}, bf16[256,1024]{1,0:T(8,128)(2,1)S(1)}) custom-call(s32[2,12]{1,0:T(2,128)S(1)} %pad_add_fusion.scal_ref, bf16[2,128,1024]{2,1,0:T(8,128)(2,1)S(1)} %norm_both.1.refs_0_.refs_8_, ...), custom_call_target="tpu_custom_call", output_to_operand_aliasing={{0}: (4, {})} | custom-call | flops 1000000 | bytes 65536 | tf_op jit(solution)/shard_map/own_keys/pallas_call | solution.py:212
  66.1 3.5 %collective-permute-done.14.refs_2_ = bf16[2,128,1024]{2,1,0:T(8,128)(2,1)S(1)} collective-permute-done((bf16[2,128,1024]{2,1,0:T(8,128)(2,1)S(1)}, bf16[2,128,1024]{2,1,0:T(8,128)(2,1)S(1)}, u32[]{:S(2)}, u32[]{:S(2)}) %collective-permute-start.14) | collective-permute-done | bytes 524320 | tf_op jit(solution)/shard_map/gather/ppermute | solution.py:444
  69.6 4.0 %collective-permute-start.17 = (bf16[2,128,1024]{2,1,0:T(8,128)(2,1)S(1)}, bf16[2,128,1024]{2,1,0:T(8,128)(2,1)S(1)}, u32[]{:S(2)}, u32[]{:S(2)}) collective-permute-start(bf16[2,128,1024]{2,1,0:T(8,128)(2,1)S(1)} %collective-permute-done.14.refs_2_), channel_id=1, source_target_pairs={{0,6},{1,7},{2,0},{3,1},{4,2},{5,3},{6,4},{7,5},{8,14},{9,15},{10,... | collective-permute-start | bytes 1572872 | tf_op jit(solution)/shard_map/gather/ppermute | solution.py:444
  73.7 0.0 collective-permute-start.16
  73.7 0.0 collective-permute-done.13.refs_1_
  73.7 2.0 %collective-permute-done.12.refs_0_ = bf16[2,128,1024]{2,1,0:T(8,128)(2,1)S(1)} collective-permute-done((bf16[2,128,1024]{2,1,0:T(8,128)(2,1)S(1)}, bf16[2,128,1024]{2,1,0:T(8,128)(2,1)S(1)}, u32[]{:S(2)}, u32[]{:S(2)}) %collective-permute-start.12) | collective-permute-done | bytes 524320 | tf_op jit(solution)/shard_map/gather/ppermute | solution.py:444
  75.7 0.0 collective-permute-start.15
  75.7 7.8 %own_sides.1 = (f32[512,1024]{1,0:T(8,128)S(1)}, f32[256,1024]{1,0:T(8,128)S(1)}) custom-call(s32[2,12]{1,0:T(2,128)S(1)} %pad_add_fusion.scal_ref, bf16[2,128,1024]{2,1,0:T(8,128)(2,1)S(1)} %collective-permute-done.12.refs_0_, bf16[2,128,1024]{2,1,0:T(8,128)(2,1)S(1)} %collective-permute-done.13.refs_1_, ...), custom_call_target="tpu_custom_call", output_to_operand_aliasing={{0}: (6, {}), {1}: (8, {})} | custom-call | flops 1000000 | bytes 65536 | tf_op jit(solution)/shard_map/own_sides/pallas_call | solution.py:212
  83.6 0.1 collective-permute-done.17.refs_1_
  83.6 6.1 %collective-permute-done.16.refs_0_ = bf16[2,128,1024]{2,1,0:T(8,128)(2,1)S(1)} collective-permute-done((bf16[2,128,1024]{2,1,0:T(8,128)(2,1)S(1)}, bf16[2,128,1024]{2,1,0:T(8,128)(2,1)S(1)}, u32[]{:S(2)}, u32[]{:S(2)}) %collective-permute-start.16) | collective-permute-done | bytes 524320 | tf_op jit(solution)/shard_map/gather/ppermute | solution.py:444
  89.7 0.0 collective-permute-start.18
  89.7 5.1 %near_sides.1 = (f32[512,1024]{1,0:T(8,128)S(1)}, f32[256,1024]{1,0:T(8,128)S(1)}) custom-call(s32[2,12]{1,0:T(2,128)S(1)} %pad_add_fusion.scal_ref, bf16[2,128,1024]{2,1,0:T(8,128)(2,1)S(1)} %collective-permute-done.16.refs_0_, bf16[2,128,1024]{2,1,0:T(8,128)(2,1)S(1)} %collective-permute-done.17.refs_1_, ...), custom_call_target="tpu_custom_call", output_to_operand_aliasing={{0}: (5, {}), {1}: (7, {})} | custom-call | flops 1000000 | bytes 65536 | tf_op jit(solution)/shard_map/near_sides/pallas_call | solution.py:212
  94.8 3.5 %collective-permute-done.15.refs_0_ = bf16[2,128,1024]{2,1,0:T(8,128)(2,1)S(1)} collective-permute-done((bf16[2,128,1024]{2,1,0:T(8,128)(2,1)S(1)}, bf16[2,128,1024]{2,1,0:T(8,128)(2,1)S(1)}, u32[]{:S(2)}, u32[]{:S(2)}) %collective-permute-start.15) | collective-permute-done | bytes 524320 | tf_op jit(solution)/shard_map/gather/ppermute | solution.py:444
  98.3 0.6 collective-permute-done.18.refs_1_
  98.9 8.9 %far_finish.1 = (bf16[2,128,1024]{2,1,0:T(8,128)(2,1)}, bf16[512,1024]{1,0:T(8,128)(2,1)}) custom-call(s32[2,12]{1,0:T(2,128)S(1)} %pad_add_fusion.scal_ref, bf16[2,128,1024]{2,1,0:T(8,128)(2,1)S(1)} %collective-permute-done.15.refs_0_, bf16[2,128,1024]{2,1,0:T(8,128)(2,1)S(1)} %collective-permute-done.18.refs_1_, bf16[1024,4096]{1,0:T(8,128)(2,1)S(1)} %bitcast.18, ...), custom_call_target="tpu_custom_call" | custom-call | flops 1000000 | bytes 65536 | tf_op jit(solution)/shard_map/far_finish/pallas_call | solution.py:212
  (8 shorter events, 0.0 us)
Async XLA Ops:
  2.5 2.9 %collective-permute-start.2 = (bf16[4,128,1024]{2,1,0:T(8,128)(2,1)S(1)}, bf16[4,128,1024]{2,1,0:T(8,128)(2,1)S(1)}, u32[]{:S(2)}, u32[]{:S(2)}) collective-permute-start(bf16[4,128,1024]{2,1,0:T(8,128)(2,1)S(1)} %pack.1), channel_id=1, source_target_pairs={{0,8},{8,0},{16,24},{24,16},{32,40},{40,32},{48,56},{56,48},{64,72... | collective-permute-start | bytes 3145736 | tf_op jit(solution)/shard_map/sum_core/ppermute | solution.py:440
  4.7 5.2 %collective-permute-start = (bf16[4,128,1024]{2,1,0:T(8,128)(2,1)S(1)}, bf16[4,128,1024]{2,1,0:T(8,128)(2,1)S(1)}, u32[]{:S(2)}, u32[]{:S(2)}) collective-permute-start(bf16[4,128,1024]{2,1,0:T(8,128)(2,1)S(1)} %get-tuple-element.47), channel_id=1, source_target_pairs={{0,8},{8,0},{16,24},{24,16},{32,40},{40,32},{48,56},{56,48},{64,72... | collective-permute-start | bytes 3145736 | tf_op jit(solution)/shard_map/sum_core/ppermute | solution.py:440
  5.3 4.6 %collective-permute-start.1 = (bf16[4,128,1024]{2,1,0:T(8,128)(2,1)S(1)}, bf16[4,128,1024]{2,1,0:T(8,128)(2,1)S(1)}, u32[]{:S(2)}, u32[]{:S(2)}) collective-permute-start(bf16[4,128,1024]{2,1,0:T(8,128)(2,1)S(1)} %get-tuple-element.48), channel_id=1, source_target_pairs={{0,8},{8,0},{16,24},{24,16},{32,40},{40,32},{48,56},{56,48},{64,72... | collective-permute-start | bytes 3145736 | tf_op jit(solution)/shard_map/sum_core/ppermute | solution.py:440
  8.2 10.9 %copy-start.3 = (s32[512]{0:T(512)S(1)}, s32[512]{0:T(512)}, u32[]{:S(2)}) copy-start(s32[512]{0:T(512)} %param.9) | copy-start | bytes 6148
  8.2 12.1 %copy-start.4 = (s32[2]{0:T(128)S(1)}, s32[2]{0:T(128)}, u32[]{:S(2)}) copy-start(s32[2]{0:T(128)} %param.8) | copy-start | bytes 28
  8.2 26.1 %collective-permute-start.7 = (bf16[4,128,1024]{2,1,0:T(8,128)(2,1)}, bf16[4,128,1024]{2,1,0:T(8,128)(2,1)S(1)}, u32[]{:S(2)}, u32[]{:S(2)}) collective-permute-start(bf16[4,128,1024]{2,1,0:T(8,128)(2,1)} %over_y.1), channel_id=1, source_target_pairs={{0,16},{8,24},{16,0},{24,8},{32,48},{40,56},{48,32},{56,40},{64,80... | collective-permute-start | bytes 3145736 | tf_op jit(solution)/shard_map/sum_y_second/ppermute | solution.py:440
  13.7 20.5 %collective-permute-start.6 = (bf16[4,128,1024]{2,1,0:T(8,128)(2,1)}, bf16[4,128,1024]{2,1,0:T(8,128)(2,1)}, u32[]{:S(2)}, u32[]{:S(2)}) collective-permute-start(bf16[4,128,1024]{2,1,0:T(8,128)(2,1)} %get-tuple-element.52), channel_id=1, source_target_pairs={{0,8},{8,0},{16,24},{24,16},{32,40},{40,32},{48,56},{56,48},{64,72... | collective-permute-start | bytes 3145736 | tf_op jit(solution)/shard_map/sum_core/ppermute | solution.py:440
  14.0 25.7 %collective-permute-start.3 = (bf16[2,128,1024]{2,1,0:T(8,128)(2,1)}, bf16[2,128,1024]{2,1,0:T(8,128)(2,1)}, u32[]{:S(2)}, u32[]{:S(2)}) collective-permute-start(bf16[2,128,1024]{2,1,0:T(8,128)(2,1)} %get-tuple-element.54), channel_id=1, source_target_pairs={{0,32},{8,40},{16,48},{24,56},{32,64},{40,72},{48,80},{56,88},{64,... | collective-permute-start | bytes 1572872 | tf_op jit(solution)/shard_map/sum_x_first/ppermute | solution.py:440
  15.5 25.8 %collective-permute-start.4 = (bf16[2,128,1024]{2,1,0:T(8,128)(2,1)}, bf16[2,128,1024]{2,1,0:T(8,128)(2,1)}, u32[]{:S(2)}, u32[]{:S(2)}) collective-permute-start(bf16[2,128,1024]{2,1,0:T(8,128)(2,1)} %get-tuple-element.55), channel_id=1, source_target_pairs={{0,96},{8,104},{16,112},{24,120},{32,0},{40,8},{48,16},{56,24},{64... | collective-permute-start | bytes 1572872 | tf_op jit(solution)/shard_map/sum_x_first/ppermute | solution.py:440
  17.2 25.3 %collective-permute-start.5 = (bf16[2,128,1024]{2,1,0:T(8,128)(2,1)}, bf16[2,128,1024]{2,1,0:T(8,128)(2,1)}, u32[]{:S(2)}, u32[]{:S(2)}) collective-permute-start(bf16[2,128,1024]{2,1,0:T(8,128)(2,1)} %get-tuple-element.56), channel_id=1, source_target_pairs={{0,64},{8,72},{16,80},{24,88},{32,96},{40,104},{48,112},{56,120},{... | collective-permute-start | bytes 1572872 | tf_op jit(solution)/shard_map/sum_x_first/ppermute | solution.py:440
  22.4 3.4 %copy-start = (bf16[1024,4096]{1,0:T(8,128)(2,1)S(1)}, bf16[1024,4096]{1,0:T(8,128)(2,1)}, u32[]{:S(2)}) copy-start(bf16[1024,4096]{1,0:T(8,128)(2,1)} %refs_2_.3) | copy-start | bytes 25165828
  25.8 1.2 %copy-start.2 = (bf16[512,1024]{1,0:T(8,128)(2,1)S(1)}, bf16[512,1024]{1,0:T(8,128)(2,1)}, u32[]{:S(2)}) copy-start(bf16[512,1024]{1,0:T(8,128)(2,1)} %feats_ref.1) | copy-start | bytes 3145732
  36.3 11.6 %collective-permute-start.9 = (bf16[128,1024]{1,0:T(8,128)(2,1)S(1)}, bf16[128,1024]{1,0:T(8,128)(2,1)S(1)}, u32[]{:S(2)}, u32[]{:S(2)}) collective-permute-start(bf16[128,1024]{1,0:T(8,128)(2,1)S(1)} %get-tuple-element.60), channel_id=1, source_target_pairs={{0,32},{8,40},{16,48},{24,56},{32,64},{40,72},{48,80},{56,88},{64,... | collective-permute-start | bytes 786440 | tf_op jit(solution)/shard_map/sum_y_second/ppermute | solution.py:440
  37.7 10.3 %collective-permute-start.10 = (bf16[128,1024]{1,0:T(8,128)(2,1)S(1)}, bf16[128,1024]{1,0:T(8,128)(2,1)S(1)}, u32[]{:S(2)}, u32[]{:S(2)}) collective-permute-start(bf16[128,1024]{1,0:T(8,128)(2,1)S(1)} %get-tuple-element.61), channel_id=1, source_target_pairs={{0,96},{8,104},{16,112},{24,120},{32,0},{40,8},{48,16},{56,24},{64... | collective-permute-start | bytes 786440 | tf_op jit(solution)/shard_map/sum_y_second/ppermute | solution.py:440
  39.6 22.1 %slice-start = ((s8[8388608]{0:T(1024)(128)(4,1)}), s8[4194304]{0:T(1024)(128)(4,1)S(1)}, s32[]{:S(2)}) async-start(s8[8388608]{0:T(1024)(128)(4,1)} %bitcast.17), calls=%async_computation | async-start | bytes 8388608
  39.6 22.1 %slice-start.1 = ((s8[8388608]{0:T(1024)(128)(4,1)}), s8[4194304]{0:T(1024)(128)(4,1)S(1)}, s32[]{:S(2)}) async-start(s8[8388608]{0:T(1024)(128)(4,1)} %bitcast.17), calls=%async_computation.1 | async-start | bytes 8388608
  39.6 13.4 %collective-permute-start.11 = (bf16[128,1024]{1,0:T(8,128)(2,1)S(1)}, bf16[128,1024]{1,0:T(8,128)(2,1)S(1)}, u32[]{:S(2)}, u32[]{:S(2)}) collective-permute-start(bf16[128,1024]{1,0:T(8,128)(2,1)S(1)} %get-tuple-element.62), channel_id=1, source_target_pairs={{0,64},{8,72},{16,80},{24,88},{32,96},{40,104},{48,112},{56,120},{... | collective-permute-start | bytes 786440 | tf_op jit(solution)/shard_map/sum_y_second/ppermute | solution.py:440
  44.9 9.0 %collective-permute-start.8 = (bf16[128,1024]{1,0:T(8,128)(2,1)S(1)}, bf16[128,1024]{1,0:T(8,128)(2,1)S(1)}, u32[]{:S(2)}, u32[]{:S(2)}) collective-permute-start(bf16[128,1024]{1,0:T(8,128)(2,1)S(1)} %get-tuple-element.67), channel_id=1, source_target_pairs={{0,16},{8,24},{16,0},{24,8},{32,48},{40,56},{48,32},{56,40},{64,80... | collective-permute-start | bytes 786440 | tf_op jit(solution)/shard_map/sum_x_first/ppermute | solution.py:440
  54.7 15.0 %collective-permute-start.14 = (bf16[2,128,1024]{2,1,0:T(8,128)(2,1)S(1)}, bf16[2,128,1024]{2,1,0:T(8,128)(2,1)S(1)}, u32[]{:S(2)}, u32[]{:S(2)}) collective-permute-start(bf16[2,128,1024]{2,1,0:T(8,128)(2,1)S(1)} %norm_both.1.refs_0_.refs_8_), channel_id=1, source_target_pairs={{0,1},{1,0},{2,3},{3,2},{4,5},{5,4},{6,7},{7,6},{8,9},{9,8},{10,11... | collective-permute-start | bytes 1572872 | tf_op jit(solution)/shard_map/gather/ppermute | solution.py:444
  57.7 16.0 %collective-permute-start.13 = (bf16[2,128,1024]{2,1,0:T(8,128)(2,1)S(1)}, bf16[2,128,1024]{2,1,0:T(8,128)(2,1)S(1)}, u32[]{:S(2)}, u32[]{:S(2)}) collective-permute-start(bf16[2,128,1024]{2,1,0:T(8,128)(2,1)S(1)} %norm_both.1.refs_0_.refs_8_), channel_id=1, source_target_pairs={{0,6},{1,7},{2,0},{3,1},{4,2},{5,3},{6,4},{7,5},{8,14},{9,15},{10,... | collective-permute-start | bytes 1572872 | tf_op jit(solution)/shard_map/gather/ppermute | solution.py:444
  61.7 14.0 %collective-permute-start.12 = (bf16[2,128,1024]{2,1,0:T(8,128)(2,1)S(1)}, bf16[2,128,1024]{2,1,0:T(8,128)(2,1)S(1)}, u32[]{:S(2)}, u32[]{:S(2)}) collective-permute-start(bf16[2,128,1024]{2,1,0:T(8,128)(2,1)S(1)} %norm_both.1.refs_0_.refs_8_), channel_id=1, source_target_pairs={{0,2},{1,3},{2,4},{3,5},{4,6},{5,7},{6,0},{7,1},{8,10},{9,11},{10,... | collective-permute-start | bytes 1572872 | tf_op jit(solution)/shard_map/gather/ppermute | solution.py:444
  69.6 14.0 %collective-permute-start.17 = (bf16[2,128,1024]{2,1,0:T(8,128)(2,1)S(1)}, bf16[2,128,1024]{2,1,0:T(8,128)(2,1)S(1)}, u32[]{:S(2)}, u32[]{:S(2)}) collective-permute-start(bf16[2,128,1024]{2,1,0:T(8,128)(2,1)S(1)} %collective-permute-done.14.refs_2_), channel_id=1, source_target_pairs={{0,6},{1,7},{2,0},{3,1},{4,2},{5,3},{6,4},{7,5},{8,14},{9,15},{10,... | collective-permute-start | bytes 1572872 | tf_op jit(solution)/shard_map/gather/ppermute | solution.py:444
  73.7 16.1 %collective-permute-start.16 = (bf16[2,128,1024]{2,1,0:T(8,128)(2,1)S(1)}, bf16[2,128,1024]{2,1,0:T(8,128)(2,1)S(1)}, u32[]{:S(2)}, u32[]{:S(2)}) collective-permute-start(bf16[2,128,1024]{2,1,0:T(8,128)(2,1)S(1)} %collective-permute-done.14.refs_2_), channel_id=1, source_target_pairs={{0,2},{1,3},{2,4},{3,5},{4,6},{5,7},{6,0},{7,1},{8,10},{9,11},{10,... | collective-permute-start | bytes 1572872 | tf_op jit(solution)/shard_map/gather/ppermute | solution.py:444
  75.7 22.6 %collective-permute-start.15 = (bf16[2,128,1024]{2,1,0:T(8,128)(2,1)S(1)}, bf16[2,128,1024]{2,1,0:T(8,128)(2,1)S(1)}, u32[]{:S(2)}, u32[]{:S(2)}) collective-permute-start(bf16[2,128,1024]{2,1,0:T(8,128)(2,1)S(1)} %collective-permute-done.12.refs_0_), channel_id=1, source_target_pairs={{0,2},{1,3},{2,4},{3,5},{4,6},{5,7},{6,0},{7,1},{8,10},{9,11},{10,... | collective-permute-start | bytes 1572872 | tf_op jit(solution)/shard_map/gather/ppermute | solution.py:444
  89.7 9.2 %collective-permute-start.18 = (bf16[2,128,1024]{2,1,0:T(8,128)(2,1)S(1)}, bf16[2,128,1024]{2,1,0:T(8,128)(2,1)S(1)}, u32[]{:S(2)}, u32[]{:S(2)}) collective-permute-start(bf16[2,128,1024]{2,1,0:T(8,128)(2,1)S(1)} %collective-permute-done.17.refs_1_), channel_id=1, source_target_pairs={{0,6},{1,7},{2,0},{3,1},{4,2},{5,3},{6,4},{7,5},{8,14},{9,15},{10,... | collective-permute-start | bytes 1572872 | tf_op jit(solution)/shard_map/gather/ppermute | solution.py:444
  89.7 9.2 %copy-start.1 = (bf16[1024,1024]{1,0:T(8,128)(2,1)S(1)}, bf16[1024,1024]{1,0:T(8,128)(2,1)}, u32[]{:S(2)}) copy-start(bf16[1024,1024]{1,0:T(8,128)(2,1)} %refs_12_.1) | copy-start | bytes 6291460

commit v4 on v3

--- a/solution.py
+++ b/solution.py
@@ -21,7 +21,7 @@
 GROUP = 512
 SHIFTS = (0, -1, 1, 2)
 HIDE = 1 << 16
-HOPS = (1, 3, 2)
+HOPS = (2, 1, 3)
 SIDES = (lambda s: s[1], lambda s: 1 - s[1])
 
 

time: 108 us -> 109 us (level)
  starting transfers between devices: 24.3 us -> 26.6 us
  waiting for transfers between devices: 24.7 us -> 22.6 us
    ppermute x12, waiting for transfers between devices: 8.84 us -> 5.96 us  [to_user(): return lax.ppermute(array, 'user', user_perm(dx, dy, dcore))]
    ppermute x12, starting transfers between devices: 13.2 us -> 15.6 us  [to_user(): return lax.ppermute(array, 'user', user_perm(dx, dy, dcore))]
  transfers between devices with their start and end apart: 19 -> 19, of which waited for: 9 -> 8; matrix products, arithmetic and copies ran while one was open for 3% -> 3% of each run, Pallas kernels for 36% -> 36%
where the time goes in v4:
time: 109 us; the launch traced here: 108 us
  Pallas kernels  49.9 us (46%)
  starting transfers between devices  26.6 us (24%)
  waiting for transfers between devices  22.6 us (21%)
  local copies, waits for them, and re-layouts  6.67 us (6%)
  between operations  1.65 us (2%)
    pallas_call x5, Pallas kernels, kernel_call(): pl.pallas_call(body, in_specs=in_specs, out_specs=[pl.BlockSpec(memory_sp...  33.4 us
    ppermute x7, waiting for transfers between devices, to_cand(): return lax.ppermute(array, 'cand', cand_perm(dz, dy))  16.6 us
    pallas_call x8, Pallas kernels, block_sums(): pl.pallas_call(body, in_specs=[pl.BlockSpec(memory_space=pltpu.SMEM)] + [...  16.5 us
    ppermute x12, starting transfers between devices, to_user(): return lax.ppermute(array, 'user', user_perm(dx, dy, dcore))  15.6 us
    ppermute x7, starting transfers between devices, to_cand(): return lax.ppermute(array, 'cand', cand_perm(dz, dy))  11.1 us
    ppermute x12, waiting for transfers between devices, to_user(): return lax.ppermute(array, 'user', user_perm(dx, dy, dcore))  5.96 us
    unnamed x14, local copies, waits for them, and re-layouts  4.62 us
  transfers between devices with their start and end apart: 19, of which 8 were waited for; matrix products, arithmetic and copies ran while one was open for 3% of the time, Pallas kernels for 36%

profile of v4, /device:TPU:0, one launch (start us, length us, event | category | flops | bytes accessed | tf_op | source)
XLA Modules:
  0.0 108.2 jit_solution(10497411209767955740)
XLA Ops:
  0.6 0.1 pad_add_fusion.1.scal_ref
  0.7 1.8 %pack.1 = bf16[4,128,1024]{2,1,0:T(8,128)(2,1)S(1)} custom-call(s32[3]{0:T(128)S(1)} %pad_add_fusion.1.scal_ref, bf16[4,2,2,2,128,1024]{5,4,3,2,1,0:T(8,128)(2,1)} %bitcast.20), custom_call_target="tpu_custom_call" | custom-call | flops 1000000 | bytes 65536 | tf_op jit(solution)/shard_map/sum_core/pack/pallas_call | solution.py:107
  2.5 0.1 collective-permute-start.2
  2.6 2.1 %pack_all.1 = (bf16[4,128,1024]{2,1,0:T(8,128)(2,1)S(1)}, bf16[4,128,1024]{2,1,0:T(8,128)(2,1)S(1)}) custom-call(s32[3]{0:T(128)S(1)} %pad_add_fusion.1.scal_ref, bf16[4,2,2,2,128,1024]{5,4,3,2,1,0:T(8,128)(2,1)} %bitcast.21), custom_call_target="tpu_custom_call" | custom-call | flops 1000000 | bytes 65536 | tf_op jit(solution)/shard_map/sum_core/pack_all/pallas_call | solution.py:107
  4.7 0.6 collective-permute-start
  5.3 0.1 collective-permute-start.1
  5.4 0.0 collective-permute-done.2.refs_1_
  5.4 2.8 %over_y.1 = bf16[4,128,1024]{2,1,0:T(8,128)(2,1)} custom-call(s32[3]{0:T(128)S(1)} %pad_add_fusion.1.scal_ref, bf16[4,2,2,2,128,1024]{5,4,3,2,1,0:T(8,128)(2,1)} %bitcast.22, bf16[4,128,1024]{2,1,0:T(8,128)(2,1)S(1)} %collective-permute-done.2.refs_1_), custom_call_target="tpu_custom_call" | custom-call | flops 1000000 | bytes 65536 | tf_op jit(solution)/shard_map/sum_y_second/over_y/pallas_call | solution.py:107
  8.2 0.0 copy-start.3
  8.2 0.0 copy-start.4
  8.2 1.7 %collective-permute-start.7 = (bf16[4,128,1024]{2,1,0:T(8,128)(2,1)}, bf16[4,128,1024]{2,1,0:T(8,128)(2,1)S(1)}, u32[]{:S(2)}, u32[]{:S(2)}) collective-permute-start(bf16[4,128,1024]{2,1,0:T(8,128)(2,1)} %over_y.1), channel_id=1, source_target_pairs={{0,16},{8,24},{16,0},{24,8},{32,48},{40,56},{48,32},{56,40},{64,80... | collective-permute-start | bytes 3145736 | tf_op jit(solution)/shard_map/sum_y_second/ppermute | solution.py:440
  9.9 0.0 collective-permute-done.refs_1_
  9.9 0.0 collective-permute-done.1.refs_2_
  9.9 3.8 %away_x.1 = (bf16[2,128,1024]{2,1,0:T(8,128)(2,1)}, bf16[2,128,1024]{2,1,0:T(8,128)(2,1)}, bf16[2,128,1024]{2,1,0:T(8,128)(2,1)}, bf16[4,128,1024]{2,1,0:T(8,128)(2,1)}) custom-call(s32[3]{0:T(128)S(1)} %pad_add_fusion.1.scal_ref, bf16[4,2,2,2,128,1024]{5,4,3,2,1,0:T(8,128)(2,1)} %bitcast.23, bf16[4,128,1024]{2,1,0:T(8,128)(2,1)S(1)} %collective-permute-done.refs_1_, ...), custom_call_target="tpu_custom_call" | custom-call | flops 1000000 | bytes 65536 | tf_op jit(solution)/shard_map/sum_x_first/away_x/pallas_call | solution.py:107
  13.7 0.2 collective-permute-start.6
  14.0 3.0 %collective-permute-start.3 = (bf16[2,128,1024]{2,1,0:T(8,128)(2,1)}, bf16[2,128,1024]{2,1,0:T(8,128)(2,1)}, u32[]{:S(2)}, u32[]{:S(2)}) collective-permute-start(bf16[2,128,1024]{2,1,0:T(8,128)(2,1)} %get-tuple-element.54), channel_id=1, source_target_pairs={{0,64},{8,72},{16,80},{24,88},{32,96},{40,104},{48,112},{56,120},{... | collective-permute-start | bytes 1572872 | tf_op jit(solution)/shard_map/sum_x_first/ppermute | solution.py:440
  17.0 0.6 collective-permute-start.4
  17.6 2.6 %collective-permute-start.5 = (bf16[2,128,1024]{2,1,0:T(8,128)(2,1)}, bf16[2,128,1024]{2,1,0:T(8,128)(2,1)}, u32[]{:S(2)}, u32[]{:S(2)}) collective-permute-start(bf16[2,128,1024]{2,1,0:T(8,128)(2,1)} %get-tuple-element.56), channel_id=1, source_target_pairs={{0,96},{8,104},{16,112},{24,120},{32,0},{40,8},{48,16},{56,24},{64... | collective-permute-start | bytes 1572872 | tf_op jit(solution)/shard_map/sum_x_first/ppermute | solution.py:440
  20.2 0.0 copy-done.3
  20.2 0.7 fusion
  21.5 0.0 copy-done.4
  21.5 0.6 fusion.1
  22.1 0.7 stack.79
  22.9 0.7 stack.77
  23.6 0.0 copy-start
  23.6 3.4 %copy-done = bf16[1024,4096]{1,0:T(8,128)(2,1)S(1)} copy-done((bf16[1024,4096]{1,0:T(8,128)(2,1)S(1)}, bf16[1024,4096]{1,0:T(8,128)(2,1)}, u32[]{:S(2)}) %copy-start) | copy-done | bytes 8388632
  27.0 1.2 %copy-done.2 = bf16[512,1024]{1,0:T(8,128)(2,1)S(1)} copy-done((bf16[512,1024]{1,0:T(8,128)(2,1)S(1)}, bf16[512,1024]{1,0:T(8,128)(2,1)}, u32[]{:S(2)}) %copy-start.2) | copy-done | bytes 1048600
  28.2 7.2 %cand_project.1 = (bf16[512,1024]{1,0:T(8,128)(2,1)S(1)}, bf16[512,1024]{1,0:T(8,128)(2,1)S(1)}, bf16[512,1024]{1,0:T(8,128)(2,1)S(1)}, bf16[512,512]{1,0:T(8,128)(2,1)S(1)}, f32[512,1024]{1,0:T(8,128)S(1)}) custom-call(s32[1,512]{1,0:T(1,128)S(1)} %bitcast.19, bf16[512,1024]{1,0:T(8,128)(2,1)S(1)} %copy-done.2, bf16[1024,4096]{1,0:T(8,128)(2,1)S(1)} %copy-done), custom_call_target="tpu_custom_call" | custom-call | flops 1000000 | bytes 65536 | tf_op jit(solution)/shard_map/cand_project/pallas_call | solution.py:212
  35.4 0.0 collective-permute-done.7.refs_2_.refs_7_
  35.5 0.0 collective-permute-done.6.refs_1_.refs_6_
  35.5 2.0 %join_y.1 = (bf16[128,1024]{1,0:T(8,128)(2,1)S(1)}, bf16[128,1024]{1,0:T(8,128)(2,1)S(1)}, bf16[128,1024]{1,0:T(8,128)(2,1)S(1)}) custom-call(s32[3]{0:T(128)S(1)} %pad_add_fusion.1.scal_ref, bf16[4,2,2,2,128,1024]{5,4,3,2,1,0:T(8,128)(2,1)} %bitcast.24, bf16[4,128,1024]{2,1,0:T(8,128)(2,1)} %collective-permute-done.6.refs_1_.refs_6_, ...), custom_call_target="tpu_custom_call" | custom-call | flops 1000000 | bytes 65536 | tf_op jit(solution)/shard_map/sum_y_second/join_y/pallas_call | solution.py:107
  37.5 1.7 %collective-permute-start.9 = (bf16[128,1024]{1,0:T(8,128)(2,1)S(1)}, bf16[128,1024]{1,0:T(8,128)(2,1)S(1)}, u32[]{:S(2)}, u32[]{:S(2)}) collective-permute-start(bf16[128,1024]{1,0:T(8,128)(2,1)S(1)} %get-tuple-element.60), channel_id=1, source_target_pairs={{0,64},{8,72},{16,80},{24,88},{32,96},{40,104},{48,112},{56,120},{... | collective-permute-start | bytes 786440 | tf_op jit(solution)/shard_map/sum_y_second/ppermute | solution.py:440
  39.2 0.6 collective-permute-start.10
  39.8 0.0 collective-permute-done.3.refs_3_
  39.8 2.6 %collective-permute-start.11 = (bf16[128,1024]{1,0:T(8,128)(2,1)S(1)}, bf16[128,1024]{1,0:T(8,128)(2,1)S(1)}, u32[]{:S(2)}, u32[]{:S(2)}) collective-permute-start(bf16[128,1024]{1,0:T(8,128)(2,1)S(1)} %get-tuple-element.62), channel_id=1, source_target_pairs={{0,96},{8,104},{16,112},{24,120},{32,0},{40,8},{48,16},{56,24},{64... | collective-permute-start | bytes 786440 | tf_op jit(solution)/shard_map/sum_y_second/ppermute | solution.py:440
  42.5 0.0 collective-permute-done.4.refs_4_
  42.5 0.0 collective-permute-done.5.refs_5_
  42.5 2.4 %join_x.1 = (f32[128,1024]{1,0:T(8,128)S(1)}, bf16[128,1024]{1,0:T(8,128)(2,1)S(1)}, f32[128,1024]{1,0:T(8,128)S(1)}) custom-call(s32[3]{0:T(128)S(1)} %pad_add_fusion.1.scal_ref, bf16[4,2,2,2,128,1024]{5,4,3,2,1,0:T(8,128)(2,1)} %bitcast.25, bf16[4,128,1024]{2,1,0:T(8,128)(2,1)S(1)} %collective-permute-done.refs_1_, ...), custom_call_target="tpu_custom_call" | custom-call | flops 1000000 | bytes 65536 | tf_op jit(solution)/shard_map/sum_x_first/join_x/pallas_call | solution.py:107
  44.9 1.7 %collective-permute-start.8 = (bf16[128,1024]{1,0:T(8,128)(2,1)S(1)}, bf16[128,1024]{1,0:T(8,128)(2,1)S(1)}, u32[]{:S(2)}, u32[]{:S(2)}) collective-permute-start(bf16[128,1024]{1,0:T(8,128)(2,1)S(1)} %get-tuple-element.67), channel_id=1, source_target_pairs={{0,16},{8,24},{16,0},{24,8},{32,48},{40,56},{48,32},{56,40},{64,80... | collective-permute-start | bytes 786440 | tf_op jit(solution)/shard_map/sum_x_first/ppermute | solution.py:440
  46.6 1.8 %collective-permute-done.9.refs_1_ = bf16[128,1024]{1,0:T(8,128)(2,1)S(1)} collective-permute-done((bf16[128,1024]{1,0:T(8,128)(2,1)S(1)}, bf16[128,1024]{1,0:T(8,128)(2,1)S(1)}, u32[]{:S(2)}, u32[]{:S(2)}) %collective-permute-start.9) | collective-permute-done | bytes 262176 | tf_op jit(solution)/shard_map/sum_y_second/ppermute | solution.py:440
  48.4 4.1 %collective-permute-done.10.refs_2_ = bf16[128,1024]{1,0:T(8,128)(2,1)S(1)} collective-permute-done((bf16[128,1024]{1,0:T(8,128)(2,1)S(1)}, bf16[128,1024]{1,0:T(8,128)(2,1)S(1)}, u32[]{:S(2)}, u32[]{:S(2)}) %collective-permute-start.10) | collective-permute-done | bytes 262176 | tf_op jit(solution)/shard_map/sum_y_second/ppermute | solution.py:440
  52.4 0.0 collective-permute-done.11.refs_3_
  52.5 0.8 norm_sum.1.refs_2_
  53.3 0.0 collective-permute-done.8.refs_1_
  53.4 0.8 norm_both.1.refs_0_.refs_8_
  54.2 3.0 %collective-permute-start.14 = (bf16[2,128,1024]{2,1,0:T(8,128)(2,1)S(1)}, bf16[2,128,1024]{2,1,0:T(8,128)(2,1)S(1)}, u32[]{:S(2)}, u32[]{:S(2)}) collective-permute-start(bf16[2,128,1024]{2,1,0:T(8,128)(2,1)S(1)} %norm_both.1.refs_0_.refs_8_), channel_id=1, source_target_pairs={{0,1},{1,0},{2,3},{3,2},{4,5},{5,4},{6,7},{7,6},{8,9},{9,8},{10,11... | collective-permute-start | bytes 1572872 | tf_op jit(solution)/shard_map/gather/ppermute | solution.py:444
  57.1 4.0 %collective-permute-start.13 = (bf16[2,128,1024]{2,1,0:T(8,128)(2,1)S(1)}, bf16[2,128,1024]{2,1,0:T(8,128)(2,1)S(1)}, u32[]{:S(2)}, u32[]{:S(2)}) collective-permute-start(bf16[2,128,1024]{2,1,0:T(8,128)(2,1)S(1)} %norm_both.1.refs_0_.refs_8_), channel_id=1, source_target_pairs={{0,6},{1,7},{2,0},{3,1},{4,2},{5,3},{6,4},{7,5},{8,14},{9,15},{10,... | collective-permute-start | bytes 1572872 | tf_op jit(solution)/shard_map/gather/ppermute | solution.py:444
  61.2 0.0 collective-permute-start.12
  61.2 0.0 slice-done.1
  61.2 4.4 %own_keys.1 = (f32[512,1024]{1,0:T(8,128)S(1)}, f32[256,1024]{1,0:T(8,128)S(1)}, bf16[256,1024]{1,0:T(8,128)(2,1)S(1)}, bf16[256,1024]{1,0:T(8,128)(2,1)S(1)}) custom-call(s32[2,12]{1,0:T(2,128)S(1)} %pad_add_fusion.scal_ref, bf16[2,128,1024]{2,1,0:T(8,128)(2,1)S(1)} %norm_both.1.refs_0_.refs_8_, ...), custom_call_target="tpu_custom_call", output_to_operand_aliasing={{0}: (4, {})} | custom-call | flops 1000000 | bytes 65536 | tf_op jit(solution)/shard_map/own_keys/pallas_call | solution.py:212
  65.6 4.0 %collective-permute-done.14.refs_2_ = bf16[2,128,1024]{2,1,0:T(8,128)(2,1)S(1)} collective-permute-done((bf16[2,128,1024]{2,1,0:T(8,128)(2,1)S(1)}, bf16[2,128,1024]{2,1,0:T(8,128)(2,1)S(1)}, u32[]{:S(2)}, u32[]{:S(2)}) %collective-permute-start.14) | collective-permute-done | bytes 524320 | tf_op jit(solution)/shard_map/gather/ppermute | solution.py:444
  69.5 4.0 %collective-permute-start.17 = (bf16[2,128,1024]{2,1,0:T(8,128)(2,1)S(1)}, bf16[2,128,1024]{2,1,0:T(8,128)(2,1)S(1)}, u32[]{:S(2)}, u32[]{:S(2)}) collective-permute-start(bf16[2,128,1024]{2,1,0:T(8,128)(2,1)S(1)} %collective-permute-done.14.refs_2_), channel_id=1, source_target_pairs={{0,6},{1,7},{2,0},{3,1},{4,2},{5,3},{6,4},{7,5},{8,14},{9,15},{10,... | collective-permute-start | bytes 1572872 | tf_op jit(solution)/shard_map/gather/ppermute | solution.py:444
  73.6 0.0 collective-permute-start.16
  73.6 0.0 collective-permute-done.13.refs_1_
  73.6 2.0 %collective-permute-done.12.refs_0_ = bf16[2,128,1024]{2,1,0:T(8,128)(2,1)S(1)} collective-permute-done((bf16[2,128,1024]{2,1,0:T(8,128)(2,1)S(1)}, bf16[2,128,1024]{2,1,0:T(8,128)(2,1)S(1)}, u32[]{:S(2)}, u32[]{:S(2)}) %collective-permute-start.12) | collective-permute-done | bytes 524320 | tf_op jit(solution)/shard_map/gather/ppermute | solution.py:444
  75.6 0.0 collective-permute-start.15
  75.6 7.8 %own_sides.1 = (f32[512,1024]{1,0:T(8,128)S(1)}, f32[256,1024]{1,0:T(8,128)S(1)}) custom-call(s32[2,12]{1,0:T(2,128)S(1)} %pad_add_fusion.scal_ref, bf16[2,128,1024]{2,1,0:T(8,128)(2,1)S(1)} %collective-permute-done.12.refs_0_, bf16[2,128,1024]{2,1,0:T(8,128)(2,1)S(1)} %collective-permute-done.13.refs_1_, ...), custom_call_target="tpu_custom_call", output_to_operand_aliasing={{0}: (6, {}), {1}: (8, {})} | custom-call | flops 1000000 | bytes 65536 | tf_op jit(solution)/shard_map/own_sides/pallas_call | solution.py:212
  83.5 0.6 collective-permute-done.17.refs_1_
  84.0 5.6 %collective-permute-done.16.refs_0_ = bf16[2,128,1024]{2,1,0:T(8,128)(2,1)S(1)} collective-permute-done((bf16[2,128,1024]{2,1,0:T(8,128)(2,1)S(1)}, bf16[2,128,1024]{2,1,0:T(8,128)(2,1)S(1)}, u32[]{:S(2)}, u32[]{:S(2)}) %collective-permute-start.16) | collective-permute-done | bytes 524320 | tf_op jit(solution)/shard_map/gather/ppermute | solution.py:444
  89.6 0.0 collective-permute-start.18
  89.6 5.1 %near_sides.1 = (f32[512,1024]{1,0:T(8,128)S(1)}, f32[256,1024]{1,0:T(8,128)S(1)}) custom-call(s32[2,12]{1,0:T(2,128)S(1)} %pad_add_fusion.scal_ref, bf16[2,128,1024]{2,1,0:T(8,128)(2,1)S(1)} %collective-permute-done.16.refs_0_, bf16[2,128,1024]{2,1,0:T(8,128)(2,1)S(1)} %collective-permute-done.17.refs_1_, ...), custom_call_target="tpu_custom_call", output_to_operand_aliasing={{0}: (5, {}), {1}: (7, {})} | custom-call | flops 1000000 | bytes 65536 | tf_op jit(solution)/shard_map/near_sides/pallas_call | solution.py:212
  94.7 4.0 %collective-permute-done.15.refs_0_ = bf16[2,128,1024]{2,1,0:T(8,128)(2,1)S(1)} collective-permute-done((bf16[2,128,1024]{2,1,0:T(8,128)(2,1)S(1)}, bf16[2,128,1024]{2,1,0:T(8,128)(2,1)S(1)}, u32[]{:S(2)}, u32[]{:S(2)}) %collective-permute-start.15) | collective-permute-done | bytes 524320 | tf_op jit(solution)/shard_map/gather/ppermute | solution.py:444
  98.7 0.5 collective-permute-done.18.refs_1_
  99.2 8.9 %far_finish.1 = (bf16[2,128,1024]{2,1,0:T(8,128)(2,1)}, bf16[512,1024]{1,0:T(8,128)(2,1)}) custom-call(s32[2,12]{1,0:T(2,128)S(1)} %pad_add_fusion.scal_ref, bf16[2,128,1024]{2,1,0:T(8,128)(2,1)S(1)} %collective-permute-done.15.refs_0_, bf16[2,128,1024]{2,1,0:T(8,128)(2,1)S(1)} %collective-permute-done.18.refs_1_, bf16[1024,4096]{1,0:T(8,128)(2,1)S(1)} %bitcast.18, ...), custom_call_target="tpu_custom_call" | custom-call | flops 1000000 | bytes 65536 | tf_op jit(solution)/shard_map/far_finish/pallas_call | solution.py:212
  (8 shorter events, 0.0 us)
Async XLA Ops:
  2.5 2.9 %collective-permute-start.2 = (bf16[4,128,1024]{2,1,0:T(8,128)(2,1)S(1)}, bf16[4,128,1024]{2,1,0:T(8,128)(2,1)S(1)}, u32[]{:S(2)}, u32[]{:S(2)}) collective-permute-start(bf16[4,128,1024]{2,1,0:T(8,128)(2,1)S(1)} %pack.1), channel_id=1, source_target_pairs={{0,8},{8,0},{16,24},{24,16},{32,40},{40,32},{48,56},{56,48},{64,72... | collective-permute-start | bytes 3145736 | tf_op jit(solution)/shard_map/sum_core/ppermute | solution.py:440
  4.7 5.2 %collective-permute-start = (bf16[4,128,1024]{2,1,0:T(8,128)(2,1)S(1)}, bf16[4,128,1024]{2,1,0:T(8,128)(2,1)S(1)}, u32[]{:S(2)}, u32[]{:S(2)}) collective-permute-start(bf16[4,128,1024]{2,1,0:T(8,128)(2,1)S(1)} %get-tuple-element.47), channel_id=1, source_target_pairs={{0,8},{8,0},{16,24},{24,16},{32,40},{40,32},{48,56},{56,48},{64,72... | collective-permute-start | bytes 3145736 | tf_op jit(solution)/shard_map/sum_core/ppermute | solution.py:440
  5.3 4.6 %collective-permute-start.1 = (bf16[4,128,1024]{2,1,0:T(8,128)(2,1)S(1)}, bf16[4,128,1024]{2,1,0:T(8,128)(2,1)S(1)}, u32[]{:S(2)}, u32[]{:S(2)}) collective-permute-start(bf16[4,128,1024]{2,1,0:T(8,128)(2,1)S(1)} %get-tuple-element.48), channel_id=1, source_target_pairs={{0,8},{8,0},{16,24},{24,16},{32,40},{40,32},{48,56},{56,48},{64,72... | collective-permute-start | bytes 3145736 | tf_op jit(solution)/shard_map/sum_core/ppermute | solution.py:440
  8.2 12.1 %copy-start.3 = (s32[512]{0:T(512)S(1)}, s32[512]{0:T(512)}, u32[]{:S(2)}) copy-start(s32[512]{0:T(512)} %param.9) | copy-start | bytes 6148
  8.2 13.4 %copy-start.4 = (s32[2]{0:T(128)S(1)}, s32[2]{0:T(128)}, u32[]{:S(2)}) copy-start(s32[2]{0:T(128)} %param.8) | copy-start | bytes 28
  8.2 27.3 %collective-permute-start.7 = (bf16[4,128,1024]{2,1,0:T(8,128)(2,1)}, bf16[4,128,1024]{2,1,0:T(8,128)(2,1)S(1)}, u32[]{:S(2)}, u32[]{:S(2)}) collective-permute-start(bf16[4,128,1024]{2,1,0:T(8,128)(2,1)} %over_y.1), channel_id=1, source_target_pairs={{0,16},{8,24},{16,0},{24,8},{32,48},{40,56},{48,32},{56,40},{64,80... | collective-permute-start | bytes 3145736 | tf_op jit(solution)/shard_map/sum_y_second/ppermute | solution.py:440
  13.7 21.7 %collective-permute-start.6 = (bf16[4,128,1024]{2,1,0:T(8,128)(2,1)}, bf16[4,128,1024]{2,1,0:T(8,128)(2,1)}, u32[]{:S(2)}, u32[]{:S(2)}) collective-permute-start(bf16[4,128,1024]{2,1,0:T(8,128)(2,1)} %get-tuple-element.52), channel_id=1, source_target_pairs={{0,8},{8,0},{16,24},{24,16},{32,40},{40,32},{48,56},{56,48},{64,72... | collective-permute-start | bytes 3145736 | tf_op jit(solution)/shard_map/sum_core/ppermute | solution.py:440
  14.0 25.9 %collective-permute-start.3 = (bf16[2,128,1024]{2,1,0:T(8,128)(2,1)}, bf16[2,128,1024]{2,1,0:T(8,128)(2,1)}, u32[]{:S(2)}, u32[]{:S(2)}) collective-permute-start(bf16[2,128,1024]{2,1,0:T(8,128)(2,1)} %get-tuple-element.54), channel_id=1, source_target_pairs={{0,64},{8,72},{16,80},{24,88},{32,96},{40,104},{48,112},{56,120},{... | collective-permute-start | bytes 1572872 | tf_op jit(solution)/shard_map/sum_x_first/ppermute | solution.py:440
  17.0 25.5 %collective-permute-start.4 = (bf16[2,128,1024]{2,1,0:T(8,128)(2,1)}, bf16[2,128,1024]{2,1,0:T(8,128)(2,1)}, u32[]{:S(2)}, u32[]{:S(2)}) collective-permute-start(bf16[2,128,1024]{2,1,0:T(8,128)(2,1)} %get-tuple-element.55), channel_id=1, source_target_pairs={{0,32},{8,40},{16,48},{24,56},{32,64},{40,72},{48,80},{56,88},{64,... | collective-permute-start | bytes 1572872 | tf_op jit(solution)/shard_map/sum_x_first/ppermute | solution.py:440
  17.6 24.9 %collective-permute-start.5 = (bf16[2,128,1024]{2,1,0:T(8,128)(2,1)}, bf16[2,128,1024]{2,1,0:T(8,128)(2,1)}, u32[]{:S(2)}, u32[]{:S(2)}) collective-permute-start(bf16[2,128,1024]{2,1,0:T(8,128)(2,1)} %get-tuple-element.56), channel_id=1, source_target_pairs={{0,96},{8,104},{16,112},{24,120},{32,0},{40,8},{48,16},{56,24},{64... | collective-permute-start | bytes 1572872 | tf_op jit(solution)/shard_map/sum_x_first/ppermute | solution.py:440
  23.6 3.4 %copy-start = (bf16[1024,4096]{1,0:T(8,128)(2,1)S(1)}, bf16[1024,4096]{1,0:T(8,128)(2,1)}, u32[]{:S(2)}) copy-start(bf16[1024,4096]{1,0:T(8,128)(2,1)} %refs_2_.3) | copy-start | bytes 25165828
  27.0 1.2 %copy-start.2 = (bf16[512,1024]{1,0:T(8,128)(2,1)S(1)}, bf16[512,1024]{1,0:T(8,128)(2,1)}, u32[]{:S(2)}) copy-start(bf16[512,1024]{1,0:T(8,128)(2,1)} %feats_ref.1) | copy-start | bytes 3145732
  37.5 10.9 %collective-permute-start.9 = (bf16[128,1024]{1,0:T(8,128)(2,1)S(1)}, bf16[128,1024]{1,0:T(8,128)(2,1)S(1)}, u32[]{:S(2)}, u32[]{:S(2)}) collective-permute-start(bf16[128,1024]{1,0:T(8,128)(2,1)S(1)} %get-tuple-element.60), channel_id=1, source_target_pairs={{0,64},{8,72},{16,80},{24,88},{32,96},{40,104},{48,112},{56,120},{... | collective-permute-start | bytes 786440 | tf_op jit(solution)/shard_map/sum_y_second/ppermute | solution.py:440
  39.2 13.2 %collective-permute-start.10 = (bf16[128,1024]{1,0:T(8,128)(2,1)S(1)}, bf16[128,1024]{1,0:T(8,128)(2,1)S(1)}, u32[]{:S(2)}, u32[]{:S(2)}) collective-permute-start(bf16[128,1024]{1,0:T(8,128)(2,1)S(1)} %get-tuple-element.61), channel_id=1, source_target_pairs={{0,32},{8,40},{16,48},{24,56},{32,64},{40,72},{48,80},{56,88},{64,... | collective-permute-start | bytes 786440 | tf_op jit(solution)/shard_map/sum_y_second/ppermute | solution.py:440
  39.8 21.4 %slice-start = ((s8[8388608]{0:T(1024)(128)(4,1)}), s8[4194304]{0:T(1024)(128)(4,1)S(1)}, s32[]{:S(2)}) async-start(s8[8388608]{0:T(1024)(128)(4,1)} %bitcast.17), calls=%async_computation | async-start | bytes 8388608
  39.8 21.4 %slice-start.1 = ((s8[8388608]{0:T(1024)(128)(4,1)}), s8[4194304]{0:T(1024)(128)(4,1)S(1)}, s32[]{:S(2)}) async-start(s8[8388608]{0:T(1024)(128)(4,1)} %bitcast.17), calls=%async_computation.1 | async-start | bytes 8388608
  39.8 12.7 %collective-permute-start.11 = (bf16[128,1024]{1,0:T(8,128)(2,1)S(1)}, bf16[128,1024]{1,0:T(8,128)(2,1)S(1)}, u32[]{:S(2)}, u32[]{:S(2)}) collective-permute-start(bf16[128,1024]{1,0:T(8,128)(2,1)S(1)} %get-tuple-element.62), channel_id=1, source_target_pairs={{0,96},{8,104},{16,112},{24,120},{32,0},{40,8},{48,16},{56,24},{64... | collective-permute-start | bytes 786440 | tf_op jit(solution)/shard_map/sum_y_second/ppermute | solution.py:440
  44.9 8.4 %collective-permute-start.8 = (bf16[128,1024]{1,0:T(8,128)(2,1)S(1)}, bf16[128,1024]{1,0:T(8,128)(2,1)S(1)}, u32[]{:S(2)}, u32[]{:S(2)}) collective-permute-start(bf16[128,1024]{1,0:T(8,128)(2,1)S(1)} %get-tuple-element.67), channel_id=1, source_target_pairs={{0,16},{8,24},{16,0},{24,8},{32,48},{40,56},{48,32},{56,40},{64,80... | collective-permute-start | bytes 786440 | tf_op jit(solution)/shard_map/sum_x_first/ppermute | solution.py:440
  54.2 15.4 %collective-permute-start.14 = (bf16[2,128,1024]{2,1,0:T(8,128)(2,1)S(1)}, bf16[2,128,1024]{2,1,0:T(8,128)(2,1)S(1)}, u32[]{:S(2)}, u32[]{:S(2)}) collective-permute-start(bf16[2,128,1024]{2,1,0:T(8,128)(2,1)S(1)} %norm_both.1.refs_0_.refs_8_), channel_id=1, source_target_pairs={{0,1},{1,0},{2,3},{3,2},{4,5},{5,4},{6,7},{7,6},{8,9},{9,8},{10,11... | collective-permute-start | bytes 1572872 | tf_op jit(solution)/shard_map/gather/ppermute | solution.py:444
  57.1 16.4 %collective-permute-start.13 = (bf16[2,128,1024]{2,1,0:T(8,128)(2,1)S(1)}, bf16[2,128,1024]{2,1,0:T(8,128)(2,1)S(1)}, u32[]{:S(2)}, u32[]{:S(2)}) collective-permute-start(bf16[2,128,1024]{2,1,0:T(8,128)(2,1)S(1)} %norm_both.1.refs_0_.refs_8_), channel_id=1, source_target_pairs={{0,6},{1,7},{2,0},{3,1},{4,2},{5,3},{6,4},{7,5},{8,14},{9,15},{10,... | collective-permute-start | bytes 1572872 | tf_op jit(solution)/shard_map/gather/ppermute | solution.py:444
  61.2 14.4 %collective-permute-start.12 = (bf16[2,128,1024]{2,1,0:T(8,128)(2,1)S(1)}, bf16[2,128,1024]{2,1,0:T(8,128)(2,1)S(1)}, u32[]{:S(2)}, u32[]{:S(2)}) collective-permute-start(bf16[2,128,1024]{2,1,0:T(8,128)(2,1)S(1)} %norm_both.1.refs_0_.refs_8_), channel_id=1, source_target_pairs={{0,2},{1,3},{2,4},{3,5},{4,6},{5,7},{6,0},{7,1},{8,10},{9,11},{10,... | collective-permute-start | bytes 1572872 | tf_op jit(solution)/shard_map/gather/ppermute | solution.py:444
  69.5 14.5 %collective-permute-start.17 = (bf16[2,128,1024]{2,1,0:T(8,128)(2,1)S(1)}, bf16[2,128,1024]{2,1,0:T(8,128)(2,1)S(1)}, u32[]{:S(2)}, u32[]{:S(2)}) collective-permute-start(bf16[2,128,1024]{2,1,0:T(8,128)(2,1)S(1)} %collective-permute-done.14.refs_2_), channel_id=1, source_target_pairs={{0,6},{1,7},{2,0},{3,1},{4,2},{5,3},{6,4},{7,5},{8,14},{9,15},{10,... | collective-permute-start | bytes 1572872 | tf_op jit(solution)/shard_map/gather/ppermute | solution.py:444
  73.6 16.1 %collective-permute-start.16 = (bf16[2,128,1024]{2,1,0:T(8,128)(2,1)S(1)}, bf16[2,128,1024]{2,1,0:T(8,128)(2,1)S(1)}, u32[]{:S(2)}, u32[]{:S(2)}) collective-permute-start(bf16[2,128,1024]{2,1,0:T(8,128)(2,1)S(1)} %collective-permute-done.14.refs_2_), channel_id=1, source_target_pairs={{0,2},{1,3},{2,4},{3,5},{4,6},{5,7},{6,0},{7,1},{8,10},{9,11},{10,... | collective-permute-start | bytes 1572872 | tf_op jit(solution)/shard_map/gather/ppermute | solution.py:444
  75.6 23.0 %collective-permute-start.15 = (bf16[2,128,1024]{2,1,0:T(8,128)(2,1)S(1)}, bf16[2,128,1024]{2,1,0:T(8,128)(2,1)S(1)}, u32[]{:S(2)}, u32[]{:S(2)}) collective-permute-start(bf16[2,128,1024]{2,1,0:T(8,128)(2,1)S(1)} %collective-permute-done.12.refs_0_), channel_id=1, source_target_pairs={{0,2},{1,3},{2,4},{3,5},{4,6},{5,7},{6,0},{7,1},{8,10},{9,11},{10,... | collective-permute-start | bytes 1572872 | tf_op jit(solution)/shard_map/gather/ppermute | solution.py:444
  89.6 9.5 %collective-permute-start.18 = (bf16[2,128,1024]{2,1,0:T(8,128)(2,1)S(1)}, bf16[2,128,1024]{2,1,0:T(8,128)(2,1)S(1)}, u32[]{:S(2)}, u32[]{:S(2)}) collective-permute-start(bf16[2,128,1024]{2,1,0:T(8,128)(2,1)S(1)} %collective-permute-done.17.refs_1_), channel_id=1, source_target_pairs={{0,6},{1,7},{2,0},{3,1},{4,2},{5,3},{6,4},{7,5},{8,14},{9,15},{10,... | collective-permute-start | bytes 1572872 | tf_op jit(solution)/shard_map/gather/ppermute | solution.py:444
  89.6 9.5 %copy-start.1 = (bf16[1024,1024]{1,0:T(8,128)(2,1)S(1)}, bf16[1024,1024]{1,0:T(8,128)(2,1)}, u32[]{:S(2)}) copy-start(bf16[1024,1024]{1,0:T(8,128)(2,1)} %refs_12_.1) | copy-start | bytes 6291460

commit v5 on v3

--- a/solution.py
+++ b/solution.py
@@ -91,17 +91,12 @@
             if len(held) == 1 and not copies:
                 dst[...] = held[0][...]
             if len(held) > 1:
-                step = SLOTS if norm else SLOTS // 2
-
-                @pl.loop(0, SLOTS // step)
-                def _(r):
-                    rows = pl.ds(pl.multiple_of(r * step, step), step)
-                    exact = len(held) == 2 and not norm and all(ref.dtype == BF16 for ref in held)
-                    total = None
-                    for ref in held:
-                        value = ref[rows, :] if exact else ref[rows, :].astype(F32)
-                        total = value if total is None else total + value
-                    dst[rows, :] = (layer_norm(total) if norm else total).astype(dst.dtype)
+                exact = len(held) == 2 and not norm and all(ref.dtype == BF16 for ref in held)
+                total = None
+                for ref in held:
+                    value = ref[...] if exact else ref[...].astype(F32)
+                    total = value if total is None else total + value
+                dst[...] = (layer_norm(total) if norm else total).astype(dst.dtype)
 
     hbm, anywhere = pl.BlockSpec(memory_space=pltpu.HBM), pl.BlockSpec(memory_space=pl.ANY)
     return pl.pallas_call(

time: 108 us -> 108 us (level)
  no operation moved by 1% of the time
where the time goes in v5:
time: 108 us
  Pallas kernels  49.9 us (46%)
  waiting for transfers between devices  24.7 us (23%)
  starting transfers between devices  24.3 us (22%)
  local copies, waits for them, and re-layouts  6.67 us (6%)
  between operations  1.65 us (2%)
    pallas_call x5, Pallas kernels, kernel_call(): pl.pallas_call(body, in_specs=in_specs, out_specs=[pl.BlockSpec(memory_sp...  33.4 us
    pallas_call x8, Pallas kernels, block_sums(): pl.pallas_call(body, in_specs=[pl.BlockSpec(memory_space=pltpu.SMEM)] + [...  16.5 us
    ppermute x7, waiting for transfers between devices, to_cand(): return lax.ppermute(array, 'cand', cand_perm(dz, dy))  15.9 us
    ppermute x12, starting transfers between devices, to_user(): return lax.ppermute(array, 'user', user_perm(dx, dy, dcore))  13.2 us
    ppermute x7, starting transfers between devices, to_cand(): return lax.ppermute(array, 'cand', cand_perm(dz, dy))  11.1 us
    ppermute x12, waiting for transfers between devices, to_user(): return lax.ppermute(array, 'user', user_perm(dx, dy, dcore))  8.83 us
    unnamed x14, local copies, waits for them, and re-layouts  4.62 us
  transfers between devices with their start and end apart: 19, of which 9 were waited for; matrix products, arithmetic and copies ran while one was open for 3% of the time, Pallas kernels for 36%

profile of v5, /device:TPU:0, one launch (start us, length us, event | category | flops | bytes accessed | tf_op | source)
XLA Modules:
  0.0 108.0 jit_solution(5997464102133767271)
XLA Ops:
  0.6 0.1 pad_add_fusion.1.scal_ref
  0.7 1.8 %pack.1 = bf16[4,128,1024]{2,1,0:T(8,128)(2,1)S(1)} custom-call(s32[3]{0:T(128)S(1)} %pad_add_fusion.1.scal_ref, bf16[4,2,2,2,128,1024]{5,4,3,2,1,0:T(8,128)(2,1)} %bitcast.20), custom_call_target="tpu_custom_call" | custom-call | flops 1000000 | bytes 65536 | tf_op jit(solution)/shard_map/sum_core/pack/pallas_call | solution.py:102
  2.5 0.1 collective-permute-start.2
  2.6 2.1 %pack_all.1 = (bf16[4,128,1024]{2,1,0:T(8,128)(2,1)S(1)}, bf16[4,128,1024]{2,1,0:T(8,128)(2,1)S(1)}) custom-call(s32[3]{0:T(128)S(1)} %pad_add_fusion.1.scal_ref, bf16[4,2,2,2,128,1024]{5,4,3,2,1,0:T(8,128)(2,1)} %bitcast.21), custom_call_target="tpu_custom_call" | custom-call | flops 1000000 | bytes 65536 | tf_op jit(solution)/shard_map/sum_core/pack_all/pallas_call | solution.py:102
  4.7 0.6 collective-permute-start
  5.3 0.1 collective-permute-start.1
  5.4 0.0 collective-permute-done.2.refs_1_
  5.4 2.8 %over_y.1 = bf16[4,128,1024]{2,1,0:T(8,128)(2,1)} custom-call(s32[3]{0:T(128)S(1)} %pad_add_fusion.1.scal_ref, bf16[4,2,2,2,128,1024]{5,4,3,2,1,0:T(8,128)(2,1)} %bitcast.22, bf16[4,128,1024]{2,1,0:T(8,128)(2,1)S(1)} %collective-permute-done.2.refs_1_), custom_call_target="tpu_custom_call" | custom-call | flops 1000000 | bytes 65536 | tf_op jit(solution)/shard_map/sum_y_second/over_y/pallas_call | solution.py:102
  8.2 0.0 copy-start.3
  8.2 0.0 copy-start.4
  8.2 1.7 %collective-permute-start.7 = (bf16[4,128,1024]{2,1,0:T(8,128)(2,1)}, bf16[4,128,1024]{2,1,0:T(8,128)(2,1)S(1)}, u32[]{:S(2)}, u32[]{:S(2)}) collective-permute-start(bf16[4,128,1024]{2,1,0:T(8,128)(2,1)} %over_y.1), channel_id=1, source_target_pairs={{0,16},{8,24},{16,0},{24,8},{32,48},{40,56},{48,32},{56,40},{64,80... | collective-permute-start | bytes 3145736 | tf_op jit(solution)/shard_map/sum_y_second/ppermute | solution.py:435
  9.9 0.0 collective-permute-done.refs_1_
  9.9 0.0 collective-permute-done.1.refs_2_
  9.9 3.8 %away_x.1 = (bf16[2,128,1024]{2,1,0:T(8,128)(2,1)}, bf16[2,128,1024]{2,1,0:T(8,128)(2,1)}, bf16[2,128,1024]{2,1,0:T(8,128)(2,1)}, bf16[4,128,1024]{2,1,0:T(8,128)(2,1)}) custom-call(s32[3]{0:T(128)S(1)} %pad_add_fusion.1.scal_ref, bf16[4,2,2,2,128,1024]{5,4,3,2,1,0:T(8,128)(2,1)} %bitcast.23, bf16[4,128,1024]{2,1,0:T(8,128)(2,1)S(1)} %collective-permute-done.refs_1_, ...), custom_call_target="tpu_custom_call" | custom-call | flops 1000000 | bytes 65536 | tf_op jit(solution)/shard_map/sum_x_first/away_x/pallas_call | solution.py:102
  13.7 0.2 collective-permute-start.6
  14.0 1.5 %collective-permute-start.3 = (bf16[2,128,1024]{2,1,0:T(8,128)(2,1)}, bf16[2,128,1024]{2,1,0:T(8,128)(2,1)}, u32[]{:S(2)}, u32[]{:S(2)}) collective-permute-start(bf16[2,128,1024]{2,1,0:T(8,128)(2,1)} %get-tuple-element.54), channel_id=1, source_target_pairs={{0,32},{8,40},{16,48},{24,56},{32,64},{40,72},{48,80},{56,88},{64,... | collective-permute-start | bytes 1572872 | tf_op jit(solution)/shard_map/sum_x_first/ppermute | solution.py:435
  15.5 1.7 %collective-permute-start.4 = (bf16[2,128,1024]{2,1,0:T(8,128)(2,1)}, bf16[2,128,1024]{2,1,0:T(8,128)(2,1)}, u32[]{:S(2)}, u32[]{:S(2)}) collective-permute-start(bf16[2,128,1024]{2,1,0:T(8,128)(2,1)} %get-tuple-element.55), channel_id=1, source_target_pairs={{0,96},{8,104},{16,112},{24,120},{32,0},{40,8},{48,16},{56,24},{64... | collective-permute-start | bytes 1572872 | tf_op jit(solution)/shard_map/sum_x_first/ppermute | solution.py:435
  17.2 1.8 %collective-permute-start.5 = (bf16[2,128,1024]{2,1,0:T(8,128)(2,1)}, bf16[2,128,1024]{2,1,0:T(8,128)(2,1)}, u32[]{:S(2)}, u32[]{:S(2)}) collective-permute-start(bf16[2,128,1024]{2,1,0:T(8,128)(2,1)} %get-tuple-element.56), channel_id=1, source_target_pairs={{0,64},{8,72},{16,80},{24,88},{32,96},{40,104},{48,112},{56,120},{... | collective-permute-start | bytes 1572872 | tf_op jit(solution)/shard_map/sum_x_first/ppermute | solution.py:435
  19.0 0.0 copy-done.3
  19.0 0.7 fusion
  20.3 0.0 copy-done.4
  20.3 0.6 fusion.1
  20.9 0.7 stack.79
  21.6 0.7 stack.77
  22.4 0.0 copy-start
  22.4 3.4 %copy-done = bf16[1024,4096]{1,0:T(8,128)(2,1)S(1)} copy-done((bf16[1024,4096]{1,0:T(8,128)(2,1)S(1)}, bf16[1024,4096]{1,0:T(8,128)(2,1)}, u32[]{:S(2)}) %copy-start) | copy-done | bytes 8388632
  25.8 1.2 %copy-done.2 = bf16[512,1024]{1,0:T(8,128)(2,1)S(1)} copy-done((bf16[512,1024]{1,0:T(8,128)(2,1)S(1)}, bf16[512,1024]{1,0:T(8,128)(2,1)}, u32[]{:S(2)}) %copy-start.2) | copy-done | bytes 1048600
  27.0 7.2 %cand_project.1 = (bf16[512,1024]{1,0:T(8,128)(2,1)S(1)}, bf16[512,1024]{1,0:T(8,128)(2,1)S(1)}, bf16[512,1024]{1,0:T(8,128)(2,1)S(1)}, bf16[512,512]{1,0:T(8,128)(2,1)S(1)}, f32[512,1024]{1,0:T(8,128)S(1)}) custom-call(s32[1,512]{1,0:T(1,128)S(1)} %bitcast.19, bf16[512,1024]{1,0:T(8,128)(2,1)S(1)} %copy-done.2, bf16[1024,4096]{1,0:T(8,128)(2,1)S(1)} %copy-done), custom_call_target="tpu_custom_call" | custom-call | flops 1000000 | bytes 65536 | tf_op jit(solution)/shard_map/cand_project/pallas_call | solution.py:207
  34.2 0.0 collective-permute-done.7.refs_2_.refs_7_
  34.3 0.0 collective-permute-done.6.refs_1_.refs_6_
  34.3 2.0 %join_y.1 = (bf16[128,1024]{1,0:T(8,128)(2,1)S(1)}, bf16[128,1024]{1,0:T(8,128)(2,1)S(1)}, bf16[128,1024]{1,0:T(8,128)(2,1)S(1)}) custom-call(s32[3]{0:T(128)S(1)} %pad_add_fusion.1.scal_ref, bf16[4,2,2,2,128,1024]{5,4,3,2,1,0:T(8,128)(2,1)} %bitcast.24, bf16[4,128,1024]{2,1,0:T(8,128)(2,1)} %collective-permute-done.6.refs_1_.refs_6_, ...), custom_call_target="tpu_custom_call" | custom-call | flops 1000000 | bytes 65536 | tf_op jit(solution)/shard_map/sum_y_second/join_y/pallas_call | solution.py:102
  36.3 1.3 %collective-permute-start.9 = (bf16[128,1024]{1,0:T(8,128)(2,1)S(1)}, bf16[128,1024]{1,0:T(8,128)(2,1)S(1)}, u32[]{:S(2)}, u32[]{:S(2)}) collective-permute-start(bf16[128,1024]{1,0:T(8,128)(2,1)S(1)} %get-tuple-element.60), channel_id=1, source_target_pairs={{0,32},{8,40},{16,48},{24,56},{32,64},{40,72},{48,80},{56,88},{64,... | collective-permute-start | bytes 786440 | tf_op jit(solution)/shard_map/sum_y_second/ppermute | solution.py:435
  37.7 2.0 %collective-permute-start.10 = (bf16[128,1024]{1,0:T(8,128)(2,1)S(1)}, bf16[128,1024]{1,0:T(8,128)(2,1)S(1)}, u32[]{:S(2)}, u32[]{:S(2)}) collective-permute-start(bf16[128,1024]{1,0:T(8,128)(2,1)S(1)} %get-tuple-element.61), channel_id=1, source_target_pairs={{0,96},{8,104},{16,112},{24,120},{32,0},{40,8},{48,16},{56,24},{64... | collective-permute-start | bytes 786440 | tf_op jit(solution)/shard_map/sum_y_second/ppermute | solution.py:435
  39.6 0.0 collective-permute-done.3.refs_3_
  39.6 1.6 %collective-permute-start.11 = (bf16[128,1024]{1,0:T(8,128)(2,1)S(1)}, bf16[128,1024]{1,0:T(8,128)(2,1)S(1)}, u32[]{:S(2)}, u32[]{:S(2)}) collective-permute-start(bf16[128,1024]{1,0:T(8,128)(2,1)S(1)} %get-tuple-element.62), channel_id=1, source_target_pairs={{0,64},{8,72},{16,80},{24,88},{32,96},{40,104},{48,112},{56,120},{... | collective-permute-start | bytes 786440 | tf_op jit(solution)/shard_map/sum_y_second/ppermute | solution.py:435
  41.2 0.0 collective-permute-done.4.refs_4_
  41.2 1.2 %collective-permute-done.5.refs_5_ = bf16[2,128,1024]{2,1,0:T(8,128)(2,1)} collective-permute-done((bf16[2,128,1024]{2,1,0:T(8,128)(2,1)}, bf16[2,128,1024]{2,1,0:T(8,128)(2,1)}, u32[]{:S(2)}, u32[]{:S(2)}) %collective-permute-start.5) | collective-permute-done | bytes 524320 | tf_op jit(solution)/shard_map/sum_x_first/ppermute | solution.py:435
  42.5 2.4 %join_x.1 = (f32[128,1024]{1,0:T(8,128)S(1)}, bf16[128,1024]{1,0:T(8,128)(2,1)S(1)}, f32[128,1024]{1,0:T(8,128)S(1)}) custom-call(s32[3]{0:T(128)S(1)} %pad_add_fusion.1.scal_ref, bf16[4,2,2,2,128,1024]{5,4,3,2,1,0:T(8,128)(2,1)} %bitcast.25, bf16[4,128,1024]{2,1,0:T(8,128)(2,1)S(1)} %collective-permute-done.refs_1_, ...), custom_call_target="tpu_custom_call" | custom-call | flops 1000000 | bytes 65536 | tf_op jit(solution)/shard_map/sum_x_first/join_x/pallas_call | solution.py:102
  44.9 0.5 collective-permute-start.8
  45.4 2.5 %collective-permute-done.9.refs_1_ = bf16[128,1024]{1,0:T(8,128)(2,1)S(1)} collective-permute-done((bf16[128,1024]{1,0:T(8,128)(2,1)S(1)}, bf16[128,1024]{1,0:T(8,128)(2,1)S(1)}, u32[]{:S(2)}, u32[]{:S(2)}) %collective-permute-start.9) | collective-permute-done | bytes 262176 | tf_op jit(solution)/shard_map/sum_y_second/ppermute | solution.py:435
  48.0 0.0 collective-permute-done.10.refs_2_
  48.0 5.0 %collective-permute-done.11.refs_3_ = bf16[128,1024]{1,0:T(8,128)(2,1)S(1)} collective-permute-done((bf16[128,1024]{1,0:T(8,128)(2,1)S(1)}, bf16[128,1024]{1,0:T(8,128)(2,1)S(1)}, u32[]{:S(2)}, u32[]{:S(2)}) %collective-permute-start.11) | collective-permute-done | bytes 262176 | tf_op jit(solution)/shard_map/sum_y_second/ppermute | solution.py:435
  53.0 0.8 norm_sum.1.refs_2_
  53.9 0.0 collective-permute-done.8.refs_1_
  53.9 0.8 norm_both.1.refs_0_.refs_8_
  54.7 3.0 %collective-permute-start.14 = (bf16[2,128,1024]{2,1,0:T(8,128)(2,1)S(1)}, bf16[2,128,1024]{2,1,0:T(8,128)(2,1)S(1)}, u32[]{:S(2)}, u32[]{:S(2)}) collective-permute-start(bf16[2,128,1024]{2,1,0:T(8,128)(2,1)S(1)} %norm_both.1.refs_0_.refs_8_), channel_id=1, source_target_pairs={{0,1},{1,0},{2,3},{3,2},{4,5},{5,4},{6,7},{7,6},{8,9},{9,8},{10,11... | collective-permute-start | bytes 1572872 | tf_op jit(solution)/shard_map/gather/ppermute | solution.py:439
  57.7 4.0 %collective-permute-start.13 = (bf16[2,128,1024]{2,1,0:T(8,128)(2,1)S(1)}, bf16[2,128,1024]{2,1,0:T(8,128)(2,1)S(1)}, u32[]{:S(2)}, u32[]{:S(2)}) collective-permute-start(bf16[2,128,1024]{2,1,0:T(8,128)(2,1)S(1)} %norm_both.1.refs_0_.refs_8_), channel_id=1, source_target_pairs={{0,6},{1,7},{2,0},{3,1},{4,2},{5,3},{6,4},{7,5},{8,14},{9,15},{10,... | collective-permute-start | bytes 1572872 | tf_op jit(solution)/shard_map/gather/ppermute | solution.py:439
  61.7 0.0 collective-permute-start.12
  61.7 0.0 slice-done
  61.7 4.4 %own_keys.1 = (f32[512,1024]{1,0:T(8,128)S(1)}, f32[256,1024]{1,0:T(8,128)S(1)}, bf16[256,1024]{1,0:T(8,128)(2,1)S(1)}, bf16[256,1024]{1,0:T(8,128)(2,1)S(1)}) custom-call(s32[2,12]{1,0:T(2,128)S(1)} %pad_add_fusion.scal_ref, bf16[2,128,1024]{2,1,0:T(8,128)(2,1)S(1)} %norm_both.1.refs_0_.refs_8_, ...), custom_call_target="tpu_custom_call", output_to_operand_aliasing={{0}: (4, {})} | custom-call | flops 1000000 | bytes 65536 | tf_op jit(solution)/shard_map/own_keys/pallas_call | solution.py:207
  66.1 3.5 %collective-permute-done.14.refs_2_ = bf16[2,128,1024]{2,1,0:T(8,128)(2,1)S(1)} collective-permute-done((bf16[2,128,1024]{2,1,0:T(8,128)(2,1)S(1)}, bf16[2,128,1024]{2,1,0:T(8,128)(2,1)S(1)}, u32[]{:S(2)}, u32[]{:S(2)}) %collective-permute-start.14) | collective-permute-done | bytes 524320 | tf_op jit(solution)/shard_map/gather/ppermute | solution.py:439
  69.6 4.0 %collective-permute-start.17 = (bf16[2,128,1024]{2,1,0:T(8,128)(2,1)S(1)}, bf16[2,128,1024]{2,1,0:T(8,128)(2,1)S(1)}, u32[]{:S(2)}, u32[]{:S(2)}) collective-permute-start(bf16[2,128,1024]{2,1,0:T(8,128)(2,1)S(1)} %collective-permute-done.14.refs_2_), channel_id=1, source_target_pairs={{0,6},{1,7},{2,0},{3,1},{4,2},{5,3},{6,4},{7,5},{8,14},{9,15},{10,... | collective-permute-start | bytes 1572872 | tf_op jit(solution)/shard_map/gather/ppermute | solution.py:439
  73.7 0.0 collective-permute-start.16
  73.7 0.0 collective-permute-done.13.refs_1_
  73.7 2.0 %collective-permute-done.12.refs_0_ = bf16[2,128,1024]{2,1,0:T(8,128)(2,1)S(1)} collective-permute-done((bf16[2,128,1024]{2,1,0:T(8,128)(2,1)S(1)}, bf16[2,128,1024]{2,1,0:T(8,128)(2,1)S(1)}, u32[]{:S(2)}, u32[]{:S(2)}) %collective-permute-start.12) | collective-permute-done | bytes 524320 | tf_op jit(solution)/shard_map/gather/ppermute | solution.py:439
  75.7 0.0 collective-permute-start.15
  75.7 7.8 %own_sides.1 = (f32[512,1024]{1,0:T(8,128)S(1)}, f32[256,1024]{1,0:T(8,128)S(1)}) custom-call(s32[2,12]{1,0:T(2,128)S(1)} %pad_add_fusion.scal_ref, bf16[2,128,1024]{2,1,0:T(8,128)(2,1)S(1)} %collective-permute-done.12.refs_0_, bf16[2,128,1024]{2,1,0:T(8,128)(2,1)S(1)} %collective-permute-done.13.refs_1_, ...), custom_call_target="tpu_custom_call", output_to_operand_aliasing={{0}: (6, {}), {1}: (8, {})} | custom-call | flops 1000000 | bytes 65536 | tf_op jit(solution)/shard_map/own_sides/pallas_call | solution.py:207
  83.6 0.1 collective-permute-done.17.refs_1_
  83.6 6.1 %collective-permute-done.16.refs_0_ = bf16[2,128,1024]{2,1,0:T(8,128)(2,1)S(1)} collective-permute-done((bf16[2,128,1024]{2,1,0:T(8,128)(2,1)S(1)}, bf16[2,128,1024]{2,1,0:T(8,128)(2,1)S(1)}, u32[]{:S(2)}, u32[]{:S(2)}) %collective-permute-start.16) | collective-permute-done | bytes 524320 | tf_op jit(solution)/shard_map/gather/ppermute | solution.py:439
  89.7 0.0 collective-permute-start.18
  89.7 5.1 %near_sides.1 = (f32[512,1024]{1,0:T(8,128)S(1)}, f32[256,1024]{1,0:T(8,128)S(1)}) custom-call(s32[2,12]{1,0:T(2,128)S(1)} %pad_add_fusion.scal_ref, bf16[2,128,1024]{2,1,0:T(8,128)(2,1)S(1)} %collective-permute-done.16.refs_0_, bf16[2,128,1024]{2,1,0:T(8,128)(2,1)S(1)} %collective-permute-done.17.refs_1_, ...), custom_call_target="tpu_custom_call", output_to_operand_aliasing={{0}: (5, {}), {1}: (7, {})} | custom-call | flops 1000000 | bytes 65536 | tf_op jit(solution)/shard_map/near_sides/pallas_call | solution.py:207
  94.8 3.5 %collective-permute-done.15.refs_0_ = bf16[2,128,1024]{2,1,0:T(8,128)(2,1)S(1)} collective-permute-done((bf16[2,128,1024]{2,1,0:T(8,128)(2,1)S(1)}, bf16[2,128,1024]{2,1,0:T(8,128)(2,1)S(1)}, u32[]{:S(2)}, u32[]{:S(2)}) %collective-permute-start.15) | collective-permute-done | bytes 524320 | tf_op jit(solution)/shard_map/gather/ppermute | solution.py:439
  98.3 0.6 collective-permute-done.18.refs_1_
  98.9 8.9 %far_finish.1 = (bf16[2,128,1024]{2,1,0:T(8,128)(2,1)}, bf16[512,1024]{1,0:T(8,128)(2,1)}) custom-call(s32[2,12]{1,0:T(2,128)S(1)} %pad_add_fusion.scal_ref, bf16[2,128,1024]{2,1,0:T(8,128)(2,1)S(1)} %collective-permute-done.15.refs_0_, bf16[2,128,1024]{2,1,0:T(8,128)(2,1)S(1)} %collective-permute-done.18.refs_1_, bf16[1024,4096]{1,0:T(8,128)(2,1)S(1)} %bitcast.18, ...), custom_call_target="tpu_custom_call" | custom-call | flops 1000000 | bytes 65536 | tf_op jit(solution)/shard_map/far_finish/pallas_call | solution.py:207
  (8 shorter events, 0.0 us)
Async XLA Ops:
  2.5 2.9 %collective-permute-start.2 = (bf16[4,128,1024]{2,1,0:T(8,128)(2,1)S(1)}, bf16[4,128,1024]{2,1,0:T(8,128)(2,1)S(1)}, u32[]{:S(2)}, u32[]{:S(2)}) collective-permute-start(bf16[4,128,1024]{2,1,0:T(8,128)(2,1)S(1)} %pack.1), channel_id=1, source_target_pairs={{0,8},{8,0},{16,24},{24,16},{32,40},{40,32},{48,56},{56,48},{64,72... | collective-permute-start | bytes 3145736 | tf_op jit(solution)/shard_map/sum_core/ppermute | solution.py:435
  4.7 5.2 %collective-permute-start = (bf16[4,128,1024]{2,1,0:T(8,128)(2,1)S(1)}, bf16[4,128,1024]{2,1,0:T(8,128)(2,1)S(1)}, u32[]{:S(2)}, u32[]{:S(2)}) collective-permute-start(bf16[4,128,1024]{2,1,0:T(8,128)(2,1)S(1)} %get-tuple-element.47), channel_id=1, source_target_pairs={{0,8},{8,0},{16,24},{24,16},{32,40},{40,32},{48,56},{56,48},{64,72... | collective-permute-start | bytes 3145736 | tf_op jit(solution)/shard_map/sum_core/ppermute | solution.py:435
  5.3 4.6 %collective-permute-start.1 = (bf16[4,128,1024]{2,1,0:T(8,128)(2,1)S(1)}, bf16[4,128,1024]{2,1,0:T(8,128)(2,1)S(1)}, u32[]{:S(2)}, u32[]{:S(2)}) collective-permute-start(bf16[4,128,1024]{2,1,0:T(8,128)(2,1)S(1)} %get-tuple-element.48), channel_id=1, source_target_pairs={{0,8},{8,0},{16,24},{24,16},{32,40},{40,32},{48,56},{56,48},{64,72... | collective-permute-start | bytes 3145736 | tf_op jit(solution)/shard_map/sum_core/ppermute | solution.py:435
  8.2 10.9 %copy-start.3 = (s32[512]{0:T(512)S(1)}, s32[512]{0:T(512)}, u32[]{:S(2)}) copy-start(s32[512]{0:T(512)} %param.9) | copy-start | bytes 6148
  8.2 12.1 %copy-start.4 = (s32[2]{0:T(128)S(1)}, s32[2]{0:T(128)}, u32[]{:S(2)}) copy-start(s32[2]{0:T(128)} %param.8) | copy-start | bytes 28
  8.2 26.1 %collective-permute-start.7 = (bf16[4,128,1024]{2,1,0:T(8,128)(2,1)}, bf16[4,128,1024]{2,1,0:T(8,128)(2,1)S(1)}, u32[]{:S(2)}, u32[]{:S(2)}) collective-permute-start(bf16[4,128,1024]{2,1,0:T(8,128)(2,1)} %over_y.1), channel_id=1, source_target_pairs={{0,16},{8,24},{16,0},{24,8},{32,48},{40,56},{48,32},{56,40},{64,80... | collective-permute-start | bytes 3145736 | tf_op jit(solution)/shard_map/sum_y_second/ppermute | solution.py:435
  13.7 20.5 %collective-permute-start.6 = (bf16[4,128,1024]{2,1,0:T(8,128)(2,1)}, bf16[4,128,1024]{2,1,0:T(8,128)(2,1)}, u32[]{:S(2)}, u32[]{:S(2)}) collective-permute-start(bf16[4,128,1024]{2,1,0:T(8,128)(2,1)} %get-tuple-element.52), channel_id=1, source_target_pairs={{0,8},{8,0},{16,24},{24,16},{32,40},{40,32},{48,56},{56,48},{64,72... | collective-permute-start | bytes 3145736 | tf_op jit(solution)/shard_map/sum_core/ppermute | solution.py:435
  14.0 25.7 %collective-permute-start.3 = (bf16[2,128,1024]{2,1,0:T(8,128)(2,1)}, bf16[2,128,1024]{2,1,0:T(8,128)(2,1)}, u32[]{:S(2)}, u32[]{:S(2)}) collective-permute-start(bf16[2,128,1024]{2,1,0:T(8,128)(2,1)} %get-tuple-element.54), channel_id=1, source_target_pairs={{0,32},{8,40},{16,48},{24,56},{32,64},{40,72},{48,80},{56,88},{64,... | collective-permute-start | bytes 1572872 | tf_op jit(solution)/shard_map/sum_x_first/ppermute | solution.py:435
  15.5 25.8 %collective-permute-start.4 = (bf16[2,128,1024]{2,1,0:T(8,128)(2,1)}, bf16[2,128,1024]{2,1,0:T(8,128)(2,1)}, u32[]{:S(2)}, u32[]{:S(2)}) collective-permute-start(bf16[2,128,1024]{2,1,0:T(8,128)(2,1)} %get-tuple-element.55), channel_id=1, source_target_pairs={{0,96},{8,104},{16,112},{24,120},{32,0},{40,8},{48,16},{56,24},{64... | collective-permute-start | bytes 1572872 | tf_op jit(solution)/shard_map/sum_x_first/ppermute | solution.py:435
  17.2 25.3 %collective-permute-start.5 = (bf16[2,128,1024]{2,1,0:T(8,128)(2,1)}, bf16[2,128,1024]{2,1,0:T(8,128)(2,1)}, u32[]{:S(2)}, u32[]{:S(2)}) collective-permute-start(bf16[2,128,1024]{2,1,0:T(8,128)(2,1)} %get-tuple-element.56), channel_id=1, source_target_pairs={{0,64},{8,72},{16,80},{24,88},{32,96},{40,104},{48,112},{56,120},{... | collective-permute-start | bytes 1572872 | tf_op jit(solution)/shard_map/sum_x_first/ppermute | solution.py:435
  22.4 3.4 %copy-start = (bf16[1024,4096]{1,0:T(8,128)(2,1)S(1)}, bf16[1024,4096]{1,0:T(8,128)(2,1)}, u32[]{:S(2)}) copy-start(bf16[1024,4096]{1,0:T(8,128)(2,1)} %refs_2_.3) | copy-start | bytes 25165828
  25.8 1.2 %copy-start.2 = (bf16[512,1024]{1,0:T(8,128)(2,1)S(1)}, bf16[512,1024]{1,0:T(8,128)(2,1)}, u32[]{:S(2)}) copy-start(bf16[512,1024]{1,0:T(8,128)(2,1)} %feats_ref.1) | copy-start | bytes 3145732
  36.3 11.7 %collective-permute-start.9 = (bf16[128,1024]{1,0:T(8,128)(2,1)S(1)}, bf16[128,1024]{1,0:T(8,128)(2,1)S(1)}, u32[]{:S(2)}, u32[]{:S(2)}) collective-permute-start(bf16[128,1024]{1,0:T(8,128)(2,1)S(1)} %get-tuple-element.60), channel_id=1, source_target_pairs={{0,32},{8,40},{16,48},{24,56},{32,64},{40,72},{48,80},{56,88},{64,... | collective-permute-start | bytes 786440 | tf_op jit(solution)/shard_map/sum_y_second/ppermute | solution.py:435
  37.7 10.3 %collective-permute-start.10 = (bf16[128,1024]{1,0:T(8,128)(2,1)S(1)}, bf16[128,1024]{1,0:T(8,128)(2,1)S(1)}, u32[]{:S(2)}, u32[]{:S(2)}) collective-permute-start(bf16[128,1024]{1,0:T(8,128)(2,1)S(1)} %get-tuple-element.61), channel_id=1, source_target_pairs={{0,96},{8,104},{16,112},{24,120},{32,0},{40,8},{48,16},{56,24},{64... | collective-permute-start | bytes 786440 | tf_op jit(solution)/shard_map/sum_y_second/ppermute | solution.py:435
  39.6 22.1 %slice-start = ((s8[8388608]{0:T(1024)(128)(4,1)}), s8[4194304]{0:T(1024)(128)(4,1)S(1)}, s32[]{:S(2)}) async-start(s8[8388608]{0:T(1024)(128)(4,1)} %bitcast.17), calls=%async_computation | async-start | bytes 8388608
  39.6 22.1 %slice-start.1 = ((s8[8388608]{0:T(1024)(128)(4,1)}), s8[4194304]{0:T(1024)(128)(4,1)S(1)}, s32[]{:S(2)}) async-start(s8[8388608]{0:T(1024)(128)(4,1)} %bitcast.17), calls=%async_computation.1 | async-start | bytes 8388608
  39.6 13.4 %collective-permute-start.11 = (bf16[128,1024]{1,0:T(8,128)(2,1)S(1)}, bf16[128,1024]{1,0:T(8,128)(2,1)S(1)}, u32[]{:S(2)}, u32[]{:S(2)}) collective-permute-start(bf16[128,1024]{1,0:T(8,128)(2,1)S(1)} %get-tuple-element.62), channel_id=1, source_target_pairs={{0,64},{8,72},{16,80},{24,88},{32,96},{40,104},{48,112},{56,120},{... | collective-permute-start | bytes 786440 | tf_op jit(solution)/shard_map/sum_y_second/ppermute | solution.py:435
  44.9 9.0 %collective-permute-start.8 = (bf16[128,1024]{1,0:T(8,128)(2,1)S(1)}, bf16[128,1024]{1,0:T(8,128)(2,1)S(1)}, u32[]{:S(2)}, u32[]{:S(2)}) collective-permute-start(bf16[128,1024]{1,0:T(8,128)(2,1)S(1)} %get-tuple-element.67), channel_id=1, source_target_pairs={{0,16},{8,24},{16,0},{24,8},{32,48},{40,56},{48,32},{56,40},{64,80... | collective-permute-start | bytes 786440 | tf_op jit(solution)/shard_map/sum_x_first/ppermute | solution.py:435
  54.7 15.0 %collective-permute-start.14 = (bf16[2,128,1024]{2,1,0:T(8,128)(2,1)S(1)}, bf16[2,128,1024]{2,1,0:T(8,128)(2,1)S(1)}, u32[]{:S(2)}, u32[]{:S(2)}) collective-permute-start(bf16[2,128,1024]{2,1,0:T(8,128)(2,1)S(1)} %norm_both.1.refs_0_.refs_8_), channel_id=1, source_target_pairs={{0,1},{1,0},{2,3},{3,2},{4,5},{5,4},{6,7},{7,6},{8,9},{9,8},{10,11... | collective-permute-start | bytes 1572872 | tf_op jit(solution)/shard_map/gather/ppermute | solution.py:439
  57.7 16.0 %collective-permute-start.13 = (bf16[2,128,1024]{2,1,0:T(8,128)(2,1)S(1)}, bf16[2,128,1024]{2,1,0:T(8,128)(2,1)S(1)}, u32[]{:S(2)}, u32[]{:S(2)}) collective-permute-start(bf16[2,128,1024]{2,1,0:T(8,128)(2,1)S(1)} %norm_both.1.refs_0_.refs_8_), channel_id=1, source_target_pairs={{0,6},{1,7},{2,0},{3,1},{4,2},{5,3},{6,4},{7,5},{8,14},{9,15},{10,... | collective-permute-start | bytes 1572872 | tf_op jit(solution)/shard_map/gather/ppermute | solution.py:439
  61.7 14.0 %collective-permute-start.12 = (bf16[2,128,1024]{2,1,0:T(8,128)(2,1)S(1)}, bf16[2,128,1024]{2,1,0:T(8,128)(2,1)S(1)}, u32[]{:S(2)}, u32[]{:S(2)}) collective-permute-start(bf16[2,128,1024]{2,1,0:T(8,128)(2,1)S(1)} %norm_both.1.refs_0_.refs_8_), channel_id=1, source_target_pairs={{0,2},{1,3},{2,4},{3,5},{4,6},{5,7},{6,0},{7,1},{8,10},{9,11},{10,... | collective-permute-start | bytes 1572872 | tf_op jit(solution)/shard_map/gather/ppermute | solution.py:439
  69.6 14.0 %collective-permute-start.17 = (bf16[2,128,1024]{2,1,0:T(8,128)(2,1)S(1)}, bf16[2,128,1024]{2,1,0:T(8,128)(2,1)S(1)}, u32[]{:S(2)}, u32[]{:S(2)}) collective-permute-start(bf16[2,128,1024]{2,1,0:T(8,128)(2,1)S(1)} %collective-permute-done.14.refs_2_), channel_id=1, source_target_pairs={{0,6},{1,7},{2,0},{3,1},{4,2},{5,3},{6,4},{7,5},{8,14},{9,15},{10,... | collective-permute-start | bytes 1572872 | tf_op jit(solution)/shard_map/gather/ppermute | solution.py:439
  73.7 16.1 %collective-permute-start.16 = (bf16[2,128,1024]{2,1,0:T(8,128)(2,1)S(1)}, bf16[2,128,1024]{2,1,0:T(8,128)(2,1)S(1)}, u32[]{:S(2)}, u32[]{:S(2)}) collective-permute-start(bf16[2,128,1024]{2,1,0:T(8,128)(2,1)S(1)} %collective-permute-done.14.refs_2_), channel_id=1, source_target_pairs={{0,2},{1,3},{2,4},{3,5},{4,6},{5,7},{6,0},{7,1},{8,10},{9,11},{10,... | collective-permute-start | bytes 1572872 | tf_op jit(solution)/shard_map/gather/ppermute | solution.py:439
  75.7 22.6 %collective-permute-start.15 = (bf16[2,128,1024]{2,1,0:T(8,128)(2,1)S(1)}, bf16[2,128,1024]{2,1,0:T(8,128)(2,1)S(1)}, u32[]{:S(2)}, u32[]{:S(2)}) collective-permute-start(bf16[2,128,1024]{2,1,0:T(8,128)(2,1)S(1)} %collective-permute-done.12.refs_0_), channel_id=1, source_target_pairs={{0,2},{1,3},{2,4},{3,5},{4,6},{5,7},{6,0},{7,1},{8,10},{9,11},{10,... | collective-permute-start | bytes 1572872 | tf_op jit(solution)/shard_map/gather/ppermute | solution.py:439
  89.7 9.2 %collective-permute-start.18 = (bf16[2,128,1024]{2,1,0:T(8,128)(2,1)S(1)}, bf16[2,128,1024]{2,1,0:T(8,128)(2,1)S(1)}, u32[]{:S(2)}, u32[]{:S(2)}) collective-permute-start(bf16[2,128,1024]{2,1,0:T(8,128)(2,1)S(1)} %collective-permute-done.17.refs_1_), channel_id=1, source_target_pairs={{0,6},{1,7},{2,0},{3,1},{4,2},{5,3},{6,4},{7,5},{8,14},{9,15},{10,... | collective-permute-start | bytes 1572872 | tf_op jit(solution)/shard_map/gather/ppermute | solution.py:439
  89.7 9.2 %copy-start.1 = (bf16[1024,1024]{1,0:T(8,128)(2,1)S(1)}, bf16[1024,1024]{1,0:T(8,128)(2,1)}, u32[]{:S(2)}) copy-start(bf16[1024,1024]{1,0:T(8,128)(2,1)} %refs_12_.1) | copy-start | bytes 6291460
